TPU v7x, 32 devices: a whole 2x2x4 slice. The times are simulated.
32 devices in a mesh: region: 4 (over x, core), dev: 8 (over z, y).
Axes of the slice: x: 2, y: 2, z: 4, core: 2. Of those that a mesh axis runs over, the one named last changes fastest.
Arguments:
- tile_values: bfloat16 [2048, 3, 128, 128], P(('region', 'dev')), as said below
- basis_tiles: bfloat16 [2048, 128, 128], P(('region', 'dev')), may hold values from -0.09375 to 0.09375
- tile_offsets: int32 [2048, 2], replicated, may hold values from -2 to 2, as said below
- aggregate_ids: int32 [2048], replicated, may hold values from 0 to 95, as said below
Outputs:
- prolongator: bfloat16 [2048, 3, 128, 128], P(('region', 'dev'))
- coarse_tiles: bfloat16 [128, 3, 128, 128], P('dev')
Inputs may be any that keep to these rules, and one draw needn't show every extreme that they name: `tile_offsets`: each block's two offsets are distinct and point to a block inside the 2048 blocks. `aggregate_ids`: aggregates are runs of whole units of 8 consecutive blocks inside one device's 64 blocks; ids count up from 0 along the blocks without gaps; each device holds 2 to 4 aggregates, some device exactly 4; the devices of block ranges 2i and 2i + 1 together hold 6 aggregates. `tile_values`: the diagonal entries of tile 0 of every block lie between 1.5 and 4.5.
All inputs are finite; a program needn't handle non-finite values.
Results may differ from a plain program's by a relative error of at most 0.0031.
Values may be sent and summed in bfloat16 or wider, within the bound.
No kernel may reach another device: no remote copies, remote signals or barrier semaphores. Data moves between devices by JAX's collectives and lax.ppermute only.
A program may use at most 192 MiB of HBM per device.

v0:
```python
import jax
import jax.numpy as jnp
from jax import lax
from jax.sharding import PartitionSpec as P

MOSTA = 4


damping = 0.6


def extended(block, sides, width):
    for axis, dim in sides:
        count = lax.axis_size(axis)
        forward = [(i, i + 1) for i in range(count - 1)]
        backward = [(target, source) for source, target in forward]
        low = lax.ppermute(
            lax.slice_in_dim(block, block.shape[dim] - width, None, axis=dim), axis, forward
        )
        high = lax.ppermute(lax.slice_in_dim(block, 0, width, axis=dim), axis, backward)
        block = jnp.concatenate([low, block, high], axis=dim)
    return block


def band_terms(tile_block, offset_block, neighbour_prol, neighbour_offsets, own_prol):
    slot_index = offset_block[:, :, None] + neighbour_offsets + 4
    one_hot = (slot_index[..., None] == jnp.arange(9, dtype=jnp.int32)).astype(jnp.float32)
    products = jnp.einsum(
        "pkij,pkqjc->pkqic", tile_block, neighbour_prol, preferred_element_type=jnp.float32
    )
    band_rows = jnp.einsum(
        "pkqs,pkqic->psic", one_hot, products, precision=lax.Precision.HIGHEST
    ).astype(jnp.bfloat16)
    return jnp.einsum("pkic,psid->pkscd", own_prol, band_rows, preferred_element_type=jnp.float32)


def smooth_rows(tiles, basis_window, offsets, own_basis):
    row_total = tiles.shape[0]
    near_index = jnp.arange(row_total, dtype=jnp.int32)[:, None] + 2 + offsets
    product = jnp.einsum(
        "pkij,pkjc->pkic", tiles, basis_window[near_index], preferred_element_type=jnp.float32
    )
    diag_values = jnp.diagonal(tiles[:, 0], axis1=1, axis2=2).astype(jnp.float32)
    inverse_diag = 1.0 / jnp.where(diag_values == 0.0, 1.0, diag_values)
    selector = (jnp.arange(3) == 0).astype(jnp.float32)
    identity_part = selector[None, :, None, None] * own_basis.astype(jnp.float32)[:, None]
    return (identity_part - damping * inverse_diag[:, None, :, None] * product).astype(jnp.bfloat16)


def local(tile_values, basis_tiles, tile_offsets, aggregate_ids):
    own_rows = tile_values.shape[0]
    block_count = tile_offsets.shape[0]
    coarse_width = basis_tiles.shape[2]
    first_row = lax.axis_index(("region", "dev")) * own_rows
    leading = jnp.zeros((block_count, 1), jnp.int32)
    padded_offsets = jnp.pad(jnp.concatenate([leading, tile_offsets], axis=1), ((8, 8), (0, 0)))
    local_offsets = lax.dynamic_slice_in_dim(padded_offsets, first_row + 8, own_rows, 0)
    joined = jnp.concatenate([basis_tiles[:, None], tile_values], axis=1)
    margin = 4
    joined_window = extended(joined, ((("region", "dev"), 0),), 2)
    basis_window = joined_window[:, 0]
    prolongator = smooth_rows(tile_values, basis_window, local_offsets, basis_tiles)
    tile_window = jnp.pad(joined_window[:, 1:], ((2, 2), (0, 0), (0, 0), (0, 0)))
    prol_window = jnp.pad(
        extended(prolongator, ((("region", "dev"), 0),), 4), ((2, 2), (0, 0), (0, 0), (0, 0))
    )
    window_rows = own_rows + 2 * margin
    offset_window = lax.dynamic_slice_in_dim(
        padded_offsets, first_row - margin + 6, window_rows + 4, 0
    )
    base_agg = aggregate_ids[first_row]
    agg_count = aggregate_ids[first_row + own_rows - 1] - base_agg + 1
    group_rows = 8
    group_span = jnp.arange(group_rows, dtype=jnp.int32)
    band_span = jnp.arange(9, dtype=jnp.int32) - 4
    target_count = (MOSTA + 2) * 3
    target_span = jnp.arange(target_count, dtype=jnp.int32)

    def accumulate(buffer, begin_row):
        tile_block = lax.dynamic_slice_in_dim(tile_window, begin_row, group_rows, 0)
        offset_block = lax.dynamic_slice_in_dim(offset_window, begin_row + 2, group_rows, 0)
        window_index = begin_row + group_span
        near_rows = window_index[:, None] + 2 + offset_block
        own_prol = lax.dynamic_slice_in_dim(prol_window, begin_row + 2, group_rows, 0)
        terms = band_terms(
            tile_block, offset_block, prol_window[near_rows], offset_window[near_rows], own_prol
        )
        global_rows = first_row - margin + window_index
        fine_rows = jnp.clip(global_rows[:, None] + offset_block, 0, block_count - 1)
        fine_cols = jnp.clip(global_rows[:, None] + band_span, 0, block_count - 1)
        row_aggs = aggregate_ids[fine_rows]
        col_aggs = aggregate_ids[fine_cols]
        bands = col_aggs[:, None, :] - row_aggs[:, :, None] + 1
        slots = jnp.broadcast_to((row_aggs - base_agg + 1)[:, :, None], bands.shape)
        targets = (slots * 3 + bands).reshape(-1)
        placing = (targets[None, :] == target_span[:, None]).astype(jnp.float32)
        flat_terms = terms.reshape(-1, coarse_width * coarse_width)
        added = jnp.dot(
            placing, flat_terms, precision=lax.Precision.HIGHEST, preferred_element_type=jnp.float32
        )
        return (buffer + added.reshape(MOSTA + 2, 3, coarse_width, coarse_width), None)

    begins = jnp.arange(window_rows // group_rows, dtype=jnp.int32) * group_rows
    initial = jnp.zeros((MOSTA + 2, 3, coarse_width, coarse_width), jnp.float32)
    buffer, ignored = lax.scan(accumulate, initial, begins)
    valid = (jnp.arange(MOSTA, dtype=jnp.int32) < agg_count).astype(jnp.float32)
    coarse = (buffer[1 : MOSTA + 1] * valid[:, None, None, None]).astype(jnp.bfloat16)
    relayed = lax.all_gather(coarse, "region", axis=0, tiled=True)
    return (prolongator, relayed)


def solution(mesh):
    placed = (P(("region", "dev"), None, None, None), P(("region", "dev"), None, None), P(), P())
    return jax.shard_map(
        local,
        mesh=mesh,
        in_specs=placed,
        out_specs=(P(("region", "dev"), None, None, None), P("dev", None, None, None)),
        check_vma=False,
    )
```

profile of v0, /device:TPU:0, one launch (start us, length us, event | category | flops | bytes accessed | tf_op | source)
XLA Modules:
  0.0 805.8 jit_solution(7569002440387992904)
XLA Ops:
  32.5 9.9 %gather_fusion.5 = bf16[192,128,128]{2,1,0:T(8,128)(2,1)} fusion(bf16[68,128,128]{2,1,0:T(8,128)(2,1)} %maximum_bitcast_fusion, s32[1024]{0:T(1024)S(1)} %pad_clamp_fusion.3), kind=kCustom, calls=%fused_computation.5 | custom fusion | bytes 12583680 | tf_op jit(solution)/shard_map/gather | solution.py:41
  42.4 10.5 %fusion.26 = bf16[64,3,128,128]{2,3,1,0:T(8,128)(2,1)} fusion(f32[64,128]{1,0:T(8,128)S(1)} %copy.40, f32[64,128,128]{1,2,0:T(8,128)} %copy.38, f32[3]{0:T(128)S(1)} %compare_convert_fusion.1, bf16[64,3,128,128]{3,2,1,0:T(8,128)(2,1)} %bitcast.120, bf16[64,3,128,128]{3,2,1,0:T(8,128)(2,1)} %param.6), kind=kOutput, calls=%fused_computation.51 | convolution fusion | flops 817889280 | bytes 23101452 | tf_op jit(solution)/shard_map/pkij,pkjc->pkic/dot_general | solution.py:40
  65.6 10.7 %collective-permute-done.2 = bf16[4,3,128,128]{2,3,1,0:T(8,128)(2,1)S(1)} collective-permute-done((bf16[4,3,128,128]{2,3,1,0:T(8,128)(2,1)S(1)}, bf16[4,3,128,128]{2,3,1,0:T(8,128)(2,1)S(1)}, u32[]{:S(2)}, u32[]{:S(2)}) %collective-permute-start.2) | collective-permute-done | bytes 393248 | tf_op jit(solution)/shard_map/ppermute | solution.py:17
  80.1 10.3 %copy.57 = bf16[72,3,128,128]{3,2,1,0:T(8,128)(2,1)} copy(bf16[72,3,128,128]{2,3,1,0:T(8,128)(2,1)} %pad_maximum_fusion) | data formatting | bytes 14155776
  90.3 9.1 %pad.14.clone = bf16[76,3,128,128]{3,2,1,0:T(8,128)(2,1)} pad(bf16[72,3,128,128]{3,2,1,0:T(8,128)(2,1)} %copy.57, bf16[]{:T(256)} %constant.116.clone.1), padding=2_2x0_0x0_0x0_0 | pad | bytes 14548994 | tf_op jit(solution)/shard_map/jit(_pad)/pad | solution.py:64
  99.4 673.0 %while.13 = (s32[]{:T(128)}, f32[6,3,128,128]{3,0,2,1:T(8,128)}, s32[]{:T(128)}, s32[9]{0:T(128)S(1)}, s32[76,3]{1,0:T(8,128)S(1)}, /*index=5*/s32[2048]{0:T(102...) while((s32[]{:T(128)}, f32[6,3,128,128]{3,0,2,1:T(8,128)}, ...), condition=%wide.region_1.2_spmd.clone, body=%wide.region_0.1_spmd.clone.sunk | while | flops 2101552128 | bytes 100688144 | solution.py:105
  123.5 8.6 %fusion.56 = bf16[8,9,128,128,1]{3,1,2,0,4:T(8,128)(2,1)S(1)} fusion(f32[8,3,3,128,128]{4,2,1,3,0:T(4,128)} %copy.83, s32[8,3,3]{2,1,0:T(4,128)S(1)} %copy.85), kind=kOutput, calls=%fused_computation.15.clone.1 | convolution fusion | flops 128582280 | bytes 7078176 | tf_op jit(solution)/shard_map/while/body/eval_jaxpr/pkqs,pkqic->psic/dot_general | solution.py:31
  140.3 15.3 %copy.86 = f32[8,3,9,128,128]{4,3,2,1,0:T(8,128)} copy(f32[8,3,9,128,128]{3,4,1,2,0:T(8,128)} %convolution_bitcast_fusion.5) | data formatting | bytes 28311552 | tf_op jit(solution)/shard_map/while/body/eval_jaxpr/pkic,psid->pkscd/transpose | solution.py:34
  155.6 17.4 %select_add_fusion.2 = f32[6,3,128,128]{3,0,2,1:T(8,128)S(1)} fusion(f32[6,3,128,128]{3,0,2,1:T(8,128)S(1)} %copy-done.1, pred[]{:T(512)S(6)} %compare.45, s32[6,3]{0,1:T(4,128)S(1)} %copy.82, s32[216]{0:T(256)S(1)} %add.423, f32[27,8,128,128]{3,2,1,0:T(8,128)} %bitcast.111), kind=kOutput, calls=%fused_computation.18.clone.1 | convolution fusion | flops 765005632 | bytes 16516009 | tf_op jit(solution)/shard_map/while/body/eval_jaxpr/dot_general | solution.py:98
  198.3 8.6 %fusion.56 = bf16[8,9,128,128,1]{3,1,2,0,4:T(8,128)(2,1)S(1)} fusion(f32[8,3,3,128,128]{4,2,1,3,0:T(4,128)} %copy.83, s32[8,3,3]{2,1,0:T(4,128)S(1)} %copy.85), kind=kOutput, calls=%fused_computation.15.clone.1 | convolution fusion | flops 128582280 | bytes 7078176 | tf_op jit(solution)/shard_map/while/body/eval_jaxpr/pkqs,pkqic->psic/dot_general | solution.py:31
  215.1 15.3 %copy.86 = f32[8,3,9,128,128]{4,3,2,1,0:T(8,128)} copy(f32[8,3,9,128,128]{3,4,1,2,0:T(8,128)} %convolution_bitcast_fusion.5) | data formatting | bytes 28311552 | tf_op jit(solution)/shard_map/while/body/eval_jaxpr/pkic,psid->pkscd/transpose | solution.py:34
  230.4 17.4 %select_add_fusion.2 = f32[6,3,128,128]{3,0,2,1:T(8,128)S(1)} fusion(f32[6,3,128,128]{3,0,2,1:T(8,128)S(1)} %copy-done.1, pred[]{:T(512)S(6)} %compare.45, s32[6,3]{0,1:T(4,128)S(1)} %copy.82, s32[216]{0:T(256)S(1)} %add.423, f32[27,8,128,128]{3,2,1,0:T(8,128)} %bitcast.111), kind=kOutput, calls=%fused_computation.18.clone.1 | convolution fusion | flops 765005632 | bytes 16516009 | tf_op jit(solution)/shard_map/while/body/eval_jaxpr/dot_general | solution.py:98
  273.0 8.6 %fusion.56 = bf16[8,9,128,128,1]{3,1,2,0,4:T(8,128)(2,1)S(1)} fusion(f32[8,3,3,128,128]{4,2,1,3,0:T(4,128)} %copy.83, s32[8,3,3]{2,1,0:T(4,128)S(1)} %copy.85), kind=kOutput, calls=%fused_computation.15.clone.1 | convolution fusion | flops 128582280 | bytes 7078176 | tf_op jit(solution)/shard_map/while/body/eval_jaxpr/pkqs,pkqic->psic/dot_general | solution.py:31
  289.9 15.3 %copy.86 = f32[8,3,9,128,128]{4,3,2,1,0:T(8,128)} copy(f32[8,3,9,128,128]{3,4,1,2,0:T(8,128)} %convolution_bitcast_fusion.5) | data formatting | bytes 28311552 | tf_op jit(solution)/shard_map/while/body/eval_jaxpr/pkic,psid->pkscd/transpose | solution.py:34
  305.2 17.4 %select_add_fusion.2 = f32[6,3,128,128]{3,0,2,1:T(8,128)S(1)} fusion(f32[6,3,128,128]{3,0,2,1:T(8,128)S(1)} %copy-done.1, pred[]{:T(512)S(6)} %compare.45, s32[6,3]{0,1:T(4,128)S(1)} %copy.82, s32[216]{0:T(256)S(1)} %add.423, f32[27,8,128,128]{3,2,1,0:T(8,128)} %bitcast.111), kind=kOutput, calls=%fused_computation.18.clone.1 | convolution fusion | flops 765005632 | bytes 16516009 | tf_op jit(solution)/shard_map/while/body/eval_jaxpr/dot_general | solution.py:98
  347.8 8.6 %fusion.56 = bf16[8,9,128,128,1]{3,1,2,0,4:T(8,128)(2,1)S(1)} fusion(f32[8,3,3,128,128]{4,2,1,3,0:T(4,128)} %copy.83, s32[8,3,3]{2,1,0:T(4,128)S(1)} %copy.85), kind=kOutput, calls=%fused_computation.15.clone.1 | convolution fusion | flops 128582280 | bytes 7078176 | tf_op jit(solution)/shard_map/while/body/eval_jaxpr/pkqs,pkqic->psic/dot_general | solution.py:31
  364.7 15.3 %copy.86 = f32[8,3,9,128,128]{4,3,2,1,0:T(8,128)} copy(f32[8,3,9,128,128]{3,4,1,2,0:T(8,128)} %convolution_bitcast_fusion.5) | data formatting | bytes 28311552 | tf_op jit(solution)/shard_map/while/body/eval_jaxpr/pkic,psid->pkscd/transpose | solution.py:34
  380.0 17.4 %select_add_fusion.2 = f32[6,3,128,128]{3,0,2,1:T(8,128)S(1)} fusion(f32[6,3,128,128]{3,0,2,1:T(8,128)S(1)} %copy-done.1, pred[]{:T(512)S(6)} %compare.45, s32[6,3]{0,1:T(4,128)S(1)} %copy.82, s32[216]{0:T(256)S(1)} %add.423, f32[27,8,128,128]{3,2,1,0:T(8,128)} %bitcast.111), kind=kOutput, calls=%fused_computation.18.clone.1 | convolution fusion | flops 765005632 | bytes 16516009 | tf_op jit(solution)/shard_map/while/body/eval_jaxpr/dot_general | solution.py:98
  422.6 8.6 %fusion.56 = bf16[8,9,128,128,1]{3,1,2,0,4:T(8,128)(2,1)S(1)} fusion(f32[8,3,3,128,128]{4,2,1,3,0:T(4,128)} %copy.83, s32[8,3,3]{2,1,0:T(4,128)S(1)} %copy.85), kind=kOutput, calls=%fused_computation.15.clone.1 | convolution fusion | flops 128582280 | bytes 7078176 | tf_op jit(solution)/shard_map/while/body/eval_jaxpr/pkqs,pkqic->psic/dot_general | solution.py:31
  439.4 15.3 %copy.86 = f32[8,3,9,128,128]{4,3,2,1,0:T(8,128)} copy(f32[8,3,9,128,128]{3,4,1,2,0:T(8,128)} %convolution_bitcast_fusion.5) | data formatting | bytes 28311552 | tf_op jit(solution)/shard_map/while/body/eval_jaxpr/pkic,psid->pkscd/transpose | solution.py:34
  454.7 17.4 %select_add_fusion.2 = f32[6,3,128,128]{3,0,2,1:T(8,128)S(1)} fusion(f32[6,3,128,128]{3,0,2,1:T(8,128)S(1)} %copy-done.1, pred[]{:T(512)S(6)} %compare.45, s32[6,3]{0,1:T(4,128)S(1)} %copy.82, s32[216]{0:T(256)S(1)} %add.423, f32[27,8,128,128]{3,2,1,0:T(8,128)} %bitcast.111), kind=kOutput, calls=%fused_computation.18.clone.1 | convolution fusion | flops 765005632 | bytes 16516009 | tf_op jit(solution)/shard_map/while/body/eval_jaxpr/dot_general | solution.py:98
  514.2 15.3 %copy.86 = f32[8,3,9,128,128]{4,3,2,1,0:T(8,128)} copy(f32[8,3,9,128,128]{3,4,1,2,0:T(8,128)} %convolution_bitcast_fusion.5) | data formatting | bytes 28311552 | tf_op jit(solution)/shard_map/while/body/eval_jaxpr/pkic,psid->pkscd/transpose | solution.py:34
  529.5 17.4 %select_add_fusion.2 = f32[6,3,128,128]{3,0,2,1:T(8,128)S(1)} fusion(f32[6,3,128,128]{3,0,2,1:T(8,128)S(1)} %copy-done.1, pred[]{:T(512)S(6)} %compare.45, s32[6,3]{0,1:T(4,128)S(1)} %copy.82, s32[216]{0:T(256)S(1)} %add.423, f32[27,8,128,128]{3,2,1,0:T(8,128)} %bitcast.111), kind=kOutput, calls=%fused_computation.18.clone.1 | convolution fusion | flops 765005632 | bytes 16516009 | tf_op jit(solution)/shard_map/while/body/eval_jaxpr/dot_general | solution.py:98
  589.0 15.3 %copy.86 = f32[8,3,9,128,128]{4,3,2,1,0:T(8,128)} copy(f32[8,3,9,128,128]{3,4,1,2,0:T(8,128)} %convolution_bitcast_fusion.5) | data formatting | bytes 28311552 | tf_op jit(solution)/shard_map/while/body/eval_jaxpr/pkic,psid->pkscd/transpose | solution.py:34
  604.3 17.4 %select_add_fusion.2 = f32[6,3,128,128]{3,0,2,1:T(8,128)S(1)} fusion(f32[6,3,128,128]{3,0,2,1:T(8,128)S(1)} %copy-done.1, pred[]{:T(512)S(6)} %compare.45, s32[6,3]{0,1:T(4,128)S(1)} %copy.82, s32[216]{0:T(256)S(1)} %add.423, f32[27,8,128,128]{3,2,1,0:T(8,128)} %bitcast.111), kind=kOutput, calls=%fused_computation.18.clone.1 | convolution fusion | flops 765005632 | bytes 16516009 | tf_op jit(solution)/shard_map/while/body/eval_jaxpr/dot_general | solution.py:98
  663.8 15.3 %copy.86 = f32[8,3,9,128,128]{4,3,2,1,0:T(8,128)} copy(f32[8,3,9,128,128]{3,4,1,2,0:T(8,128)} %convolution_bitcast_fusion.5) | data formatting | bytes 28311552 | tf_op jit(solution)/shard_map/while/body/eval_jaxpr/pkic,psid->pkscd/transpose | solution.py:34
  679.1 17.4 %select_add_fusion.2 = f32[6,3,128,128]{3,0,2,1:T(8,128)S(1)} fusion(f32[6,3,128,128]{3,0,2,1:T(8,128)S(1)} %copy-done.1, pred[]{:T(512)S(6)} %compare.45, s32[6,3]{0,1:T(4,128)S(1)} %copy.82, s32[216]{0:T(256)S(1)} %add.423, f32[27,8,128,128]{3,2,1,0:T(8,128)} %bitcast.111), kind=kOutput, calls=%fused_computation.18.clone.1 | convolution fusion | flops 765005632 | bytes 16516009 | tf_op jit(solution)/shard_map/while/body/eval_jaxpr/dot_general | solution.py:98
  721.7 8.6 %fusion.56 = bf16[8,9,128,128,1]{3,1,2,0,4:T(8,128)(2,1)S(1)} fusion(f32[8,3,3,128,128]{4,2,1,3,0:T(4,128)} %copy.83, s32[8,3,3]{2,1,0:T(4,128)S(1)} %copy.85), kind=kOutput, calls=%fused_computation.15.clone.1 | convolution fusion | flops 128582280 | bytes 7078176 | tf_op jit(solution)/shard_map/while/body/eval_jaxpr/pkqs,pkqic->psic/dot_general | solution.py:31
  738.6 15.3 %copy.86 = f32[8,3,9,128,128]{4,3,2,1,0:T(8,128)} copy(f32[8,3,9,128,128]{3,4,1,2,0:T(8,128)} %convolution_bitcast_fusion.5) | data formatting | bytes 28311552 | tf_op jit(solution)/shard_map/while/body/eval_jaxpr/pkic,psid->pkscd/transpose | solution.py:34
  753.9 17.4 %select_add_fusion.2 = f32[6,3,128,128]{3,0,2,1:T(8,128)S(1)} fusion(f32[6,3,128,128]{3,0,2,1:T(8,128)S(1)} %copy-done.1, pred[]{:T(512)S(6)} %compare.45, s32[6,3]{0,1:T(4,128)S(1)} %copy.82, s32[216]{0:T(256)S(1)} %add.423, f32[27,8,128,128]{3,2,1,0:T(8,128)} %bitcast.111), kind=kOutput, calls=%fused_computation.18.clone.1 | convolution fusion | flops 765005632 | bytes 16516009 | tf_op jit(solution)/shard_map/while/body/eval_jaxpr/dot_general | solution.py:98
  775.0 8.6 %copy.45 = bf16[64,3,128,128]{3,2,1,0:T(8,128)(2,1)} copy(bf16[64,3,128,128]{2,3,1,0:T(8,128)(2,1)} %fusion.26) | data formatting | bytes 12582912
  783.6 12.7 %all-gather.2.cloned.1.call-done = bf16[16,3,128,128]{3,2,1,0:T(8,128)(2,1)} async-done(((bf16[4,3,128,128]{3,2,1,0:T(8,128)(2,1)}), bf16[16,3,128,128]{3,2,1,0:T(8,128)(2,1)}) %all-gather.2.cloned.1.call-update) | async-done | bytes 1572880 | tf_op jit(solution)/shard_map/all_gather | solution.py:108
  (365 shorter events, 342.7 us)
Async XLA Ops:
  7.2 789.1 %all-gather.2.cloned.1.call-start = ((), (), s32[]{:S(2)}) async-start(), calls=%async_computation | async-start | bytes 1966080 | tf_op jit(solution)/shard_map/all_gather | solution.py:108
  7.2 9.1 %copy-start.5 = (s32[2048,2]{0,1:T(2,128)S(1)}, s32[2048,2]{0,1:T(2,128)}, u32[]{:S(2)}) copy-start(s32[2048,2]{0,1:T(2,128)} %param.8) | copy-start | bytes 49156
  7.2 9.5 %slice-start.2 = ((bf16[64,3,128,128]{3,2,1,0:T(8,128)(2,1)}), bf16[64,1,128,128]{3,2,1,0:T(8,128)(2,1)S(1)}, s32[]{:S(2)}) async-start(bf16[64,3,128,128]{3,2,1,0:T(8,128)(2,1)} %param.6), calls=%async_computation.3 | async-start | bytes 4194304 | tf_op jit(solution)/shard_map/slice | solution.py:43
  9.3 13.4 %copy-start = (s32[2048]{0:T(1024)S(1)}, s32[2048]{0:T(1024)}, u32[]{:S(2)}) copy-start(s32[2048]{0:T(1024)} %param.9) | copy-start | bytes 24580
  9.3 20.5 %collective-permute-start = (bf16[2,4,128,128]{3,2,1,0:T(8,128)(2,1)}, bf16[2,4,128,128]{3,2,1,0:T(8,128)(2,1)}, u32[]{:S(2)}, u32[]{:S(2)}) collective-permute-start(bf16[2,4,128,128]{3,2,1,0:T(8,128)(2,1)} %get-tuple-element.246), channel_id=1, source_target_pairs={{0,1},{1,2},{2,3},{3,4},{4,5},{5,6},{6,7},{7,8},{8,9},{9,10},{10,1... | collective-permute-start | bytes 786440 | tf_op jit(solution)/shard_map/ppermute | solution.py:17
  15.0 14.8 %collective-permute-start.1 = (bf16[2,4,128,128]{3,2,1,0:T(8,128)(2,1)}, bf16[2,4,128,128]{3,2,1,0:T(8,128)(2,1)}, u32[]{:S(2)}, u32[]{:S(2)}) collective-permute-start(bf16[2,4,128,128]{3,2,1,0:T(8,128)(2,1)} %get-tuple-element.247), channel_id=1, source_target_pairs={{1,0},{2,1},{3,2},{4,3},{5,4},{6,5},{7,6},{8,7},{9,8},{10,9},{11,1... | collective-permute-start | bytes 786440 | tf_op jit(solution)/shard_map/ppermute | solution.py:20
  20.6 9.2 %copy-start.3 = (bf16[64,128,128]{2,1,0:T(8,128)(2,1)S(1)}, bf16[64,128,128]{2,1,0:T(8,128)(2,1)}, u32[]{:S(2)}) copy-start(bf16[64,128,128]{2,1,0:T(8,128)(2,1)} %param.7) | copy-start | bytes 6291460
  32.5 27.7 %slice-start = ((s8[6291456]{0:T(1024)(128)(4,1)}), s8[2097152]{0:T(1024)(128)(4,1)S(1)}, s32[]{:S(2)}) async-start(s8[6291456]{0:T(1024)(128)(4,1)} %bitcast.113), calls=%async_computation.1 | async-start | bytes 4194304
  42.4 17.9 %slice-start.1 = ((s8[6291456]{0:T(1024)(128)(4,1)}), s8[4194304]{0:T(1024)(128)(4,1)S(1)}, s32[]{:S(2)}) async-start(s8[6291456]{0:T(1024)(128)(4,1)} %bitcast.113), calls=%async_computation.2 | async-start | bytes 8388608
  42.4 17.9 %copy-start.4 = (bf16[64,128,128]{2,1,0:T(8,128)(2,1)S(1)}, bf16[64,128,128]{2,1,0:T(8,128)(2,1)}, u32[]{:S(2)}) copy-start(bf16[64,128,128]{2,1,0:T(8,128)(2,1)} %param.7) | copy-start | bytes 6291460
  54.1 22.2 %collective-permute-start.2 = (bf16[4,3,128,128]{2,3,1,0:T(8,128)(2,1)S(1)}, bf16[4,3,128,128]{2,3,1,0:T(8,128)(2,1)S(1)}, u32[]{:S(2)}, u32[]{:S(2)}) collective-permute-start(bf16[4,3,128,128]{2,3,1,0:T(8,128)(2,1)S(1)} %get-tuple-element.248), channel_id=1, source_target_pairs={{0,1},{1,2},{2,3},{3,4},{4,5},{5,6},{6,7},{7,8},{8,9},{9,10},{10,1... | collective-permute-start | bytes 1179656 | tf_op jit(solution)/shard_map/ppermute | solution.py:17
  58.6 17.9 %slice-start.3 = ((s8[6291456]{0:T(1024)(128)(4,1)}), s8[4194304]{0:T(1024)(128)(4,1)S(1)}, s32[]{:S(2)}) async-start(s8[6291456]{0:T(1024)(128)(4,1)} %bitcast.115), calls=%async_computation.4 | async-start | bytes 8388608
  58.6 17.8 %slice-start.4 = ((s8[6291456]{0:T(1024)(128)(4,1)}), s8[2097152]{0:T(1024)(128)(4,1)S(1)}, s32[]{:S(2)}) async-start(s8[6291456]{0:T(1024)(128)(4,1)} %bitcast.115), calls=%async_computation.5 | async-start | bytes 4194304
  58.7 17.8 %collective-permute-start.3 = (bf16[4,3,128,128]{2,3,1,0:T(8,128)(2,1)S(1)}, bf16[4,3,128,128]{2,3,1,0:T(8,128)(2,1)S(1)}, u32[]{:S(2)}, u32[]{:S(2)}) collective-permute-start(bf16[4,3,128,128]{2,3,1,0:T(8,128)(2,1)S(1)} %get-tuple-element.249), channel_id=1, source_target_pairs={{1,0},{2,1},{3,2},{4,3},{5,4},{6,5},{7,6},{8,7},{9,8},{10,9},{11,1... | collective-permute-start | bytes 1179656 | tf_op jit(solution)/shard_map/ppermute | solution.py:20
  99.4 674.6 %copy-start.6 = (f32[4]{0:T(128)S(1)}, f32[4]{0:T(128)}, u32[]{:S(2)}) copy-start(f32[4]{0:T(128)} %compare_convert_fusion) | copy-start | bytes 52
  140.3 15.3 %copy-start.1 = (f32[6,3,128,128]{3,0,2,1:T(8,128)S(1)}, f32[6,3,128,128]{3,0,2,1:T(8,128)}, u32[]{:S(2)}) copy-start(f32[6,3,128,128]{3,0,2,1:T(8,128)} %get-tuple-element.330) | copy-start | bytes 3538948 | tf_op jit(solution)/shard_map/while
  173.1 1.1 copy-start.2
  215.1 15.3 %copy-start.1 = (f32[6,3,128,128]{3,0,2,1:T(8,128)S(1)}, f32[6,3,128,128]{3,0,2,1:T(8,128)}, u32[]{:S(2)}) copy-start(f32[6,3,128,128]{3,0,2,1:T(8,128)} %get-tuple-element.330) | copy-start | bytes 3538948 | tf_op jit(solution)/shard_map/while
  247.8 1.1 copy-start.2
  289.9 15.3 %copy-start.1 = (f32[6,3,128,128]{3,0,2,1:T(8,128)S(1)}, f32[6,3,128,128]{3,0,2,1:T(8,128)}, u32[]{:S(2)}) copy-start(f32[6,3,128,128]{3,0,2,1:T(8,128)} %get-tuple-element.330) | copy-start | bytes 3538948 | tf_op jit(solution)/shard_map/while
  322.6 1.1 copy-start.2
  364.7 15.3 %copy-start.1 = (f32[6,3,128,128]{3,0,2,1:T(8,128)S(1)}, f32[6,3,128,128]{3,0,2,1:T(8,128)}, u32[]{:S(2)}) copy-start(f32[6,3,128,128]{3,0,2,1:T(8,128)} %get-tuple-element.330) | copy-start | bytes 3538948 | tf_op jit(solution)/shard_map/while
  397.4 1.1 copy-start.2
  439.4 15.3 %copy-start.1 = (f32[6,3,128,128]{3,0,2,1:T(8,128)S(1)}, f32[6,3,128,128]{3,0,2,1:T(8,128)}, u32[]{:S(2)}) copy-start(f32[6,3,128,128]{3,0,2,1:T(8,128)} %get-tuple-element.330) | copy-start | bytes 3538948 | tf_op jit(solution)/shard_map/while
  472.2 1.1 copy-start.2
  514.2 15.3 %copy-start.1 = (f32[6,3,128,128]{3,0,2,1:T(8,128)S(1)}, f32[6,3,128,128]{3,0,2,1:T(8,128)}, u32[]{:S(2)}) copy-start(f32[6,3,128,128]{3,0,2,1:T(8,128)} %get-tuple-element.330) | copy-start | bytes 3538948 | tf_op jit(solution)/shard_map/while
  546.9 1.1 copy-start.2
  589.0 15.3 %copy-start.1 = (f32[6,3,128,128]{3,0,2,1:T(8,128)S(1)}, f32[6,3,128,128]{3,0,2,1:T(8,128)}, u32[]{:S(2)}) copy-start(f32[6,3,128,128]{3,0,2,1:T(8,128)} %get-tuple-element.330) | copy-start | bytes 3538948 | tf_op jit(solution)/shard_map/while
  621.7 1.1 copy-start.2
  663.8 15.3 %copy-start.1 = (f32[6,3,128,128]{3,0,2,1:T(8,128)S(1)}, f32[6,3,128,128]{3,0,2,1:T(8,128)}, u32[]{:S(2)}) copy-start(f32[6,3,128,128]{3,0,2,1:T(8,128)} %get-tuple-element.330) | copy-start | bytes 3538948 | tf_op jit(solution)/shard_map/while
  696.5 1.1 copy-start.2
  738.6 15.3 %copy-start.1 = (f32[6,3,128,128]{3,0,2,1:T(8,128)S(1)}, f32[6,3,128,128]{3,0,2,1:T(8,128)}, u32[]{:S(2)}) copy-start(f32[6,3,128,128]{3,0,2,1:T(8,128)} %get-tuple-element.330) | copy-start | bytes 3538948 | tf_op jit(solution)/shard_map/while
  (1 other events, 1.1 us)
Sparse Core Ops, SparseCore 0:
  775.1 21.1 all-gather.1
where the time goes:
time: 811 us; the launch traced here: 806 us
  matrix products  356 us (44%)
  local copies, waits for them, and re-layouts  338 us (42%)
  loops' own time  30 us (4%)
  other arithmetic  29.4 us (4%)
  waiting for transfers between devices  23.5 us (3%)
  between operations  15.5 us (2%)
  starting transfers between devices  13.2 us (2%)
    dot_general x9, matrix products, accumulate(): jnp.dot(placing, flat_terms, precision=lax.Precision.HIGHEST, preferred_e...  157 us
    transpose x9, local copies, waits for them, and re-layouts, band_terms(): jnp.einsum('pkic,psid->pkscd', own_prol, band_rows, preferred_element_typ...  138 us
    dot_general x9, matrix products, band_terms(): jnp.einsum('pkqs,pkqic->psic', one_hot, products, precision=lax.Precision...  77.5 us
    dot_general x9, matrix products, band_terms(): jnp.einsum('pkic,psid->pkscd', own_prol, band_rows, preferred_element_typ...  74 us
    transpose x9, local copies, waits for them, and re-layouts, band_terms(): jnp.einsum('pkij,pkqjc->pkqic', tile_block, neighbour_prol, preferred_ele...  63.3 us
    gather x9, local copies, waits for them, and re-layouts, accumulate(): prol_window[near_rows]  37.2 us
    dot_general x9, matrix products, band_terms(): jnp.einsum('pkij,pkqjc->pkqic', tile_block, neighbour_prol, preferred_ele...  37.1 us
    another operation x1, loops' own time, local(): buffer, ignored = lax.scan(accumulate, initial, begins)  30 us
  transfers between devices with their start and end apart: 5, of which 3 were waited for; matrix products, arithmetic and copies ran while one was open for 3% of the time, Pallas kernels for 0%

commit v1 on v0

v1 whole, which is shorter than its diff:
```python
import functools

import jax
import jax.numpy as jnp
from jax import lax
from jax.experimental import pallas as pl
from jax.experimental.pallas import tpu as pltpu
from jax.sharding import PartitionSpec as P

MOSTA = 4
GRP = 8
HALF = 4
damping = 0.6
f32, bf16 = jnp.float32, jnp.bfloat16
AXES = ("region", "dev")


def row_scale(diagonal_tile):
    size = diagonal_tile.shape[0]
    on = lax.broadcasted_iota(jnp.int32, (size, size), 0) == lax.broadcasted_iota(
        jnp.int32, (size, size), 1
    )
    diag = jnp.sum(jnp.where(on, diagonal_tile.astype(f32), 0.0), axis=1, keepdims=True)
    return damping * (1.0 / jnp.where(diag == 0.0, 1.0, diag))


def dot(a, b):
    return jnp.dot(a, b, preferred_element_type=f32)


def dot_t(a, b):
    return lax.dot_general(a, b, (((0,), (0,)), ((), ())), preferred_element_type=f32)


def tall(blocks):
    return jnp.concatenate(blocks, axis=0)


def wide(blocks):
    return jnp.concatenate(blocks, axis=1)


def smooth_row(tiles, near):
    scale = row_scale(tiles[0])
    head = near[0].astype(f32) - scale * dot(tiles[0], near[0])
    rest = [-(scale * dot(tiles[k], near[k])) for k in (1, 2)]
    return [x.astype(bf16) for x in (head, *rest)]


def edges_kernel(rows, offs, tiles_hbm, basis_hbm, low_ref, high_ref, tiles, basis, sems):
    own = (lax.axis_index("region") * lax.axis_size("dev") + lax.axis_index("dev")) * rows
    copies = [
        pltpu.make_async_copy(tiles_hbm.at[pl.ds(0, 4)], tiles.at[pl.ds(0, 4)], sems.at[0]),
        pltpu.make_async_copy(basis_hbm.at[pl.ds(0, 6)], basis.at[pl.ds(0, 6)], sems.at[1]),
        pltpu.make_async_copy(tiles_hbm.at[pl.ds(rows - 4, 4)], tiles.at[pl.ds(4, 4)], sems.at[2]),
        pltpu.make_async_copy(basis_hbm.at[pl.ds(rows - 6, 6)], basis.at[pl.ds(6, 6)], sems.at[3]),
    ]
    for c in copies:
        c.start()
    for side, out in enumerate((low_ref, high_ref)):
        copies[2 * side].wait()
        copies[2 * side + 1].wait()
        for i in range(4):
            m = i if side == 0 else rows - 4 + i
            at = i if side == 0 else i + 2
            near, weights = [basis[6 * side + at]], []
            for k in range(2):
                n = at + offs[k, own + m]
                weights.append(jnp.where((n >= 0) & (n <= 5), 1.0, 0.0).astype(f32))
                near.append(basis[6 * side + jnp.clip(n, 0, 5)])
            p0, p1, p2 = smooth_row([tiles[4 * side + i, k] for k in range(3)], near)
            total = p0.astype(f32) + weights[0] * p1.astype(f32) + weights[1] * p2.astype(f32)
            out[6 + i] = total.astype(bf16)
        for i in range(2):
            e = i if side == 0 else i + 2
            for k in range(3):
                out[3 * i + k] = tiles[4 * side + e, k]
            out[10 + i] = basis[i if side == 0 else 10 + i]


def interior_kernel(
    rows, offs, aggs, tiles_hbm, basis_hbm, prol_hbm, early_ref, mid_ref, pc_ref,
    tiles, basis, prol, cols, acc, tile_sems, basis_sem, out_sems,
):
    own = (lax.axis_index("region") * lax.axis_size("dev") + lax.axis_index("dev")) * rows
    units = rows // GRP
    base = aggs[own]
    count = aggs[own + rows - 1] - base + 1

    def tile_copy(u):
        part = pl.ds(u * GRP, GRP)
        return pltpu.make_async_copy(tiles_hbm.at[part], tiles.at[part], tile_sems.at[u])

    def out_copy(u):
        part = pl.ds(u * GRP, GRP)
        return pltpu.make_async_copy(prol.at[part], prol_hbm.at[part], out_sems.at[u])

    basis_copy = pltpu.make_async_copy(basis_hbm, basis, basis_sem)
    basis_copy.start()
    for u in range(units):
        tile_copy(u).start()
    acc[...] = jnp.zeros_like(acc)
    basis_copy.wait()

    def agg_of(m):
        return aggs[own + m]

    def near_of(m):
        return [m] + [jnp.clip(m + offs[k, own + m], 0, rows - 1) for k in range(2)]

    def smooth(u):
        mine = agg_of(u * GRP)
        slot = lax.rem(mine, 2)
        for i in range(GRP):
            m = u * GRP + i
            n = near_of(m)
            row = smooth_row([tiles[m, k] for k in range(3)], [basis[x] for x in n])
            for k in range(3):
                prol[m, k] = row[k]
            p0, p1, p2 = [x.astype(f32) for x in row]
            if 2 <= i < GRP - 2:
                cols[m, slot] = (p0 + p1 + p2).astype(bf16)
                cols[m, 1 - slot] = jnp.zeros_like(row[0])
            else:
                w1, w2 = [jnp.where(agg_of(x) == mine, 1.0, 0.0).astype(f32) for x in n[1:]]
                cols[m, slot] = (p0 + w1 * p1 + w2 * p2).astype(bf16)
                cols[m, 1 - slot] = ((1.0 - w1) * p1 + (1.0 - w2) * p2).astype(bf16)

    def gather_half(h, columns_of):
        left, right = [], []
        for i in range(HALF):
            m = h * HALF + i
            n = near_of(m)
            lhs = wide([tiles[m, k] for k in range(3)])
            right.append(dot(lhs, tall([columns_of(x) for x in n])).astype(bf16))
            left.append(columns_of(m))
        return dot_t(tall(left), tall(right))

    def half(h):
        low = agg_of(h * HALF - jnp.where(lax.rem(h, 2) == 0, 1, 0))
        high = agg_of(h * HALF + jnp.where(lax.rem(h, 2) == 0, 0, HALF))

        @pl.when(low == high)
        def _():
            slot = lax.rem(low, 2)
            acc[low - base, 1] += gather_half(h, lambda x: cols[x, slot])

        @pl.when(low != high)
        def _():
            size = tiles.shape[-1]
            added = gather_half(h, lambda x: wide([cols[x, 0], cols[x, 1]]))
            at = [jnp.where(lax.rem(low, 2) == s, low, high) for s in range(2)]
            for r in range(2):
                for s in range(2):
                    acc[at[r] - base, at[s] - at[r] + 1] += added[
                        r * size : (r + 1) * size, s * size : (s + 1) * size
                    ]

    def unit(u, carry):
        tile_copy(u).wait()
        smooth(u)
        out_copy(u).start()

        @pl.when(u > 0)
        def _():
            half(2 * u - 1)
            half(2 * u)

        return carry

    lax.fori_loop(0, units, unit, 0)
    first_slot, last_slot = lax.rem(base, 2), lax.rem(agg_of(rows - 1), 2)
    for i in range(4):
        pc_ref[i] = cols[2 + i, first_slot]
        pc_ref[4 + i] = cols[rows - 6 + i, last_slot]
    early_ref[0] = acc[0, 2].astype(bf16)
    early_ref[7] = acc[count - 1, 0].astype(bf16)
    for j in (1, 2):
        kept = jnp.where(j < count - 1, 1.0, 0.0).astype(f32)
        for b in range(3):
            early_ref[3 * j - 2 + b] = (kept * acc[j, b]).astype(bf16)
    mid_ref[0] = acc[0, 1]
    mid_ref[1] = acc[count - 1, 1]
    for u in range(units):
        out_copy(u).wait()


def rim_kernel(
    rows, total, offs, low_ref, high_ref, tiles_hbm, basis_hbm, pc_ref, mid_ref, prol_in,
    prol_hbm, late_ref, tiles, basis, prol, cols, sems,
):
    own = (lax.axis_index("region") * lax.axis_size("dev") + lax.axis_index("dev")) * rows
    size = tiles.shape[-1]
    copies = [
        pltpu.make_async_copy(tiles_hbm.at[pl.ds(0, 4)], tiles.at[0, pl.ds(2, 4)], sems.at[0]),
        pltpu.make_async_copy(basis_hbm.at[pl.ds(0, 4)], basis.at[0, pl.ds(2, 4)], sems.at[1]),
        pltpu.make_async_copy(tiles_hbm.at[pl.ds(rows - 4, 4)], tiles.at[1, pl.ds(0, 4)], sems.at[2]),
        pltpu.make_async_copy(basis_hbm.at[pl.ds(rows - 4, 4)], basis.at[1, pl.ds(0, 4)], sems.at[3]),
    ]
    for c in copies:
        c.start()
    outs = []
    for side, got in enumerate((low_ref, high_ref)):
        start = -2 if side == 0 else rows - 4
        theirs = (0, 1) if side == 0 else (4, 5)
        mine = (2, 3) if side == 0 else (2, 3)
        plain = (4, 5) if side == 0 else (0, 1)
        for i, e in enumerate(theirs):
            for k in range(3):
                tiles[side, e, k] = got[3 * i + k]
            basis[side, e] = got[10 + i]
        copies[2 * side].wait()
        copies[2 * side + 1].wait()
        nb, me = (0, 1) if side == 0 else (1, 0)
        zero = jnp.zeros((size, size), bf16)

        def near_of(e):
            m = own + start + e
            inside = (m >= 0) & (m < total)
            at = jnp.clip(m, 0, total - 1)
            return [e] + [e + jnp.where(inside, offs[k, at], 0) for k in range(2)]

        def is_mine(e):
            return (e >= 2) if side == 0 else (e <= 3)

        for i in range(4):
            e = i - 2 if side == 0 else i + 4
            cols[side, 2 + e, :, nb * size : (nb + 1) * size] = got[6 + i]
            if not 0 <= e <= 5 or e not in theirs:
                cols[side, 2 + e, :, me * size : (me + 1) * size] = zero
            e = i + 4 if side == 0 else i - 2
            cols[side, 2 + e, :, me * size : (me + 1) * size] = pc_ref[4 * side + i]
            cols[side, 2 + e, :, nb * size : (nb + 1) * size] = zero
        for e in mine:
            n = near_of(e)
            row = smooth_row([tiles[side, e, k] for k in range(3)], [basis[side, jnp.clip(x, 0, 5)] for x in n])
            for k in range(3):
                prol[side, e - 2, k] = row[k]
            p0, p1, p2 = [x.astype(f32) for x in row]
            w1, w2 = [jnp.where(is_mine(x), 1.0, 0.0).astype(f32) for x in n[1:]]
            cols[side, 2 + e, :, me * size : (me + 1) * size] = (p0 + w1 * p1 + w2 * p2).astype(bf16)
            cols[side, 2 + e, :, nb * size : (nb + 1) * size] = ((1.0 - w1) * p1 + (1.0 - w2) * p2).astype(bf16)
        out = pltpu.make_async_copy(
            prol.at[side], prol_hbm.at[pl.ds(0 if side == 0 else rows - 2, 2)], sems.at[4 + side]
        )
        out.start()
        outs.append(out)
        for e in theirs:
            n = near_of(e)
            row = smooth_row([tiles[side, e, k] for k in range(3)], [basis[side, jnp.clip(x, 0, 5)] for x in n])
            p0, p1, p2 = [x.astype(f32) for x in row]
            w1, w2 = [jnp.where(is_mine(x), 1.0, 0.0).astype(f32) for x in n[1:]]
            cols[side, 2 + e, :, me * size : (me + 1) * size] = (w1 * p1 + w2 * p2).astype(bf16)
        left, right = [], []
        for e in range(6):
            n = near_of(e)
            lhs = wide([tiles[side, e, k] for k in range(3)])
            right.append(dot(lhs, tall([cols[side, 2 + x] for x in n])).astype(bf16))
            left.append(cols[side, 2 + e, :, me * size : (me + 1) * size])
        added = dot_t(tall(left), tall(right))
        if side == 0:
            late_ref[0] = added[:, :size].astype(bf16)
            late_ref[1] = (added[:, size:] + mid_ref[0]).astype(bf16)
        else:
            late_ref[2] = (added[:, :size] + mid_ref[1]).astype(bf16)
            late_ref[3] = added[:, size:].astype(bf16)
    for out in outs:
        out.wait()


def place_kernel(rows, aggs, *refs):
    out = refs[-1]
    region, dev = lax.axis_index("region"), lax.axis_index("dev")
    for j in range(4):
        late, early = refs[2 * j], refs[2 * j + 1]
        source = lax.bitwise_xor(region, j)
        own = (source * lax.axis_size("dev") + dev) * rows
        count = aggs[own + rows - 1] - aggs[own] + 1
        at = source * MOSTA
        out[at, 0] = late[0]
        out[at, 1] = late[1]
        out[at, 2] = early[0]
        for b in range(3):
            out[at + 1, b] = early[1 + b]
            out[at + 2, b] = early[4 + b]
            out[at + 3, b] = jnp.zeros_like(early[0])
        out[at + count - 1, 0] = early[7]
        out[at + count - 1, 1] = late[2]
        out[at + count - 1, 2] = late[3]


VM = pl.BlockSpec(memory_space=pltpu.VMEM)
SM = pl.BlockSpec(memory_space=pltpu.SMEM)
ANY = pl.BlockSpec(memory_space=pl.ANY)
DMA = pltpu.SemaphoreType.DMA


def cost(products, bytes_accessed):
    return pl.CostEstimate(flops=2 * 128**3 * products, bytes_accessed=bytes_accessed, transcendentals=0)


def exchange(block):
    count = lax.axis_size("region")
    across = lax.ppermute(block, "region", [(i, i ^ 2) for i in range(count)])
    beside = lax.ppermute(block, "region", [(i, i ^ 1) for i in range(count)])
    both = lax.ppermute(across, "region", [(i, i ^ 1) for i in range(count)])
    return block, beside, across, both


def local(tile_values, basis_tiles, tile_offsets, aggregate_ids):
    rows, _, size, width = tile_values.shape
    total = tile_offsets.shape[0]
    offs = tile_offsets.T
    params = pltpu.CompilerParams(vmem_limit_bytes=56 * 2**20)
    block = (size, width)
    sds = jax.ShapeDtypeStruct
    low, high = pl.pallas_call(
        functools.partial(edges_kernel, rows),
        out_shape=[sds((12, *block), bf16)] * 2,
        in_specs=[SM, ANY, ANY],
        out_specs=[VM, VM],
        scratch_shapes=[pltpu.VMEM((8, 3, *block), bf16), pltpu.VMEM((12, *block), bf16), DMA((4,))],
        compiler_params=pltpu.CompilerParams(vmem_limit_bytes=16 * 2**20),
        cost_estimate=cost(24, 2 * 10**6),
        name="edges",
    )(offs, tile_values, basis_tiles)
    devices = lax.axis_size(AXES)
    from_low = lax.ppermute(high, AXES, [(i, i + 1) for i in range(devices - 1)])
    from_high = lax.ppermute(low, AXES, [(i + 1, i) for i in range(devices - 1)])
    prol, early, mid, pc = pl.pallas_call(
        functools.partial(interior_kernel, rows),
        out_shape=[sds((rows, 3, *block), bf16), sds((8, *block), bf16), sds((2, *block), f32), sds((8, *block), bf16)],
        in_specs=[SM, SM, ANY, ANY],
        out_specs=[ANY, VM, VM, VM],
        scratch_shapes=[
            pltpu.VMEM((rows, 3, *block), bf16),
            pltpu.VMEM((rows, *block), bf16),
            pltpu.VMEM((rows, 3, *block), bf16),
            pltpu.VMEM((rows, 2, *block), bf16),
            pltpu.VMEM((MOSTA, 3, *block), f32),
            DMA((rows // GRP,)),
            DMA,
            DMA((rows // GRP,)),
        ],
        compiler_params=params,
        cost_estimate=cost(64 * 10, 16 * 10**6),
        name="interior",
    )(offs, aggregate_ids, tile_values, basis_tiles)
    early_all = exchange(early)
    prol, late = pl.pallas_call(
        functools.partial(rim_kernel, rows, total),
        out_shape=[sds((rows, 3, *block), bf16), sds((4, *block), bf16)],
        in_specs=[SM, VM, VM, ANY, ANY, VM, VM, ANY],
        out_specs=[ANY, VM],
        scratch_shapes=[
            pltpu.VMEM((2, 6, 3, *block), bf16),
            pltpu.VMEM((2, 6, *block), bf16),
            pltpu.VMEM((2, 2, 3, *block), bf16),
            pltpu.VMEM((2, 10, size, 2 * width), bf16),
            DMA((6,)),
        ],
        input_output_aliases={7: 0},
        compiler_params=pltpu.CompilerParams(vmem_limit_bytes=16 * 2**20),
        cost_estimate=cost(140, 3 * 10**6),
        name="rim",
    )(offs, from_low, from_high, tile_values, basis_tiles, pc, mid, prol)
    late_all = exchange(late)
    operands = [x for pair in zip(late_all, early_all) for x in pair]
    coarse = pl.pallas_call(
        functools.partial(place_kernel, rows),
        out_shape=sds((4 * MOSTA, 3, *block), bf16),
        in_specs=[SM] + [VM] * 8,
        out_specs=VM,
        compiler_params=pltpu.CompilerParams(vmem_limit_bytes=16 * 2**20),
        cost_estimate=cost(0, 3 * 10**6),
        name="place",
    )(aggregate_ids, *operands)
    return prol, coarse


def solution(mesh):
    placed = (P(AXES, None, None, None), P(AXES, None, None), P(), P())
    return jax.shard_map(
        local,
        mesh=mesh,
        in_specs=placed,
        out_specs=(P(AXES, None, None, None), P("dev", None, None, None)),
        check_vma=False,
    )
```

time: 811 us -> 59.9 us (0.07)
  matrix products: 356 us -> 0 us
  local copies, waits for them, and re-layouts: 338 us -> 8.55 us
  loops' own time: 30 us -> 0 us
  other arithmetic: 29.4 us -> 0.01 us
  Pallas kernels: 0 us -> 24.2 us
  between operations: 15.5 us -> 0.75 us
  waiting for transfers between devices: 23.5 us -> 11.5 us
    dot_general x37 -> x0, matrix products: 356 us -> none  [the longest x9 157 us: accumulate(): jnp.dot(placing, flat_terms, precision=lax.Precision.HIGHEST, preferred_e...]
    transpose x18 -> x0, local copies, waits for them, and re-layouts: 201 us -> none  [the longest x9 138 us: band_terms(): jnp.einsum('pkic,psid->pkscd', own_prol, band_rows, preferred_element_typ...]
    gather x74 -> x0, local copies, waits for them, and re-layouts: 73.7 us -> none  [the longest x9 37.2 us: accumulate(): prol_window[near_rows]]
    another operation x1 -> x0, loops' own time: 30 us -> none  [local(): buffer, ignored = lax.scan(accumulate, initial, begins)]
    pallas_call x0 -> x4, Pallas kernels: none -> 24.2 us  [the longest x1 16.2 us: local(): pl.pallas_call(functools.partial(interior_kernel, rows), out_shape=[sds((...]
    unnamed x23 -> x22, local copies, waits for them, and re-layouts: 25.9 us -> 8.55 us
    all_gather x1 -> x0, waiting for transfers between devices: 12.7 us -> none  [local(): relayed = lax.all_gather(coarse, 'region', axis=0, tiled=True)]
    while x37 -> x0, local copies, waits for them, and re-layouts: 11.9 us -> none
  transfers between devices with their start and end apart: 5 -> 8, of which waited for: 3 -> 3; matrix products, arithmetic and copies ran while one was open for 3% -> 0% of each run, Pallas kernels for 0% -> 33%
where the time goes in v1:
time: 59.9 us; the launch traced here: 59.5 us
  Pallas kernels  24.2 us (40%)
  starting transfers between devices  14.6 us (24%)
  waiting for transfers between devices  11.5 us (19%)
  local copies, waits for them, and re-layouts  8.55 us (14%)
  between operations  0.75 us (1%)
    pallas_call x1, Pallas kernels, local(): pl.pallas_call(functools.partial(interior_kernel, rows), out_shape=[sds((...  16.2 us
    ppermute x2, waiting for transfers between devices, exchange(): across = lax.ppermute(block, 'region', [(i, i ^ 2) for i in range(count)])  10.2 us
    unnamed x22, local copies, waits for them, and re-layouts  8.55 us
    ppermute x2, starting transfers between devices, exchange(): across = lax.ppermute(block, 'region', [(i, i ^ 2) for i in range(count)])  8.01 us
    ppermute x1, starting transfers between devices, local(): lax.ppermute(high, AXES, [(i, i + 1) for i in range(devices - 1)])  4.9 us
    pallas_call x1, Pallas kernels, local(): pl.pallas_call(functools.partial(rim_kernel, rows, total), out_shape=[sds...  3.57 us
    pallas_call x1, Pallas kernels, local(): pl.pallas_call(functools.partial(edges_kernel, rows), out_shape=[sds((12,...  2.43 us
    pallas_call x1, Pallas kernels, local(): pl.pallas_call(functools.partial(place_kernel, rows), out_shape=sds((4 *...  1.98 us
  transfers between devices with their start and end apart: 8, of which 3 were waited for; matrix products, arithmetic and copies ran while one was open for 0% of the time, Pallas kernels for 33%

profile of v1, /device:TPU:0, one launch (start us, length us, event | category | flops | bytes accessed | tf_op | source)
XLA Modules:
  0.0 59.5 jit_solution(15573482275796478161)
XLA Ops:
  0.6 0.0 copy-start
  0.6 2.8 %copy-done = bf16[64,3,128,128]{3,2,1,0:T(8,128)(2,1)S(1)} copy-done((bf16[64,3,128,128]{3,2,1,0:T(8,128)(2,1)S(1)}, bf16[64,3,128,128]{3,2,1,0:T(8,128)(2,1)}, u32[]{:S(2)}) %copy-start) | copy-done | bytes 6291480
  3.4 1.6 %copy-done.1 = bf16[64,128,128]{2,1,0:T(8,128)(2,1)S(1)} copy-done((bf16[64,128,128]{2,1,0:T(8,128)(2,1)S(1)}, bf16[64,128,128]{2,1,0:T(8,128)(2,1)}, u32[]{:S(2)}) %copy-start.1) | copy-done | bytes 2097176
  5.0 0.7 %copy-done.6 = s32[2048,2]{0,1:T(2,128)S(1)} copy-done((s32[2048,2]{0,1:T(2,128)S(1)}, s32[2048,2]{0,1:T(2,128)}, u32[]{:S(2)}) %copy-start.6) | copy-done | bytes 16408
  5.7 2.4 %edges.1 = (bf16[12,128,128]{2,1,0:T(8,128)(2,1)S(1)}, bf16[12,128,128]{2,1,0:T(8,128)(2,1)S(1)}) custom-call(s32[2,2048]{1,0:T(2,128)S(1)} %bitcast.4, bf16[64,3,128,128]{3,2,1,0:T(8,128)(2,1)S(1)} %copy-done, bf16[64,128,128]{2,1,0:T(8,128)(2,1)S(1)} %copy-done.1), custom_call_target="tpu_custom_call" | custom-call | flops 100663296 | bytes 2000000 | tf_op jit(solution)/shard_map/edges/pallas_call | solution.py:317
  8.2 0.0 copy-start.7
  8.2 4.9 %collective-permute-start = (bf16[12,128,128]{2,1,0:T(8,128)(2,1)S(1)}, bf16[12,128,128]{2,1,0:T(8,128)(2,1)S(1)}, u32[]{:S(2)}, u32[]{:S(2)}) collective-permute-start(bf16[12,128,128]{2,1,0:T(8,128)(2,1)S(1)} %get-tuple-element.10), channel_id=1, source_target_pairs={{0,1},{1,2},{2,3},{3,4},{4,5},{5,6},{6,7},{7,8},{8,9},{9,10},{10,1... | collective-permute-start | bytes 1179656 | tf_op jit(solution)/shard_map/ppermute | solution.py:328
  13.1 0.0 slice-start.1
  13.1 1.4 %collective-permute-start.1 = (bf16[12,128,128]{2,1,0:T(8,128)(2,1)S(1)}, bf16[12,128,128]{2,1,0:T(8,128)(2,1)S(1)}, u32[]{:S(2)}, u32[]{:S(2)}) collective-permute-start(bf16[12,128,128]{2,1,0:T(8,128)(2,1)S(1)} %get-tuple-element.11), channel_id=1, source_target_pairs={{1,0},{2,1},{3,2},{4,3},{5,4},{6,5},{7,6},{8,7},{9,8},{10,9},{11,1... | collective-permute-start | bytes 1179656 | tf_op jit(solution)/shard_map/ppermute | solution.py:329
  14.5 16.2 %interior.1 = (bf16[64,3,128,128]{3,2,1,0:T(8,128)(2,1)}, bf16[8,128,128]{2,1,0:T(8,128)(2,1)}, f32[2,128,128]{2,1,0:T(8,128)}, bf16[8,128,128]{2,1,0:T(8,128)(2,1)}) custom-call(s32[2,2048]{1,0:T(2,128)} %bitcast.3, s32[2048]{0:T(1024)} %aggs.3, bf16[64,3,128,128]{3,2,1,0:T(8,128)(2,1)} %tiles_hbm.5, bf16[64,128,128]{2,1,0:T(8,128)(2,1)} %basis_hbm.5), custom_call_target="tpu_custom_call" | custom-call | flops 2684354560 | bytes 16000000 | tf_op jit(solution)/shard_map/interior/pallas_call | solution.py:330
  30.7 6.4 %collective-permute-start.5 = (bf16[8,128,128]{2,1,0:T(8,128)(2,1)}, bf16[8,128,128]{2,1,0:T(8,128)(2,1)S(1)}, u32[]{:S(2)}, u32[]{:S(2)}) collective-permute-start(bf16[8,128,128]{2,1,0:T(8,128)(2,1)} %get-tuple-element.17.refs_1_), channel_id=1, source_target_pairs={{0,16},{8,24},{16,0},{24,8},{1,17},{9,25},{17,1},{25,9},{2,18},{10... | collective-permute-start | bytes 786440 | tf_op jit(solution)/shard_map/ppermute | solution.py:304
  37.2 0.0 collective-permute-start.3
  37.2 6.0 %collective-permute-done.5.refs_5_ = bf16[8,128,128]{2,1,0:T(8,128)(2,1)S(1)} collective-permute-done((bf16[8,128,128]{2,1,0:T(8,128)(2,1)}, bf16[8,128,128]{2,1,0:T(8,128)(2,1)S(1)}, u32[]{:S(2)}, u32[]{:S(2)}) %collective-permute-start.5) | collective-permute-done | bytes 262176 | tf_op jit(solution)/shard_map/ppermute | solution.py:304
  43.2 0.0 collective-permute-start.7
  43.2 0.0 collective-permute-done.low_ref
  43.2 0.0 collective-permute-done.1.high_ref
  43.2 0.0 slice-done
  43.2 0.0 copy-start.2
  43.2 1.6 %copy-done.2 = bf16[64,128,128]{2,1,0:T(8,128)(2,1)S(1)} copy-done((bf16[64,128,128]{2,1,0:T(8,128)(2,1)S(1)}, bf16[64,128,128]{2,1,0:T(8,128)(2,1)}, u32[]{:S(2)}) %copy-start.2) | copy-done | bytes 2097176
  44.8 0.9 %copy-done.3 = bf16[8,128,128]{2,1,0:T(8,128)(2,1)S(1)} copy-done((bf16[8,128,128]{2,1,0:T(8,128)(2,1)S(1)}, bf16[8,128,128]{2,1,0:T(8,128)(2,1)}, u32[]{:S(2)}) %copy-start.3) | copy-done | bytes 262168
  45.8 0.9 %copy-done.5 = f32[2,128,128]{2,1,0:T(8,128)S(1)} copy-done((f32[2,128,128]{2,1,0:T(8,128)S(1)}, f32[2,128,128]{2,1,0:T(8,128)}, u32[]{:S(2)}) %copy-start.5) | copy-done | bytes 131096
  46.7 3.6 %rim.1 = (bf16[64,3,128,128]{3,2,1,0:T(8,128)(2,1)}, bf16[4,128,128]{2,1,0:T(8,128)(2,1)S(1)}) custom-call(s32[2,2048]{1,0:T(2,128)S(1)} %bitcast.5, bf16[12,128,128]{2,1,0:T(8,128)(2,1)S(1)} %collective-permute-done.low_ref, bf16[12,128,128]{2,1,0:T(8,128)(2,1)S(1)} %collective-permute-done.1.high_ref, ...), custom_call_target="tpu_custom_call", output_to_operand_aliasing={{0}: (7, {})} | custom-call | flops 587202560 | bytes 3000000 | tf_op jit(solution)/shard_map/rim/pallas_call | solution.py:350
  50.2 1.6 %collective-permute-start.4 = (bf16[4,128,128]{2,1,0:T(8,128)(2,1)S(1)}, bf16[4,128,128]{2,1,0:T(8,128)(2,1)S(1)}, u32[]{:S(2)}, u32[]{:S(2)}) collective-permute-start(bf16[4,128,128]{2,1,0:T(8,128)(2,1)S(1)} %get-tuple-element.16.refs_0_), channel_id=1, source_target_pairs={{0,16},{8,24},{16,0},{24,8},{1,17},{9,25},{17,1},{25,9},{2,18},{10... | collective-permute-start | bytes 393224 | tf_op jit(solution)/shard_map/ppermute | solution.py:304
  51.8 0.2 collective-permute-start.2
  52.0 4.2 %collective-permute-done.4.refs_4_ = bf16[4,128,128]{2,1,0:T(8,128)(2,1)S(1)} collective-permute-done((bf16[4,128,128]{2,1,0:T(8,128)(2,1)S(1)}, bf16[4,128,128]{2,1,0:T(8,128)(2,1)S(1)}, u32[]{:S(2)}, u32[]{:S(2)}) %collective-permute-start.4) | collective-permute-done | bytes 131104 | tf_op jit(solution)/shard_map/ppermute | solution.py:304
  56.2 0.0 collective-permute-start.6
  56.2 0.0 collective-permute-done.3.refs_3_
  56.2 0.0 collective-permute-done.2.refs_2_
  56.2 0.0 collective-permute-done.7.refs_7_
  56.2 1.3 %collective-permute-done.6.refs_6_ = bf16[4,128,128]{2,1,0:T(8,128)(2,1)S(1)} collective-permute-done((bf16[4,128,128]{2,1,0:T(8,128)(2,1)S(1)}, bf16[4,128,128]{2,1,0:T(8,128)(2,1)S(1)}, u32[]{:S(2)}, u32[]{:S(2)}) %collective-permute-start.6) | collective-permute-done | bytes 131104 | tf_op jit(solution)/shard_map/ppermute | solution.py:306
  57.6 0.0 copy-done.4
  57.6 2.0 %place.1 = bf16[16,3,128,128]{3,2,1,0:T(8,128)(2,1)} custom-call(s32[2048]{0:T(1024)S(1)} %copy-done.8, bf16[4,128,128]{2,1,0:T(8,128)(2,1)S(1)} %get-tuple-element.16.refs_0_, bf16[8,128,128]{2,1,0:T(8,128)(2,1)S(1)} %copy-done.4, bf16[4,128,128]{2,1,0:T(8,128)(2,1)S(1)} %collective-permute-done.2.refs_2_, ...), custom_call_target="tpu_custom_call" | custom-call | bytes 3000000 | tf_op jit(solution)/shard_map/place/pallas_call | solution.py:369
  (11 shorter events, 0.0 us)
Async XLA Ops:
  0.6 2.8 %copy-start = (bf16[64,3,128,128]{3,2,1,0:T(8,128)(2,1)S(1)}, bf16[64,3,128,128]{3,2,1,0:T(8,128)(2,1)}, u32[]{:S(2)}) copy-start(bf16[64,3,128,128]{3,2,1,0:T(8,128)(2,1)} %tiles_hbm.5) | copy-start | bytes 18874372
  3.4 1.6 %copy-start.1 = (bf16[64,128,128]{2,1,0:T(8,128)(2,1)S(1)}, bf16[64,128,128]{2,1,0:T(8,128)(2,1)}, u32[]{:S(2)}) copy-start(bf16[64,128,128]{2,1,0:T(8,128)(2,1)} %basis_hbm.5) | copy-start | bytes 6291460
  5.0 0.7 %copy-start.6 = (s32[2048,2]{0,1:T(2,128)S(1)}, s32[2048,2]{0,1:T(2,128)}, u32[]{:S(2)}) copy-start(s32[2048,2]{0,1:T(2,128)} %param.6) | copy-start | bytes 49156
  5.7 37.5 %slice-start = ((s8[6291456]{0:T(1024)(128)(4,1)}), s8[4194304]{0:T(1024)(128)(4,1)S(1)}, s32[]{:S(2)}) async-start(s8[6291456]{0:T(1024)(128)(4,1)} %bitcast.1), calls=%async_computation | async-start | bytes 8388608
  8.2 35.0 %copy-start.7 = (s32[2048,2]{0,1:T(2,128)S(1)}, s32[2048,2]{0,1:T(2,128)}, u32[]{:S(2)}) copy-start(s32[2048,2]{0,1:T(2,128)} %param.6) | copy-start | bytes 49156
  8.2 35.0 %collective-permute-start = (bf16[12,128,128]{2,1,0:T(8,128)(2,1)S(1)}, bf16[12,128,128]{2,1,0:T(8,128)(2,1)S(1)}, u32[]{:S(2)}, u32[]{:S(2)}) collective-permute-start(bf16[12,128,128]{2,1,0:T(8,128)(2,1)S(1)} %get-tuple-element.10), channel_id=1, source_target_pairs={{0,1},{1,2},{2,3},{3,4},{4,5},{5,6},{6,7},{7,8},{8,9},{9,10},{10,1... | collective-permute-start | bytes 1179656 | tf_op jit(solution)/shard_map/ppermute | solution.py:328
  13.1 30.1 %slice-start.1 = ((s8[6291456]{0:T(1024)(128)(4,1)}), s8[2097152]{0:T(1024)(128)(4,1)S(1)}, s32[]{:S(2)}) async-start(s8[6291456]{0:T(1024)(128)(4,1)} %bitcast.1), calls=%async_computation.1 | async-start | bytes 4194304
  13.1 30.1 %collective-permute-start.1 = (bf16[12,128,128]{2,1,0:T(8,128)(2,1)S(1)}, bf16[12,128,128]{2,1,0:T(8,128)(2,1)S(1)}, u32[]{:S(2)}, u32[]{:S(2)}) collective-permute-start(bf16[12,128,128]{2,1,0:T(8,128)(2,1)S(1)} %get-tuple-element.11), channel_id=1, source_target_pairs={{1,0},{2,1},{3,2},{4,3},{5,4},{6,5},{7,6},{8,7},{9,8},{10,9},{11,1... | collective-permute-start | bytes 1179656 | tf_op jit(solution)/shard_map/ppermute | solution.py:329
  30.7 12.4 %collective-permute-start.5 = (bf16[8,128,128]{2,1,0:T(8,128)(2,1)}, bf16[8,128,128]{2,1,0:T(8,128)(2,1)S(1)}, u32[]{:S(2)}, u32[]{:S(2)}) collective-permute-start(bf16[8,128,128]{2,1,0:T(8,128)(2,1)} %get-tuple-element.17.refs_1_), channel_id=1, source_target_pairs={{0,16},{8,24},{16,0},{24,8},{1,17},{9,25},{17,1},{25,9},{2,18},{10... | collective-permute-start | bytes 786440 | tf_op jit(solution)/shard_map/ppermute | solution.py:304
  37.2 19.1 %collective-permute-start.3 = (bf16[8,128,128]{2,1,0:T(8,128)(2,1)}, bf16[8,128,128]{2,1,0:T(8,128)(2,1)S(1)}, u32[]{:S(2)}, u32[]{:S(2)}) collective-permute-start(bf16[8,128,128]{2,1,0:T(8,128)(2,1)} %get-tuple-element.17.refs_1_), channel_id=1, source_target_pairs={{0,8},{8,0},{16,24},{24,16},{1,9},{9,1},{17,25},{25,17},{2,10},{10... | collective-permute-start | bytes 786440 | tf_op jit(solution)/shard_map/ppermute | solution.py:305
  43.2 13.1 %collective-permute-start.7 = (bf16[8,128,128]{2,1,0:T(8,128)(2,1)S(1)}, bf16[8,128,128]{2,1,0:T(8,128)(2,1)S(1)}, u32[]{:S(2)}, u32[]{:S(2)}) collective-permute-start(bf16[8,128,128]{2,1,0:T(8,128)(2,1)S(1)} %collective-permute-done.5.refs_5_), channel_id=1, source_target_pairs={{0,8},{8,0},{16,24},{24,16},{1,9},{9,1},{17,25},{25,17},{2,10},{10... | collective-permute-start | bytes 786440 | tf_op jit(solution)/shard_map/ppermute | solution.py:306
  43.2 1.6 %copy-start.2 = (bf16[64,128,128]{2,1,0:T(8,128)(2,1)S(1)}, bf16[64,128,128]{2,1,0:T(8,128)(2,1)}, u32[]{:S(2)}) copy-start(bf16[64,128,128]{2,1,0:T(8,128)(2,1)} %basis_hbm.5) | copy-start | bytes 6291460
  44.8 0.9 %copy-start.3 = (bf16[8,128,128]{2,1,0:T(8,128)(2,1)S(1)}, bf16[8,128,128]{2,1,0:T(8,128)(2,1)}, u32[]{:S(2)}) copy-start(bf16[8,128,128]{2,1,0:T(8,128)(2,1)} %get-tuple-element.12.pc_ref) | copy-start | bytes 786436
  45.8 0.9 %copy-start.5 = (f32[2,128,128]{2,1,0:T(8,128)S(1)}, f32[2,128,128]{2,1,0:T(8,128)}, u32[]{:S(2)}) copy-start(f32[2,128,128]{2,1,0:T(8,128)} %get-tuple-element.13.mid_ref) | copy-start | bytes 393220
  46.7 10.9 %copy-start.4 = (bf16[8,128,128]{2,1,0:T(8,128)(2,1)S(1)}, bf16[8,128,128]{2,1,0:T(8,128)(2,1)}, u32[]{:S(2)}) copy-start(bf16[8,128,128]{2,1,0:T(8,128)(2,1)} %get-tuple-element.17.refs_1_) | copy-start | bytes 786436
  46.7 10.9 %copy-start.8 = (s32[2048]{0:T(1024)S(1)}, s32[2048]{0:T(1024)}, u32[]{:S(2)}) copy-start(s32[2048]{0:T(1024)} %aggs.3) | copy-start | bytes 24580
  50.2 6.0 %collective-permute-start.4 = (bf16[4,128,128]{2,1,0:T(8,128)(2,1)S(1)}, bf16[4,128,128]{2,1,0:T(8,128)(2,1)S(1)}, u32[]{:S(2)}, u32[]{:S(2)}) collective-permute-start(bf16[4,128,128]{2,1,0:T(8,128)(2,1)S(1)} %get-tuple-element.16.refs_0_), channel_id=1, source_target_pairs={{0,16},{8,24},{16,0},{24,8},{1,17},{9,25},{17,1},{25,9},{2,18},{10... | collective-permute-start | bytes 393224 | tf_op jit(solution)/shard_map/ppermute | solution.py:304
  51.8 4.4 %collective-permute-start.2 = (bf16[4,128,128]{2,1,0:T(8,128)(2,1)S(1)}, bf16[4,128,128]{2,1,0:T(8,128)(2,1)S(1)}, u32[]{:S(2)}, u32[]{:S(2)}) collective-permute-start(bf16[4,128,128]{2,1,0:T(8,128)(2,1)S(1)} %get-tuple-element.16.refs_0_), channel_id=1, source_target_pairs={{0,8},{8,0},{16,24},{24,16},{1,9},{9,1},{17,25},{25,17},{2,10},{10... | collective-permute-start | bytes 393224 | tf_op jit(solution)/shard_map/ppermute | solution.py:305
  56.2 1.3 %collective-permute-start.6 = (bf16[4,128,128]{2,1,0:T(8,128)(2,1)S(1)}, bf16[4,128,128]{2,1,0:T(8,128)(2,1)S(1)}, u32[]{:S(2)}, u32[]{:S(2)}) collective-permute-start(bf16[4,128,128]{2,1,0:T(8,128)(2,1)S(1)} %collective-permute-done.4.refs_4_), channel_id=1, source_target_pairs={{0,8},{8,0},{16,24},{24,16},{1,9},{9,1},{17,25},{25,17},{2,10},{10... | collective-permute-start | bytes 393224 | tf_op jit(solution)/shard_map/ppermute | solution.py:306

commit v2 on v1

v2 whole, which is shorter than its diff:
```python
import functools

import jax
import jax.numpy as jnp
from jax import lax
from jax.experimental import pallas as pl
from jax.experimental.pallas import tpu as pltpu
from jax.sharding import PartitionSpec as P

MOSTA = 4
GRP = 8
HALF = 4
damping = 0.6
f32, bf16 = jnp.float32, jnp.bfloat16
AXES = ("region", "dev")
LIMITS = (16.0, 40.0, 16.0)


def row_scale(diagonal_tile):
    size = diagonal_tile.shape[0]
    on = lax.broadcasted_iota(jnp.int32, (size, size), 0) == lax.broadcasted_iota(
        jnp.int32, (size, size), 1
    )
    kept = jnp.where(on, diagonal_tile, jnp.zeros_like(diagonal_tile))
    diag = dot(kept, jnp.ones_like(kept))
    return -damping * (1.0 / jnp.where(diag == 0.0, 1.0, diag))


def dot(a, b):
    return jnp.dot(a, b, preferred_element_type=f32)


def dot_t(a, b):
    return lax.dot_general(a, b, (((0,), (0,)), ((), ())), preferred_element_type=f32)


def tall(blocks):
    return jnp.concatenate(blocks, axis=0)


def wide(blocks):
    return jnp.concatenate(blocks, axis=1)


def smooth_row(tiles, near):
    scale = row_scale(tiles[0])
    head = near[0].astype(f32) + scale * dot(tiles[0], near[0])
    rest = [scale * dot(tiles[k], near[k]) for k in (1, 2)]
    return [x.astype(bf16) for x in (head, *rest)]


def place_of(rows):
    return (lax.axis_index("region") * lax.axis_size("dev") + lax.axis_index("dev")) * rows


def offsets_copy(own, total, offs_hbm, offs, sem):
    start = pl.multiple_of(jnp.clip((own - 2) // 128 * 128, 0, total - 256), 128)
    return start, pltpu.make_async_copy(offs_hbm.at[:, pl.ds(start, 256)], offs, sem)


def edges_kernel(
    rows, total, offs_hbm, tiles_hbm, basis_hbm, low_ref, high_ref, keep_ref, offs, basis, sems
):
    own = place_of(rows)
    start, offs_in = offsets_copy(own, total, offs_hbm, offs, sems.at[6])
    copies = []
    for side, out in enumerate((low_ref, high_ref)):
        outer, inner, far = (0, 2, 0) if side == 0 else (rows - 2, rows - 4, rows - 6)
        copies.append(
            [
                pltpu.make_async_copy(basis_hbm.at[pl.ds(far, 6)], basis.at[side], sems.at[3 * side]),
                pltpu.make_async_copy(tiles_hbm.at[pl.ds(outer, 2)], out.at[pl.ds(0, 2)], sems.at[3 * side + 1]),
                pltpu.make_async_copy(
                    tiles_hbm.at[pl.ds(inner, 2)], keep_ref.at[side, pl.ds(0, 2)], sems.at[3 * side + 2]
                ),
            ]
        )
    offs_in.start()
    for group in copies:
        for c in group:
            c.start()
    offs_in.wait()
    for side, out in enumerate((low_ref, high_ref)):
        for c in copies[side]:
            c.wait()
        for i in range(4):
            m = i if side == 0 else rows - 4 + i
            at = i if side == 0 else i + 2
            outer = (i < 2) == (side == 0)
            held = out.at[i % 2] if outer else keep_ref.at[side, i % 2]
            near, weights = [basis[side, at]], []
            for k in range(2):
                n = at + offs[k, own - start + m]
                weights.append(jnp.where((n >= 0) & (n <= 5), 1.0, 0.0).astype(f32))
                near.append(basis[side, jnp.clip(n, 0, 5)])
            p0, p1, p2 = smooth_row([held[k] for k in range(3)], near)
            sum_ = p0.astype(f32) + weights[0] * p1.astype(f32) + weights[1] * p2.astype(f32)
            out[2 + i // 3, i % 3] = sum_.astype(bf16)
        for i in range(2):
            out[3, 1 + i] = basis[side, i if side == 0 else 4 + i]
            keep_ref[side, 2, i] = basis[side, 2 + i]
        keep_ref[side, 2, 2] = jnp.zeros(basis.shape[2:], bf16)


def interior_kernel(
    rows, total, offs_hbm, aggs_hbm, tiles_hbm, basis_hbm, prol_hbm, early_ref, mid_ref, pc_ref,
    offs, aggs, tiles, basis, prol, cols, acc, tile_sems, basis_sems, out_sems, small_sems,
):
    own = place_of(rows)
    units = rows // GRP
    start, offs_in = offsets_copy(own, total, offs_hbm, offs, small_sems.at[0])
    aggs_in = pltpu.make_async_copy(aggs_hbm, aggs, small_sems.at[1])

    def part_of(u):
        return pl.ds(u * GRP, GRP)

    def tile_copy(u):
        return pltpu.make_async_copy(tiles_hbm.at[part_of(u)], tiles.at[part_of(u)], tile_sems.at[u])

    def basis_copy(u):
        return pltpu.make_async_copy(basis_hbm.at[part_of(u)], basis.at[part_of(u)], basis_sems.at[u])

    def out_copy(u):
        return pltpu.make_async_copy(prol.at[part_of(u)], prol_hbm.at[part_of(u)], out_sems.at[u])

    offs_in.start()
    aggs_in.start()
    basis_copy(0).start()
    for u in range(units):
        tile_copy(u).start()
        if u < units - 1:
            basis_copy(u + 1).start()
    acc[...] = jnp.zeros_like(acc)
    offs_in.wait()
    aggs_in.wait()
    basis_copy(0).wait()
    base = aggs[own]
    count = aggs[own + rows - 1] - base + 1

    def agg_of(m):
        return aggs[own + m]

    def near_of(m):
        return [m] + [jnp.clip(m + offs[k, own - start + m], 0, rows - 1) for k in range(2)]

    def smooth(u):
        mine = agg_of(u * GRP)
        slot = lax.rem(mine, 2)
        for i in range(GRP):
            m = u * GRP + i
            n = near_of(m)
            row = smooth_row([tiles[m, k] for k in range(3)], [basis[x] for x in n])
            for k in range(3):
                prol[m, k] = row[k]
            p0, p1, p2 = [x.astype(f32) for x in row]
            if 2 <= i < GRP - 2:
                cols[m, slot] = (p0 + p1 + p2).astype(bf16)
                cols[m, 1 - slot] = jnp.zeros_like(row[0])
            else:
                w1, w2 = [jnp.where(agg_of(x) == mine, 1.0, 0.0).astype(f32) for x in n[1:]]
                cols[m, slot] = (p0 + w1 * p1 + w2 * p2).astype(bf16)
                cols[m, 1 - slot] = ((1.0 - w1) * p1 + (1.0 - w2) * p2).astype(bf16)

    def window(w, columns_of):
        left, right = [], []
        for i in range(GRP):
            m = w * GRP - HALF + i
            lhs = wide([tiles[m, k] for k in range(3)])
            right.append(dot(lhs, tall([columns_of(x) for x in near_of(m)])).astype(bf16))
            left.append(columns_of(m))
        return dot_t(tall(left), tall(right))

    def step(w, u):
        low, high = agg_of((w - 1) * GRP), agg_of(w * GRP)

        @pl.when(low == high)
        def _():
            slot = lax.rem(low, 2)
            added = window(w, lambda x: cols[x, slot])
            if u is not None:
                smooth(u)
            acc[low - base, 1] += added

        @pl.when(low != high)
        def _():
            size = tiles.shape[-1]
            added = window(w, lambda x: wide([cols[x, 0], cols[x, 1]]))
            if u is not None:
                smooth(u)
            at = [jnp.where(lax.rem(low, 2) == s, low, high) for s in range(2)]
            for r in range(2):
                for s in range(2):
                    acc[at[r] - base, at[s] - at[r] + 1] += added[
                        r * size : (r + 1) * size, s * size : (s + 1) * size
                    ]

    def arrived(u):
        tile_copy(u).wait()

        @pl.when(u < units - 1)
        def _():
            basis_copy(u + 1).wait()

    for u in range(2):
        arrived(u)
        smooth(u)
        out_copy(u).start()

    def unit(u, carry):
        arrived(u)
        step(u - 1, u)
        out_copy(u).start()
        return carry

    lax.fori_loop(2, units, unit, 0)
    step(units - 1, None)
    first_slot, last_slot = lax.rem(base, 2), lax.rem(agg_of(rows - 1), 2)
    for i in range(4):
        pc_ref[i] = cols[2 + i, first_slot]
        pc_ref[4 + i] = cols[rows - 6 + i, last_slot]
    early_ref[0] = acc[0, 2].astype(bf16)
    early_ref[7] = acc[count - 1, 0].astype(bf16)
    for j in (1, 2):
        kept = jnp.where(j < count - 1, 1.0, 0.0).astype(f32)
        for b in range(3):
            early_ref[3 * j - 2 + b] = (kept * acc[j, b]).astype(bf16)
    mid_ref[0] = acc[0, 1]
    mid_ref[1] = acc[count - 1, 1]
    for u in range(units):
        out_copy(u).wait()


def rim_kernel(
    rows, total, offs_hbm, low_got, high_got, low_own, high_own, keep_ref, pc_ref, mid_ref, prol_in,
    prol_hbm, late_ref, offs, prol, cols, sems,
):
    own = place_of(rows)
    size = cols.shape[-2]
    start, offs_in = offsets_copy(own, total, offs_hbm, offs, sems.at[2])
    offs_in.start()
    offs_in.wait()
    outs = []
    for side, (got, sent) in enumerate(((low_got, low_own), (high_got, high_own))):
        first = -2 if side == 0 else rows - 4
        theirs, mine, plain = ((0, 1), (2, 3), (4, 5)) if side == 0 else ((4, 5), (2, 3), (0, 1))
        nb, me = (0, 1) if side == 0 else (1, 0)
        zero = jnp.zeros((size, size), bf16)
        basis = [None] * 6
        held = [None] * 6
        for i in range(2):
            held[theirs[i]], held[mine[i]], held[plain[i]] = got.at[i], sent.at[i], keep_ref.at[side, i]

        def basis_of(x):
            order = (got, sent, None) if side == 0 else (None, sent, got)
            where = jnp.clip(x, 0, 5)
            out = None
            for group, source in enumerate(order):
                block = (
                    keep_ref[side, 2, lax.rem(where, 2)] if source is None else source[3, 1 + lax.rem(where, 2)]
                )
                out = block if out is None else jnp.where(where // 2 == group, block, out)
            return out

        def near_of(e):
            m = own + first + e
            inside = (m >= 0) & (m < total)
            at = jnp.clip(m, 0, total - 1) - start
            return [e] + [e + jnp.where(inside, offs[k, at], 0) for k in range(2)]

        def is_mine(e):
            return (e >= 2) if side == 0 else (e <= 3)

        def put(e, which, block):
            cols[side, 2 + e, :, which * size : (which + 1) * size] = block

        for i in range(4):
            e = i - 2 if side == 0 else i + 4
            put(e, nb, got[2 + i // 3, i % 3])
            if e not in theirs:
                put(e, me, zero)
            e = i + 4 if side == 0 else i - 2
            put(e, me, pc_ref[4 * side + i])
            put(e, nb, zero)
        for e in (*mine, *theirs):
            n = near_of(e)
            row = smooth_row([held[e][k] for k in range(3)], [basis_of(x) for x in n])
            p0, p1, p2 = [x.astype(f32) for x in row]
            w1, w2 = [jnp.where(is_mine(x), 1.0, 0.0).astype(f32) for x in n[1:]]
            if e in mine:
                for k in range(3):
                    prol[side, e - 2, k] = row[k]
                put(e, me, (p0 + w1 * p1 + w2 * p2).astype(bf16))
                put(e, nb, ((1.0 - w1) * p1 + (1.0 - w2) * p2).astype(bf16))
            else:
                put(e, me, (w1 * p1 + w2 * p2).astype(bf16))
        out = pltpu.make_async_copy(
            prol.at[side], prol_hbm.at[pl.ds(0 if side == 0 else rows - 2, 2)], sems.at[side]
        )
        out.start()
        outs.append(out)
        left, right = [], []
        for e in range(6):
            n = near_of(e)
            lhs = wide([held[e][k] for k in range(3)])
            right.append(dot(lhs, tall([cols[side, 2 + x] for x in n])).astype(bf16))
            left.append(cols[side, 2 + e, :, me * size : (me + 1) * size])
        added = dot_t(tall(left), tall(right))
        if side == 0:
            late_ref[0] = added[:, :size].astype(bf16)
            late_ref[1] = (added[:, size:] + mid_ref[0]).astype(bf16)
        else:
            late_ref[2] = (added[:, :size] + mid_ref[1]).astype(bf16)
            late_ref[3] = added[:, size:].astype(bf16)
    for out in outs:
        out.wait()


def source_of(rows, j, aggs):
    source = lax.bitwise_xor(lax.axis_index("region"), j)
    own = (source * lax.axis_size("dev") + lax.axis_index("dev")) * rows
    return source * MOSTA, aggs[own + rows - 1] - aggs[own] + 1


def early_kernel(rows, aggs_hbm, *refs):
    out, aggs, sem = refs[-3:]
    aggs_in = pltpu.make_async_copy(aggs_hbm, aggs, sem)
    aggs_in.start()
    aggs_in.wait()
    for j in range(4):
        early = refs[j]
        at, count = source_of(rows, j, aggs)
        out[at, 2] = early[0]
        for b in range(3):
            out[at + 1, b] = early[1 + b]
            out[at + 2, b] = early[4 + b]
            out[at + 3, b] = jnp.zeros_like(early[0])
        out[at + count - 1, 0] = early[7]


def late_kernel(rows, aggs_hbm, *refs):
    coarse_in, out, aggs, sem, sems = refs[-5:]
    aggs_in = pltpu.make_async_copy(aggs_hbm, aggs, sem)
    aggs_in.start()
    aggs_in.wait()
    copies = []
    for j in range(4):
        late = refs[j]
        at, count = source_of(rows, j, aggs)
        copies.append(
            pltpu.make_async_copy(late.at[pl.ds(0, 2)], out.at[at, pl.ds(0, 2)], sems.at[2 * j])
        )
        copies.append(
            pltpu.make_async_copy(
                late.at[pl.ds(2, 2)], out.at[at + count - 1, pl.ds(1, 2)], sems.at[2 * j + 1]
            )
        )
    for c in copies:
        c.start()
    for c in copies:
        c.wait()


VM = pl.BlockSpec(memory_space=pltpu.VMEM)
ANY = pl.BlockSpec(memory_space=pl.ANY)
DMA = pltpu.SemaphoreType.DMA


def cost(products, bytes_accessed):
    return pl.CostEstimate(flops=2 * 128**3 * products, bytes_accessed=bytes_accessed, transcendentals=0)


def swap(block, by):
    return lax.ppermute(block, "region", [(i, i ^ by) for i in range(lax.axis_size("region"))])


def local(tile_values, basis_tiles, tile_offsets, aggregate_ids):
    rows, _, size, width = tile_values.shape
    total = tile_offsets.shape[0]
    hbm = lambda x: pltpu.with_memory_space_constraint(x, pltpu.HBM)
    tile_values, basis_tiles, aggregate_ids = hbm(tile_values), hbm(basis_tiles), hbm(aggregate_ids)
    offs_all = hbm(tile_offsets.T)
    block = (size, width)
    sds = jax.ShapeDtypeStruct
    window = pltpu.SMEM((2, 256), jnp.int32)
    ids = pltpu.SMEM((total,), jnp.int32)
    first, middle, last = [pltpu.CompilerParams(vmem_limit_bytes=int(x * 2**20)) for x in LIMITS]
    low, high, keep = pl.pallas_call(
        functools.partial(edges_kernel, rows, total),
        out_shape=[pltpu.VMEM((4, 3, *block), bf16)] * 2 + [pltpu.VMEM((2, 3, 3, *block), bf16)],
        in_specs=[ANY, ANY, ANY],
        out_specs=[VM, VM, VM],
        scratch_shapes=[window, pltpu.VMEM((2, 6, *block), bf16), DMA((7,))],
        compiler_params=first,
        cost_estimate=cost(24, 2 * 10**6),
        name="edges",
    )(offs_all, tile_values, basis_tiles)
    devices = lax.axis_size(AXES)
    from_low = lax.ppermute(high, AXES, [(i, i + 1) for i in range(devices - 1)])
    from_high = lax.ppermute(low, AXES, [(i + 1, i) for i in range(devices - 1)])
    prol, early, mid, pc = pl.pallas_call(
        functools.partial(interior_kernel, rows, total),
        out_shape=[
            sds((rows, 3, *block), bf16),
            pltpu.VMEM((8, *block), bf16),
            pltpu.VMEM((2, *block), f32),
            pltpu.VMEM((8, *block), bf16),
        ],
        in_specs=[ANY, ANY, ANY, ANY],
        out_specs=[ANY, VM, VM, VM],
        scratch_shapes=[
            window,
            ids,
            pltpu.VMEM((rows, 3, *block), bf16),
            pltpu.VMEM((rows, *block), bf16),
            pltpu.VMEM((rows, 3, *block), bf16),
            pltpu.VMEM((rows, 2, *block), bf16),
            pltpu.VMEM((MOSTA, 3, *block), f32),
            DMA((rows // GRP,)),
            DMA((rows // GRP,)),
            DMA((rows // GRP,)),
            DMA((2,)),
        ],
        compiler_params=middle,
        cost_estimate=cost(64 * 10, 16 * 10**6),
        name="interior",
    )(offs_all, aggregate_ids, tile_values, basis_tiles)
    early_across, early_beside = swap(early, 2), swap(early, 1)
    prol, late = pl.pallas_call(
        functools.partial(rim_kernel, rows, total),
        out_shape=[sds((rows, 3, *block), bf16), pltpu.VMEM((4, *block), bf16)],
        in_specs=[ANY] + [VM] * 7 + [ANY],
        out_specs=[ANY, VM],
        scratch_shapes=[
            window,
            pltpu.VMEM((2, 2, 3, *block), bf16),
            pltpu.VMEM((2, 10, size, 2 * width), bf16),
            DMA((3,)),
        ],
        input_output_aliases={8: 0},
        compiler_params=last,
        cost_estimate=cost(140, 3 * 10**6),
        name="rim",
    )(offs_all, from_low, from_high, low, high, keep, pc, mid, prol)
    late_across, late_beside = swap(late, 2), swap(late, 1)
    held, ignored = lax.optimization_barrier((early_across, late))
    early_both = swap(held, 1)
    coarse = pl.pallas_call(
        functools.partial(early_kernel, rows),
        out_shape=sds((4 * MOSTA, 3, *block), bf16),
        in_specs=[ANY] + [VM] * 4,
        out_specs=VM,
        scratch_shapes=[ids, DMA],
        compiler_params=last,
        cost_estimate=cost(0, 3 * 10**6),
        name="early",
    )(aggregate_ids, early, early_beside, early_across, early_both)
    held, coarse = lax.optimization_barrier((late_across, coarse))
    late_both = swap(held, 1)
    coarse = pl.pallas_call(
        functools.partial(late_kernel, rows),
        out_shape=sds((4 * MOSTA, 3, *block), bf16),
        in_specs=[ANY] + [VM] * 4 + [ANY],
        out_specs=ANY,
        scratch_shapes=[ids, DMA, DMA((8,))],
        input_output_aliases={5: 0},
        compiler_params=last,
        cost_estimate=cost(0, 10**6),
        name="late",
    )(aggregate_ids, late, late_beside, held, late_both, coarse)
    return prol, coarse


def solution(mesh):
    placed = (P(AXES, None, None, None), P(AXES, None, None), P(), P())
    return jax.shard_map(
        local,
        mesh=mesh,
        in_specs=placed,
        out_specs=(P(AXES, None, None, None), P("dev", None, None, None)),
        check_vma=False,
    )
```

time: 59.9 us -> 39.9 us (0.67)
  local copies, waits for them, and re-layouts: 8.55 us -> 0 us
  Pallas kernels: 24.2 us -> 17.2 us
  waiting for transfers between devices: 11.5 us -> 6.87 us
    unnamed x22 -> x0, local copies, waits for them, and re-layouts: 8.55 us -> none
    pallas_call x3 -> x4, Pallas kernels: 20.6 us -> 14.7 us  [the longest x1 9.11 us: local(): pl.pallas_call(functools.partial(interior_kernel, rows, total), out_shape...]
    ppermute x6, waiting for transfers between devices: 11.5 us -> 6.42 us  [swap(): lax.ppermute(block, 'region', [(i, i ^ by) for i in range(lax.axis_size('...]
    pallas_call x1, Pallas kernels: 3.57 us -> 2.47 us  [local(): pl.pallas_call(functools.partial(rim_kernel, rows, total), out_shape=[sds...]
  transfers between devices with their start and end apart: 8 -> 8, of which waited for: 3 -> 4; matrix products, arithmetic and copies ran while one was open for 0% -> 0% of each run, Pallas kernels for 33% -> 35%
where the time goes in v2:
time: 39.9 us; the launch traced here: 39.5 us
  Pallas kernels  17.2 us (43%)
  starting transfers between devices  14.8 us (37%)
  waiting for transfers between devices  6.87 us (17%)
  between operations  0.68 us (2%)
    pallas_call x1, Pallas kernels, local(): pl.pallas_call(functools.partial(interior_kernel, rows, total), out_shape...  9.11 us
    ppermute x6, starting transfers between devices, swap(): lax.ppermute(block, 'region', [(i, i ^ by) for i in range(lax.axis_size('...  8.59 us
    ppermute x6, waiting for transfers between devices, swap(): lax.ppermute(block, 'region', [(i, i ^ by) for i in range(lax.axis_size('...  6.42 us
    ppermute x1, starting transfers between devices, local(): lax.ppermute(high, AXES, [(i, i + 1) for i in range(devices - 1)])  4.9 us
    pallas_call x1, Pallas kernels, local(): pl.pallas_call(functools.partial(rim_kernel, rows, total), out_shape=[sds...  2.47 us
    pallas_call x1, Pallas kernels, local(): pl.pallas_call(functools.partial(early_kernel, rows), out_shape=sds((4 *...  2.07 us
    pallas_call x1, Pallas kernels, local(): pl.pallas_call(functools.partial(edges_kernel, rows, total), out_shape=[p...  1.89 us
    pallas_call x1, Pallas kernels, local(): pl.pallas_call(functools.partial(late_kernel, rows), out_shape=sds((4 * M...  1.65 us
  transfers between devices with their start and end apart: 8, of which 4 were waited for; matrix products, arithmetic and copies ran while one was open for 0% of the time, Pallas kernels for 35%

profile of v2, /device:TPU:0, one launch (start us, length us, event | category | flops | bytes accessed | tf_op | source)
XLA Modules:
  0.0 39.5 jit_solution(2868601452609501680)
XLA Ops:
  0.6 1.9 %edges.1 = (bf16[4,3,128,128]{3,2,1,0:T(8,128)(2,1)S(1)}, bf16[4,3,128,128]{3,2,1,0:T(8,128)(2,1)S(1)}, bf16[2,3,3,128,128]{4,3,2,1,0:T(8,128)(2,1)S(1)}) custom-call(s32[2,2048]{1,0:T(2,128)} %bitcast.1, bf16[64,3,128,128]{3,2,1,0:T(8,128)(2,1)} %tiles_hbm.3, bf16[64,128,128]{2,1,0:T(8,128)(2,1)} %basis_hbm.3), custom_call_target="tpu_custom_call" | custom-call | flops 100663296 | bytes 2000000 | tf_op jit(solution)/shard_map/edges/pallas_call | solution.py:387
  2.5 4.9 %collective-permute-start = (bf16[4,3,128,128]{3,2,1,0:T(8,128)(2,1)S(1)}, bf16[4,3,128,128]{3,2,1,0:T(8,128)(2,1)S(1)}, u32[]{:S(2)}, u32[]{:S(2)}) collective-permute-start(bf16[4,3,128,128]{3,2,1,0:T(8,128)(2,1)S(1)} %get-tuple-element.14.high_own), channel_id=1, source_target_pairs={{0,1},{1,2},{2,3},{3,4},{4,5},{5,6},{6,7},{7,8},{8,9},{9,10},{10,1... | collective-permute-start | bytes 1179656 | tf_op jit(solution)/shard_map/ppermute | solution.py:398
  7.4 1.3 %collective-permute-start.1 = (bf16[4,3,128,128]{3,2,1,0:T(8,128)(2,1)S(1)}, bf16[4,3,128,128]{3,2,1,0:T(8,128)(2,1)S(1)}, u32[]{:S(2)}, u32[]{:S(2)}) collective-permute-start(bf16[4,3,128,128]{3,2,1,0:T(8,128)(2,1)S(1)} %get-tuple-element.15.low_own), channel_id=1, source_target_pairs={{1,0},{2,1},{3,2},{4,3},{5,4},{6,5},{7,6},{8,7},{9,8},{10,9},{11,1... | collective-permute-start | bytes 1179656 | tf_op jit(solution)/shard_map/ppermute | solution.py:399
  8.7 9.1 %interior.1 = (bf16[64,3,128,128]{3,2,1,0:T(8,128)(2,1)}, bf16[8,128,128]{2,1,0:T(8,128)(2,1)S(1)}, f32[2,128,128]{2,1,0:T(8,128)S(1)}, bf16[8,128,128]{2,1,0:T(8,128)(2,1)S(1)}) custom-call(s32[2,2048]{1,0:T(2,128)} %bitcast.2, s32[2048]{0:T(1024)} %aggs_hbm.5, bf16[64,3,128,128]{3,2,1,0:T(8,128)(2,1)} %tiles_hbm.3, bf16[64,128,128]{2,1,0:T(8,128)(2,1)} %basis_hbm.3), custom_call_target="tpu_custom_call" | custom-call | flops 2684354560 | bytes 16000000 | tf_op jit(solution)/shard_map/interior/pallas_call | solution.py:400
  17.8 5.9 %collective-permute-start.5 = (bf16[8,128,128]{2,1,0:T(8,128)(2,1)S(1)}, bf16[8,128,128]{2,1,0:T(8,128)(2,1)S(1)}, u32[]{:S(2)}, u32[]{:S(2)}) collective-permute-start(bf16[8,128,128]{2,1,0:T(8,128)(2,1)S(1)} %get-tuple-element.22.refs_0_), channel_id=1, source_target_pairs={{0,16},{8,24},{16,0},{24,8},{1,17},{9,25},{17,1},{25,9},{2,18},{10... | collective-permute-start | bytes 786440 | tf_op jit(solution)/shard_map/ppermute | solution.py:373
  23.7 0.0 collective-permute-start.4
  23.7 0.5 %collective-permute-done.low_got = bf16[4,3,128,128]{3,2,1,0:T(8,128)(2,1)S(1)} collective-permute-done((bf16[4,3,128,128]{3,2,1,0:T(8,128)(2,1)S(1)}, bf16[4,3,128,128]{3,2,1,0:T(8,128)(2,1)S(1)}, u32[]{:S(2)}, u32[]{:S(2)}) %collective-permute-start) | collective-permute-done | bytes 393248 | tf_op jit(solution)/shard_map/ppermute | solution.py:398
  24.2 0.0 collective-permute-done.1.high_got
  24.2 2.5 %rim.1 = (bf16[64,3,128,128]{3,2,1,0:T(8,128)(2,1)}, bf16[4,128,128]{2,1,0:T(8,128)(2,1)S(1)}) custom-call(s32[2,2048]{1,0:T(2,128)} %bitcast.3, bf16[4,3,128,128]{3,2,1,0:T(8,128)(2,1)S(1)} %collective-permute-done.low_got, bf16[4,3,128,128]{3,2,1,0:T(8,128)(2,1)S(1)} %collective-permute-done.1.high_got, ...), custom_call_target="tpu_custom_call", output_to_operand_aliasing={{0}: (8, {})} | custom-call | flops 587202560 | bytes 3000000 | tf_op jit(solution)/shard_map/rim/pallas_call | solution.py:428
  26.7 3.2 %collective-permute-done.5.refs_2_ = bf16[8,128,128]{2,1,0:T(8,128)(2,1)S(1)} collective-permute-done((bf16[8,128,128]{2,1,0:T(8,128)(2,1)S(1)}, bf16[8,128,128]{2,1,0:T(8,128)(2,1)S(1)}, u32[]{:S(2)}, u32[]{:S(2)}) %collective-permute-start.5) | collective-permute-done | bytes 262176 | tf_op jit(solution)/shard_map/ppermute | solution.py:373
  29.9 0.0 collective-permute-start.6
  29.9 2.5 %collective-permute-start.3 = (bf16[4,128,128]{2,1,0:T(8,128)(2,1)S(1)}, bf16[4,128,128]{2,1,0:T(8,128)(2,1)S(1)}, u32[]{:S(2)}, u32[]{:S(2)}) collective-permute-start(bf16[4,128,128]{2,1,0:T(8,128)(2,1)S(1)} %get-tuple-element.21.refs_0_), channel_id=1, source_target_pairs={{0,16},{8,24},{16,0},{24,8},{1,17},{9,25},{17,1},{25,9},{2,18},{10... | collective-permute-start | bytes 393224 | tf_op jit(solution)/shard_map/ppermute | solution.py:373
  32.4 0.2 collective-permute-start.2
  32.6 0.0 collective-permute-done.4.refs_1_
  32.6 0.0 collective-permute-done.6.refs_3_
  32.6 2.1 %early.1.refs_4_ = bf16[16,3,128,128]{3,2,1,0:T(8,128)(2,1)} custom-call(s32[2048]{0:T(1024)} %aggs_hbm.5, bf16[8,128,128]{2,1,0:T(8,128)(2,1)S(1)} %get-tuple-element.22.refs_0_, bf16[8,128,128]{2,1,0:T(8,128)(2,1)S(1)} %collective-permute-done.4.refs_1_, bf16[8,128,128]{2,1,0:T(8,128)(2,1)S(1)} %collective-permute-done.5.refs_2_, ...), custom_call_target="tpu_custom_call" | custom-call | bytes 3000000 | tf_op jit(solution)/shard_map/early/pallas_call | solution.py:447
  34.7 1.8 %collective-permute-done.3.refs_2_ = bf16[4,128,128]{2,1,0:T(8,128)(2,1)S(1)} collective-permute-done((bf16[4,128,128]{2,1,0:T(8,128)(2,1)S(1)}, bf16[4,128,128]{2,1,0:T(8,128)(2,1)S(1)}, u32[]{:S(2)}, u32[]{:S(2)}) %collective-permute-start.3) | collective-permute-done | bytes 131104 | tf_op jit(solution)/shard_map/ppermute | solution.py:373
  36.5 0.0 collective-permute-start.7
  36.5 0.0 collective-permute-done.2.refs_1_
  36.5 1.3 %collective-permute-done.7.refs_3_ = bf16[4,128,128]{2,1,0:T(8,128)(2,1)S(1)} collective-permute-done((bf16[4,128,128]{2,1,0:T(8,128)(2,1)S(1)}, bf16[4,128,128]{2,1,0:T(8,128)(2,1)S(1)}, u32[]{:S(2)}, u32[]{:S(2)}) %collective-permute-start.7) | collective-permute-done | bytes 131104 | tf_op jit(solution)/shard_map/ppermute | solution.py:373
  37.9 1.7 %late.1 = bf16[16,3,128,128]{3,2,1,0:T(8,128)(2,1)} custom-call(s32[2048]{0:T(1024)} %aggs_hbm.5, bf16[4,128,128]{2,1,0:T(8,128)(2,1)S(1)} %get-tuple-element.21.refs_0_, bf16[4,128,128]{2,1,0:T(8,128)(2,1)S(1)} %collective-permute-done.2.refs_1_, bf16[4,128,128]{2,1,0:T(8,128)(2,1)S(1)} %collective-permute-done.3.refs_2_, ...), custom_call_target="tpu_custom_call", output_to_operand_aliasing={{}: (5, {})} | custom-call | bytes 1000000 | tf_op jit(solution)/shard_map/late/pallas_call | solution.py:459
Async XLA Ops:
  2.5 21.7 %collective-permute-start = (bf16[4,3,128,128]{3,2,1,0:T(8,128)(2,1)S(1)}, bf16[4,3,128,128]{3,2,1,0:T(8,128)(2,1)S(1)}, u32[]{:S(2)}, u32[]{:S(2)}) collective-permute-start(bf16[4,3,128,128]{3,2,1,0:T(8,128)(2,1)S(1)} %get-tuple-element.14.high_own), channel_id=1, source_target_pairs={{0,1},{1,2},{2,3},{3,4},{4,5},{5,6},{6,7},{7,8},{8,9},{9,10},{10,1... | collective-permute-start | bytes 1179656 | tf_op jit(solution)/shard_map/ppermute | solution.py:398
  7.4 16.8 %collective-permute-start.1 = (bf16[4,3,128,128]{3,2,1,0:T(8,128)(2,1)S(1)}, bf16[4,3,128,128]{3,2,1,0:T(8,128)(2,1)S(1)}, u32[]{:S(2)}, u32[]{:S(2)}) collective-permute-start(bf16[4,3,128,128]{3,2,1,0:T(8,128)(2,1)S(1)} %get-tuple-element.15.low_own), channel_id=1, source_target_pairs={{1,0},{2,1},{3,2},{4,3},{5,4},{6,5},{7,6},{8,7},{9,8},{10,9},{11,1... | collective-permute-start | bytes 1179656 | tf_op jit(solution)/shard_map/ppermute | solution.py:399
  17.8 12.0 %collective-permute-start.5 = (bf16[8,128,128]{2,1,0:T(8,128)(2,1)S(1)}, bf16[8,128,128]{2,1,0:T(8,128)(2,1)S(1)}, u32[]{:S(2)}, u32[]{:S(2)}) collective-permute-start(bf16[8,128,128]{2,1,0:T(8,128)(2,1)S(1)} %get-tuple-element.22.refs_0_), channel_id=1, source_target_pairs={{0,16},{8,24},{16,0},{24,8},{1,17},{9,25},{17,1},{25,9},{2,18},{10... | collective-permute-start | bytes 786440 | tf_op jit(solution)/shard_map/ppermute | solution.py:373
  23.7 8.9 %collective-permute-start.4 = (bf16[8,128,128]{2,1,0:T(8,128)(2,1)S(1)}, bf16[8,128,128]{2,1,0:T(8,128)(2,1)S(1)}, u32[]{:S(2)}, u32[]{:S(2)}) collective-permute-start(bf16[8,128,128]{2,1,0:T(8,128)(2,1)S(1)} %get-tuple-element.22.refs_0_), channel_id=1, source_target_pairs={{0,8},{8,0},{16,24},{24,16},{1,9},{9,1},{17,25},{25,17},{2,10},{10... | collective-permute-start | bytes 786440 | tf_op jit(solution)/shard_map/ppermute | solution.py:373
  29.9 2.7 %collective-permute-start.6 = (bf16[8,128,128]{2,1,0:T(8,128)(2,1)S(1)}, bf16[8,128,128]{2,1,0:T(8,128)(2,1)S(1)}, u32[]{:S(2)}, u32[]{:S(2)}) collective-permute-start(bf16[8,128,128]{2,1,0:T(8,128)(2,1)S(1)} %collective-permute-done.5.refs_2_), channel_id=1, source_target_pairs={{0,8},{8,0},{16,24},{24,16},{1,9},{9,1},{17,25},{25,17},{2,10},{10... | collective-permute-start | bytes 786440 | tf_op jit(solution)/shard_map/ppermute | solution.py:373
  29.9 6.6 %collective-permute-start.3 = (bf16[4,128,128]{2,1,0:T(8,128)(2,1)S(1)}, bf16[4,128,128]{2,1,0:T(8,128)(2,1)S(1)}, u32[]{:S(2)}, u32[]{:S(2)}) collective-permute-start(bf16[4,128,128]{2,1,0:T(8,128)(2,1)S(1)} %get-tuple-element.21.refs_0_), channel_id=1, source_target_pairs={{0,16},{8,24},{16,0},{24,8},{1,17},{9,25},{17,1},{25,9},{2,18},{10... | collective-permute-start | bytes 393224 | tf_op jit(solution)/shard_map/ppermute | solution.py:373
  32.4 4.1 %collective-permute-start.2 = (bf16[4,128,128]{2,1,0:T(8,128)(2,1)S(1)}, bf16[4,128,128]{2,1,0:T(8,128)(2,1)S(1)}, u32[]{:S(2)}, u32[]{:S(2)}) collective-permute-start(bf16[4,128,128]{2,1,0:T(8,128)(2,1)S(1)} %get-tuple-element.21.refs_0_), channel_id=1, source_target_pairs={{0,8},{8,0},{16,24},{24,16},{1,9},{9,1},{17,25},{25,17},{2,10},{10... | collective-permute-start | bytes 393224 | tf_op jit(solution)/shard_map/ppermute | solution.py:373
  36.5 1.3 %collective-permute-start.7 = (bf16[4,128,128]{2,1,0:T(8,128)(2,1)S(1)}, bf16[4,128,128]{2,1,0:T(8,128)(2,1)S(1)}, u32[]{:S(2)}, u32[]{:S(2)}) collective-permute-start(bf16[4,128,128]{2,1,0:T(8,128)(2,1)S(1)} %collective-permute-done.3.refs_2_), channel_id=1, source_target_pairs={{0,8},{8,0},{16,24},{24,16},{1,9},{9,1},{17,25},{25,17},{2,10},{10... | collective-permute-start | bytes 393224 | tf_op jit(solution)/shard_map/ppermute | solution.py:373

commit v3 on v2

--- a/solution.py
+++ b/solution.py
@@ -49,6 +49,10 @@
     return [x.astype(bf16) for x in (head, *rest)]
 
 
+def weight(condition):
+    return jnp.where(condition, 1.0, 0.0).astype(f32)
+
+
 def place_of(rows):
     return (lax.axis_index("region") * lax.axis_size("dev") + lax.axis_index("dev")) * rows
 
@@ -59,20 +63,17 @@
 
 
 def edges_kernel(
-    rows, total, offs_hbm, tiles_hbm, basis_hbm, low_ref, high_ref, keep_ref, offs, basis, sems
+    rows, total, offs_hbm, tiles_hbm, basis_hbm, low_ref, high_ref, tiles, basis, offs, cols, sems
 ):
     own = place_of(rows)
-    start, offs_in = offsets_copy(own, total, offs_hbm, offs, sems.at[6])
+    start, offs_in = offsets_copy(own, total, offs_hbm, offs, sems.at[4])
     copies = []
-    for side, out in enumerate((low_ref, high_ref)):
-        outer, inner, far = (0, 2, 0) if side == 0 else (rows - 2, rows - 4, rows - 6)
+    for side in range(2):
+        first, far = (0, 0) if side == 0 else (rows - 4, rows - 6)
         copies.append(
             [
-                pltpu.make_async_copy(basis_hbm.at[pl.ds(far, 6)], basis.at[side], sems.at[3 * side]),
-                pltpu.make_async_copy(tiles_hbm.at[pl.ds(outer, 2)], out.at[pl.ds(0, 2)], sems.at[3 * side + 1]),
-                pltpu.make_async_copy(
-                    tiles_hbm.at[pl.ds(inner, 2)], keep_ref.at[side, pl.ds(0, 2)], sems.at[3 * side + 2]
-                ),
+                pltpu.make_async_copy(basis_hbm.at[pl.ds(far, 6)], basis.at[side], sems.at[2 * side]),
+                pltpu.make_async_copy(tiles_hbm.at[pl.ds(first, 4)], tiles.at[side], sems.at[2 * side + 1]),
             ]
         )
     offs_in.start()
@@ -80,26 +81,30 @@
         for c in group:
             c.start()
     offs_in.wait()
+    for group in copies:
+        for c in group:
+            c.wait()
     for side, out in enumerate((low_ref, high_ref)):
-        for c in copies[side]:
-            c.wait()
+        shift = 0 if side == 0 else 2
+        outer = (0, 1) if side == 0 else (2, 3)
+        near = [
+            [i + shift + offs[k, own - start + (i if side == 0 else rows - 4 + i)] for k in range(2)]
+            for i in range(4)
+        ]
         for i in range(4):
-            m = i if side == 0 else rows - 4 + i
-            at = i if side == 0 else i + 2
-            outer = (i < 2) == (side == 0)
-            held = out.at[i % 2] if outer else keep_ref.at[side, i % 2]
-            near, weights = [basis[side, at]], []
+            blocks = [basis[side, i + shift]] + [basis[side, jnp.clip(n, 0, 5)] for n in near[i]]
+            p0, p1, p2 = smooth_row([tiles[side, i, k] for k in range(3)], blocks)
+            w1, w2 = [weight((n >= 0) & (n <= 5)) for n in near[i]]
+            cols[side, i] = (p0.astype(f32) + w1 * p1.astype(f32) + w2 * p2.astype(f32)).astype(bf16)
+        for j, i in enumerate(outer):
+            out[3 * j] = tiles[side, i, 0]
             for k in range(2):
-                n = at + offs[k, own - start + m]
-                weights.append(jnp.where((n >= 0) & (n <= 5), 1.0, 0.0).astype(f32))
-                near.append(basis[side, jnp.clip(n, 0, 5)])
-            p0, p1, p2 = smooth_row([held[k] for k in range(3)], near)
-            sum_ = p0.astype(f32) + weights[0] * p1.astype(f32) + weights[1] * p2.astype(f32)
-            out[2 + i // 3, i % 3] = sum_.astype(bf16)
-        for i in range(2):
-            out[3, 1 + i] = basis[side, i if side == 0 else 4 + i]
-            keep_ref[side, 2, i] = basis[side, 2 + i]
-        keep_ref[side, 2, 2] = jnp.zeros(basis.shape[2:], bf16)
+                n = near[i][k]
+                beyond = (n >= 2) if side == 0 else (n <= 3)
+                product = dot(tiles[side, i, 1 + k], cols[side, jnp.clip(n - shift, 0, 3)]).astype(bf16)
+                out[3 * j + 1 + k] = jnp.where(beyond, product, tiles[side, i, 1 + k])
+            out[6 + j] = cols[side, i]
+            out[8 + j] = basis[side, i + shift]
 
 
 def interior_kernel(
@@ -231,79 +236,93 @@
 
 
 def rim_kernel(
-    rows, total, offs_hbm, low_got, high_got, low_own, high_own, keep_ref, pc_ref, mid_ref, prol_in,
-    prol_hbm, late_ref, offs, prol, cols, sems,
+    rows, total, offs_hbm, low_got, high_got, tiles, basis, pc_ref, mid_ref, prol_in,
+    prol_hbm, late_ref, offs, prol, low_cols, high_cols, sems,
 ):
     own = place_of(rows)
-    size = cols.shape[-2]
+    size = low_cols.shape[-2]
     start, offs_in = offsets_copy(own, total, offs_hbm, offs, sems.at[2])
     offs_in.start()
+    sides = ((0, low_got, low_cols, -2, (0, 1), (2, 3)), (1, high_got, high_cols, rows - 4, (4, 5), (2, 3)))
+    scales = []
+    for side, got, cols, first, theirs, mine in sides:
+        own_at = (0, 1) if side == 0 else (2, 3)
+        scales.append({e: row_scale(got[3 * i]) for i, e in enumerate(theirs)})
+        scales[side].update({e: row_scale(tiles[side, own_at[i], 0]) for i, e in enumerate(mine)})
     offs_in.wait()
-    outs = []
-    for side, (got, sent) in enumerate(((low_got, low_own), (high_got, high_own))):
-        first = -2 if side == 0 else rows - 4
-        theirs, mine, plain = ((0, 1), (2, 3), (4, 5)) if side == 0 else ((4, 5), (2, 3), (0, 1))
+
+    outs, near = [], []
+    for side, got, cols, first, theirs, mine in sides:
         nb, me = (0, 1) if side == 0 else (1, 0)
-        zero = jnp.zeros((size, size), bf16)
-        basis = [None] * 6
-        held = [None] * 6
-        for i in range(2):
-            held[theirs[i]], held[mine[i]], held[plain[i]] = got.at[i], sent.at[i], keep_ref.at[side, i]
-
-        def basis_of(x):
-            order = (got, sent, None) if side == 0 else (None, sent, got)
-            where = jnp.clip(x, 0, 5)
-            out = None
-            for group, source in enumerate(order):
-                block = (
-                    keep_ref[side, 2, lax.rem(where, 2)] if source is None else source[3, 1 + lax.rem(where, 2)]
-                )
-                out = block if out is None else jnp.where(where // 2 == group, block, out)
-            return out
-
-        def near_of(e):
+        shift = -2 if side == 0 else 0
+
+        def near_of(e, first=first):
             m = own + first + e
             inside = (m >= 0) & (m < total)
             at = jnp.clip(m, 0, total - 1) - start
-            return [e] + [e + jnp.where(inside, offs[k, at], 0) for k in range(2)]
-
-        def is_mine(e):
-            return (e >= 2) if side == 0 else (e <= 3)
-
-        def put(e, which, block):
-            cols[side, 2 + e, :, which * size : (which + 1) * size] = block
-
+            return [e + jnp.where(inside, offs[k, at], 0) for k in range(2)]
+
+        def put(e, which, block, cols=cols):
+            cols[2 + e, :, which * size : (which + 1) * size] = block
+
+        near.append([near_of(e) for e in range(6)])
+        for i in range(2):
+            put(theirs[i], nb, got[6 + i])
         for i in range(4):
-            e = i - 2 if side == 0 else i + 4
-            put(e, nb, got[2 + i // 3, i % 3])
-            if e not in theirs:
-                put(e, me, zero)
             e = i + 4 if side == 0 else i - 2
             put(e, me, pc_ref[4 * side + i])
-            put(e, nb, zero)
+            put(e, nb, jnp.zeros((size, size), bf16))
+
+        def basis_of(x, side=side, got=got, theirs=theirs):
+            outside = (x < 2) if side == 0 else (x > 3)
+            at = jnp.clip(x - 2 if side == 0 else x + 2, 0, 5)
+            return jnp.where(outside, got[8 + lax.rem(jnp.clip(x, 0, 5), 2)], basis[side, at])
+
         for e in (*mine, *theirs):
-            n = near_of(e)
-            row = smooth_row([held[e][k] for k in range(3)], [basis_of(x) for x in n])
-            p0, p1, p2 = [x.astype(f32) for x in row]
-            w1, w2 = [jnp.where(is_mine(x), 1.0, 0.0).astype(f32) for x in n[1:]]
+            w1, w2 = [weight((x >= 2) if side == 0 else (x <= 3)) for x in near[side][e]]
+            held = [got[3 * theirs.index(e) + k] if e in theirs else tiles[side, e + shift, k] for k in range(3)]
+            scale = scales[side][e]
+            p1, p2 = [
+                (scale * dot(held[1 + k], basis_of(near[side][e][k]))).astype(bf16) for k in range(2)
+            ]
+            q1, q2 = p1.astype(f32), p2.astype(f32)
             if e in mine:
-                for k in range(3):
-                    prol[side, e - 2, k] = row[k]
-                put(e, me, (p0 + w1 * p1 + w2 * p2).astype(bf16))
-                put(e, nb, ((1.0 - w1) * p1 + (1.0 - w2) * p2).astype(bf16))
+                here = basis[side, e - 2 if side == 0 else e + 2]
+                p0 = (here.astype(f32) + scale * dot(held[0], here)).astype(bf16)
+                for k, block in enumerate((p0, p1, p2)):
+                    prol[side, e - 2, k] = block
+                put(e, me, (p0.astype(f32) + w1 * q1 + w2 * q2).astype(bf16))
+                put(e, nb, ((1.0 - w1) * q1 + (1.0 - w2) * q2).astype(bf16))
             else:
-                put(e, me, (w1 * p1 + w2 * p2).astype(bf16))
+                put(e, me, (w1 * q1 + w2 * q2).astype(bf16))
+    for side in range(2):
         out = pltpu.make_async_copy(
             prol.at[side], prol_hbm.at[pl.ds(0 if side == 0 else rows - 2, 2)], sems.at[side]
         )
         out.start()
         outs.append(out)
+    for side, got, cols, first, theirs, mine in sides:
+        nb, me = (0, 1) if side == 0 else (1, 0)
+        shift = -2 if side == 0 else 0
         left, right = [], []
         for e in range(6):
-            n = near_of(e)
-            lhs = wide([held[e][k] for k in range(3)])
-            right.append(dot(lhs, tall([cols[side, 2 + x] for x in n])).astype(bf16))
-            left.append(cols[side, 2 + e, :, me * size : (me + 1) * size])
+            x1, x2 = near[side][e]
+            if e in theirs:
+                held = [got[3 * theirs.index(e) + k] for k in range(3)]
+                kept = [(x >= 0) & (x <= 5) for x in (x1, x2)]
+                zero = jnp.zeros_like(held[0])
+                lhs = wide([held[0]] + [jnp.where(kept[k], held[1 + k], zero) for k in range(2)])
+                more = sum(jnp.where(kept[k], zero, held[1 + k]).astype(f32) for k in range(2))
+                x1, x2 = jnp.clip(x1, 0, 5), jnp.clip(x2, 0, 5)
+            else:
+                lhs, more = wide([tiles[side, e + shift, k] for k in range(3)]), None
+            product = dot(lhs, tall([cols[2 + x] for x in (e, x1, x2)]))
+            if more is not None:
+                halves = [product[:, :size], product[:, size:]]
+                halves[nb] += more
+                product = wide(halves)
+            right.append(product.astype(bf16))
+            left.append(cols[2 + e, :, me * size : (me + 1) * size])
         added = dot_t(tall(left), tall(right))
         if side == 0:
             late_ref[0] = added[:, :size].astype(bf16)
@@ -315,47 +334,58 @@
         out.wait()
 
 
-def source_of(rows, j, aggs):
-    source = lax.bitwise_xor(lax.axis_index("region"), j)
-    own = (source * lax.axis_size("dev") + lax.axis_index("dev")) * rows
-    return source * MOSTA, aggs[own + rows - 1] - aggs[own] + 1
-
-
-def early_kernel(rows, aggs_hbm, *refs):
-    out, aggs, sem = refs[-3:]
+def place_early(block, early, count):
+    block[0, 2] = early[0]
+    for b in range(3):
+        block[1, b] = early[1 + b]
+        block[2, b] = early[4 + b]
+        block[3, b] = jnp.zeros_like(early[0])
+    block[count - 1, 0] = early[7]
+
+
+def near_kernel(rows, aggs_hbm, early_0, early_1, out_hbm, counts, aggs, blocks, sem, sems):
     aggs_in = pltpu.make_async_copy(aggs_hbm, aggs, sem)
     aggs_in.start()
     aggs_in.wait()
-    for j in range(4):
-        early = refs[j]
-        at, count = source_of(rows, j, aggs)
-        out[at, 2] = early[0]
-        for b in range(3):
-            out[at + 1, b] = early[1 + b]
-            out[at + 2, b] = early[4 + b]
-            out[at + 3, b] = jnp.zeros_like(early[0])
-        out[at + count - 1, 0] = early[7]
-
-
-def late_kernel(rows, aggs_hbm, *refs):
-    coarse_in, out, aggs, sem, sems = refs[-5:]
-    aggs_in = pltpu.make_async_copy(aggs_hbm, aggs, sem)
-    aggs_in.start()
-    aggs_in.wait()
+    region = lax.axis_index("region")
     copies = []
     for j in range(4):
-        late = refs[j]
-        at, count = source_of(rows, j, aggs)
-        copies.append(
-            pltpu.make_async_copy(late.at[pl.ds(0, 2)], out.at[at, pl.ds(0, 2)], sems.at[2 * j])
-        )
+        source = lax.bitwise_xor(region, j)
+        own = (source * lax.axis_size("dev") + lax.axis_index("dev")) * rows
+        count = aggs[own + rows - 1] - aggs[own] + 1
+        counts[j : j + 1, :] = jnp.full((1, counts.shape[1]), count, jnp.int32)
+        if j < 2:
+            place_early(blocks.at[j], (early_0, early_1)[j], count)
+            copies.append(
+                pltpu.make_async_copy(blocks.at[j], out_hbm.at[pl.ds(source * MOSTA, MOSTA)], sems.at[j])
+            )
+            copies[j].start()
+    for c in copies:
+        c.wait()
+
+
+def far_kernel(counts, early_2, early_3, late_0, late_1, late_2, late_3, coarse_in, out, blocks, sems):
+    region = lax.axis_index("region")
+    copies = []
+    for j, late in enumerate((late_0, late_1)):
+        at = lax.bitwise_xor(region, j) * MOSTA
+        copies.append(pltpu.make_async_copy(late.at[pl.ds(0, 2)], out.at[at, pl.ds(0, 2)], sems.at[2 * j]))
         copies.append(
             pltpu.make_async_copy(
-                late.at[pl.ds(2, 2)], out.at[at + count - 1, pl.ds(1, 2)], sems.at[2 * j + 1]
+                late.at[pl.ds(2, 2)], out.at[at + counts[j, 0] - 1, pl.ds(1, 2)], sems.at[2 * j + 1]
             )
         )
     for c in copies:
         c.start()
+    for j, (early, late) in enumerate(((early_2, late_2), (early_3, late_3))):
+        block, count = blocks.at[j], counts[2 + j, 0]
+        place_early(block, early, count)
+        for b in range(2):
+            block[0, b] = late[b]
+            block[count - 1, 1 + b] = late[2 + b]
+        at = lax.bitwise_xor(region, 2 + j) * MOSTA
+        copies.append(pltpu.make_async_copy(block, out.at[pl.ds(at, MOSTA)], sems.at[4 + j]))
+        copies[-1].start()
     for c in copies:
         c.wait()
 
@@ -384,12 +414,12 @@
     window = pltpu.SMEM((2, 256), jnp.int32)
     ids = pltpu.SMEM((total,), jnp.int32)
     first, middle, last = [pltpu.CompilerParams(vmem_limit_bytes=int(x * 2**20)) for x in LIMITS]
-    low, high, keep = pl.pallas_call(
+    low, high, edge_tiles, edge_basis = pl.pallas_call(
         functools.partial(edges_kernel, rows, total),
-        out_shape=[pltpu.VMEM((4, 3, *block), bf16)] * 2 + [pltpu.VMEM((2, 3, 3, *block), bf16)],
+        out_shape=[pltpu.VMEM(x + block, bf16) for x in ((10,), (10,), (2, 4, 3), (2, 6))],
         in_specs=[ANY, ANY, ANY],
-        out_specs=[VM, VM, VM],
-        scratch_shapes=[window, pltpu.VMEM((2, 6, *block), bf16), DMA((7,))],
+        out_specs=[VM] * 4,
+        scratch_shapes=[window, pltpu.VMEM((2, 4, *block), bf16), DMA((5,))],
         compiler_params=first,
         cost_estimate=cost(24, 2 * 10**6),
         name="edges",
@@ -428,45 +458,44 @@
     prol, late = pl.pallas_call(
         functools.partial(rim_kernel, rows, total),
         out_shape=[sds((rows, 3, *block), bf16), pltpu.VMEM((4, *block), bf16)],
-        in_specs=[ANY] + [VM] * 7 + [ANY],
+        in_specs=[ANY] + [VM] * 6 + [ANY],
         out_specs=[ANY, VM],
         scratch_shapes=[
             window,
             pltpu.VMEM((2, 2, 3, *block), bf16),
-            pltpu.VMEM((2, 10, size, 2 * width), bf16),
+            pltpu.VMEM((10, size, 2 * width), bf16),
+            pltpu.VMEM((10, size, 2 * width), bf16),
             DMA((3,)),
         ],
-        input_output_aliases={8: 0},
+        input_output_aliases={7: 0},
         compiler_params=last,
         cost_estimate=cost(140, 3 * 10**6),
         name="rim",
-    )(offs_all, from_low, from_high, low, high, keep, pc, mid, prol)
+    )(offs_all, from_low, from_high, edge_tiles, edge_basis, pc, mid, prol)
     late_across, late_beside = swap(late, 2), swap(late, 1)
-    held, ignored = lax.optimization_barrier((early_across, late))
-    early_both = swap(held, 1)
+    coarse, counts = pl.pallas_call(
+        functools.partial(near_kernel, rows),
+        out_shape=[sds((4 * MOSTA, 3, *block), bf16), pltpu.VMEM((8, 128), jnp.int32)],
+        in_specs=[ANY, VM, VM],
+        out_specs=[ANY, VM],
+        scratch_shapes=[ids, pltpu.VMEM((2, MOSTA, 3, *block), bf16), DMA, DMA((2,))],
+        compiler_params=last,
+        cost_estimate=cost(0, 2 * 10**6),
+        name="near",
+    )(aggregate_ids, early, early_beside)
+    early_across, late_across, coarse = lax.optimization_barrier((early_across, late_across, coarse))
+    early_both, late_both = swap(early_across, 1), swap(late_across, 1)
     coarse = pl.pallas_call(
-        functools.partial(early_kernel, rows),
+        far_kernel,
         out_shape=sds((4 * MOSTA, 3, *block), bf16),
-        in_specs=[ANY] + [VM] * 4,
-        out_specs=VM,
-        scratch_shapes=[ids, DMA],
+        in_specs=[VM] * 7 + [ANY],
+        out_specs=ANY,
+        scratch_shapes=[pltpu.VMEM((2, MOSTA, 3, *block), bf16), DMA((6,))],
+        input_output_aliases={7: 0},
         compiler_params=last,
-        cost_estimate=cost(0, 3 * 10**6),
-        name="early",
-    )(aggregate_ids, early, early_beside, early_across, early_both)
-    held, coarse = lax.optimization_barrier((late_across, coarse))
-    late_both = swap(held, 1)
-    coarse = pl.pallas_call(
-        functools.partial(late_kernel, rows),
-        out_shape=sds((4 * MOSTA, 3, *block), bf16),
-        in_specs=[ANY] + [VM] * 4 + [ANY],
-        out_specs=ANY,
-        scratch_shapes=[ids, DMA, DMA((8,))],
-        input_output_aliases={5: 0},
-        compiler_params=last,
-        cost_estimate=cost(0, 10**6),
-        name="late",
-    )(aggregate_ids, late, late_beside, held, late_both, coarse)
+        cost_estimate=cost(0, 2 * 10**6),
+        name="far",
+    )(counts, early_across, early_both, late, late_beside, late_across, late_both, coarse)
     return prol, coarse
 
 

time: 39.9 us -> 37.2 us (0.932)
  waiting for transfers between devices: 6.87 us -> 3.89 us
  starting transfers between devices: 14.8 us -> 15.9 us
  Pallas kernels: 17.2 us -> 16.4 us
    ppermute x6, waiting for transfers between devices: 6.42 us -> 3.89 us  [swap(): lax.ppermute(block, 'region', [(i, i ^ by) for i in range(lax.axis_size('...]
    ppermute x6, starting transfers between devices: 8.59 us -> 9.74 us  [swap(): lax.ppermute(block, 'region', [(i, i ^ by) for i in range(lax.axis_size('...]
    pallas_call x2, Pallas kernels: 3.72 us -> 2.76 us  [the longest x1 1.72 us: local(): pl.pallas_call(functools.partial(near_kernel, rows), out_shape=[sds((4 *...]
    ppermute x1, waiting for transfers between devices: 0.45 us -> 0.01 us  [local(): lax.ppermute(high, AXES, [(i, i + 1) for i in range(devices - 1)])]
  transfers between devices with their start and end apart: 8 -> 8, of which waited for: 4 -> 3; matrix products, arithmetic and copies ran while one was open for 0% -> 0% of each run, Pallas kernels for 35% -> 35%
where the time goes in v3:
time: 37.2 us; the launch traced here: 36.9 us
  Pallas kernels  16.4 us (44%)
  starting transfers between devices  15.9 us (43%)
  waiting for transfers between devices  3.89 us (10%)
  between operations  0.69 us (2%)
    ppermute x6, starting transfers between devices, swap(): lax.ppermute(block, 'region', [(i, i ^ by) for i in range(lax.axis_size('...  9.74 us
    pallas_call x1, Pallas kernels, local(): pl.pallas_call(functools.partial(interior_kernel, rows, total), out_shape...  9.08 us
    ppermute x1, starting transfers between devices, local(): lax.ppermute(high, AXES, [(i, i + 1) for i in range(devices - 1)])  4.89 us
    ppermute x6, waiting for transfers between devices, swap(): lax.ppermute(block, 'region', [(i, i ^ by) for i in range(lax.axis_size('...  3.89 us
    pallas_call x1, Pallas kernels, local(): pl.pallas_call(functools.partial(rim_kernel, rows, total), out_shape=[sds...  2.29 us
    pallas_call x1, Pallas kernels, local(): pl.pallas_call(functools.partial(edges_kernel, rows, total), out_shape=[p...  2.26 us
    pallas_call x1, Pallas kernels, local(): pl.pallas_call(functools.partial(near_kernel, rows), out_shape=[sds((4 *...  1.72 us
    ppermute x1, starting transfers between devices, local(): lax.ppermute(low, AXES, [(i + 1, i) for i in range(devices - 1)])  1.29 us
  transfers between devices with their start and end apart: 8, of which 3 were waited for; matrix products, arithmetic and copies ran while one was open for 0% of the time, Pallas kernels for 35%

profile of v3, /device:TPU:0, one launch (start us, length us, event | category | flops | bytes accessed | tf_op | source)
XLA Modules:
  0.0 36.9 jit_solution(13113115858505706028)
XLA Ops:
  0.6 2.3 %edges.1 = (bf16[10,128,128]{2,1,0:T(8,128)(2,1)S(1)}, bf16[10,128,128]{2,1,0:T(8,128)(2,1)S(1)}, bf16[2,4,3,128,128]{4,3,2,1,0:T(8,128)(2,1)S(1)}, bf16[2,6,128,128]{3,2,1,0:T(8,128)(2,1)S(1)}) custom-call(s32[2,2048]{1,0:T(2,128)} %bitcast.1, bf16[64,3,128,128]{3,2,1,0:T(8,128)(2,1)} %tiles_hbm.3, bf16[64,128,128]{2,1,0:T(8,128)(2,1)} %basis_hbm.3), custom_call_target="tpu_custom_call" | custom-call | flops 100663296 | bytes 2000000 | tf_op jit(solution)/shard_map/edges/pallas_call | solution.py:417
  2.9 4.9 %collective-permute-start = (bf16[10,128,128]{2,1,0:T(8,128)(2,1)S(1)}, bf16[10,128,128]{2,1,0:T(8,128)(2,1)S(1)}, u32[]{:S(2)}, u32[]{:S(2)}) collective-permute-start(bf16[10,128,128]{2,1,0:T(8,128)(2,1)S(1)} %get-tuple-element.17), channel_id=1, source_target_pairs={{0,1},{1,2},{2,3},{3,4},{4,5},{5,6},{6,7},{7,8},{8,9},{9,10},{10,1... | collective-permute-start | bytes 983048 | tf_op jit(solution)/shard_map/ppermute | solution.py:428
  7.8 1.3 %collective-permute-start.1 = (bf16[10,128,128]{2,1,0:T(8,128)(2,1)S(1)}, bf16[10,128,128]{2,1,0:T(8,128)(2,1)S(1)}, u32[]{:S(2)}, u32[]{:S(2)}) collective-permute-start(bf16[10,128,128]{2,1,0:T(8,128)(2,1)S(1)} %get-tuple-element.18), channel_id=1, source_target_pairs={{1,0},{2,1},{3,2},{4,3},{5,4},{6,5},{7,6},{8,7},{9,8},{10,9},{11,1... | collective-permute-start | bytes 983048 | tf_op jit(solution)/shard_map/ppermute | solution.py:429
  9.1 9.1 %interior.1 = (bf16[64,3,128,128]{3,2,1,0:T(8,128)(2,1)}, bf16[8,128,128]{2,1,0:T(8,128)(2,1)S(1)}, f32[2,128,128]{2,1,0:T(8,128)S(1)}, bf16[8,128,128]{2,1,0:T(8,128)(2,1)S(1)}) custom-call(s32[2,2048]{1,0:T(2,128)} %bitcast.2, s32[2048]{0:T(1024)} %aggs_hbm.3, bf16[64,3,128,128]{3,2,1,0:T(8,128)(2,1)} %tiles_hbm.3, bf16[64,128,128]{2,1,0:T(8,128)(2,1)} %basis_hbm.3), custom_call_target="tpu_custom_call" | custom-call | flops 2684354560 | bytes 16000000 | tf_op jit(solution)/shard_map/interior/pallas_call | solution.py:430
  18.2 3.8 %collective-permute-start.2 = (bf16[8,128,128]{2,1,0:T(8,128)(2,1)S(1)}, bf16[8,128,128]{2,1,0:T(8,128)(2,1)S(1)}, u32[]{:S(2)}, u32[]{:S(2)}) collective-permute-start(bf16[8,128,128]{2,1,0:T(8,128)(2,1)S(1)} %get-tuple-element.25.early_0), channel_id=1, source_target_pairs={{0,8},{8,0},{16,24},{24,16},{1,9},{9,1},{17,25},{25,17},{2,10},{10... | collective-permute-start | bytes 786440 | tf_op jit(solution)/shard_map/ppermute | solution.py:403
  22.0 2.3 %collective-permute-start.3 = (bf16[8,128,128]{2,1,0:T(8,128)(2,1)S(1)}, bf16[8,128,128]{2,1,0:T(8,128)(2,1)S(1)}, u32[]{:S(2)}, u32[]{:S(2)}) collective-permute-start(bf16[8,128,128]{2,1,0:T(8,128)(2,1)S(1)} %get-tuple-element.25.early_0), channel_id=1, source_target_pairs={{0,16},{8,24},{16,0},{24,8},{1,17},{9,25},{17,1},{25,9},{2,18},{10... | collective-permute-start | bytes 786440 | tf_op jit(solution)/shard_map/ppermute | solution.py:403
  24.2 0.0 collective-permute-done.low_got
  24.2 0.0 collective-permute-done.1.high_got
  24.2 2.3 %rim.1 = (bf16[64,3,128,128]{3,2,1,0:T(8,128)(2,1)}, bf16[4,128,128]{2,1,0:T(8,128)(2,1)S(1)}) custom-call(s32[2,2048]{1,0:T(2,128)} %bitcast.3, bf16[10,128,128]{2,1,0:T(8,128)(2,1)S(1)} %collective-permute-done.low_got, bf16[10,128,128]{2,1,0:T(8,128)(2,1)S(1)} %collective-permute-done.1.high_got, ...), custom_call_target="tpu_custom_call", output_to_operand_aliasing={{0}: (7, {})} | custom-call | flops 587202560 | bytes 3000000 | tf_op jit(solution)/shard_map/rim/pallas_call | solution.py:458
  26.5 3.2 %collective-permute-start.4 = (bf16[4,128,128]{2,1,0:T(8,128)(2,1)S(1)}, bf16[4,128,128]{2,1,0:T(8,128)(2,1)S(1)}, u32[]{:S(2)}, u32[]{:S(2)}) collective-permute-start(bf16[4,128,128]{2,1,0:T(8,128)(2,1)S(1)} %get-tuple-element.27.late_0), channel_id=1, source_target_pairs={{0,16},{8,24},{16,0},{24,8},{1,17},{9,25},{17,1},{25,9},{2,18},{10... | collective-permute-start | bytes 393224 | tf_op jit(solution)/shard_map/ppermute | solution.py:403
  29.7 0.0 collective-permute-done.2.early_1
  29.7 1.7 %near.1 = (bf16[16,3,128,128]{3,2,1,0:T(8,128)(2,1)}, s32[8,128]{1,0:T(8,128)S(1)}) custom-call(s32[2048]{0:T(1024)} %aggs_hbm.3, bf16[8,128,128]{2,1,0:T(8,128)(2,1)S(1)} %get-tuple-element.25.early_0, bf16[8,128,128]{2,1,0:T(8,128)(2,1)S(1)} %collective-permute-done.2.early_1), custom_call_target="tpu_custom_call" | custom-call | bytes 2000000 | tf_op jit(solution)/shard_map/near/pallas_call | solution.py:476
  31.4 0.0 collective-permute-done.3.early_2
  31.5 2.5 %collective-permute-done.4.late_2 = bf16[4,128,128]{2,1,0:T(8,128)(2,1)S(1)} collective-permute-done((bf16[4,128,128]{2,1,0:T(8,128)(2,1)S(1)}, bf16[4,128,128]{2,1,0:T(8,128)(2,1)S(1)}, u32[]{:S(2)}, u32[]{:S(2)}) %collective-permute-start.4) | collective-permute-done | bytes 131104 | tf_op jit(solution)/shard_map/ppermute | solution.py:403
  33.9 0.0 collective-permute-start.5
  33.9 0.5 %collective-permute-start.6 = (bf16[4,128,128]{2,1,0:T(8,128)(2,1)S(1)}, bf16[4,128,128]{2,1,0:T(8,128)(2,1)S(1)}, u32[]{:S(2)}, u32[]{:S(2)}) collective-permute-start(bf16[4,128,128]{2,1,0:T(8,128)(2,1)S(1)} %get-tuple-element.27.late_0), channel_id=1, source_target_pairs={{0,8},{8,0},{16,24},{24,16},{1,9},{9,1},{17,25},{25,17},{2,10},{10... | collective-permute-start | bytes 393224 | tf_op jit(solution)/shard_map/ppermute | solution.py:403
  34.5 0.0 collective-permute-start.7
  34.5 1.2 %collective-permute-done.6.late_1 = bf16[4,128,128]{2,1,0:T(8,128)(2,1)S(1)} collective-permute-done((bf16[4,128,128]{2,1,0:T(8,128)(2,1)S(1)}, bf16[4,128,128]{2,1,0:T(8,128)(2,1)S(1)}, u32[]{:S(2)}, u32[]{:S(2)}) %collective-permute-start.6) | collective-permute-done | bytes 131104 | tf_op jit(solution)/shard_map/ppermute | solution.py:403
  35.7 0.2 collective-permute-done.7.late_3
  35.9 0.0 collective-permute-done.5.early_3
  35.9 1.0 %far.1 = bf16[16,3,128,128]{3,2,1,0:T(8,128)(2,1)} custom-call(s32[8,128]{1,0:T(8,128)S(1)} %get-tuple-element.26.counts, bf16[8,128,128]{2,1,0:T(8,128)(2,1)S(1)} %collective-permute-done.3.early_2, bf16[8,128,128]{2,1,0:T(8,128)(2,1)S(1)} %collective-permute-done.5.early_3, ...), custom_call_target="tpu_custom_call", output_to_operand_aliasing={{}: (7, {})} | custom-call | bytes 2000000 | tf_op jit(solution)/shard_map/far/pallas_call | solution.py:488
Async XLA Ops:
  2.9 21.3 %collective-permute-start = (bf16[10,128,128]{2,1,0:T(8,128)(2,1)S(1)}, bf16[10,128,128]{2,1,0:T(8,128)(2,1)S(1)}, u32[]{:S(2)}, u32[]{:S(2)}) collective-permute-start(bf16[10,128,128]{2,1,0:T(8,128)(2,1)S(1)} %get-tuple-element.17), channel_id=1, source_target_pairs={{0,1},{1,2},{2,3},{3,4},{4,5},{5,6},{6,7},{7,8},{8,9},{9,10},{10,1... | collective-permute-start | bytes 983048 | tf_op jit(solution)/shard_map/ppermute | solution.py:428
  7.8 16.4 %collective-permute-start.1 = (bf16[10,128,128]{2,1,0:T(8,128)(2,1)S(1)}, bf16[10,128,128]{2,1,0:T(8,128)(2,1)S(1)}, u32[]{:S(2)}, u32[]{:S(2)}) collective-permute-start(bf16[10,128,128]{2,1,0:T(8,128)(2,1)S(1)} %get-tuple-element.18), channel_id=1, source_target_pairs={{1,0},{2,1},{3,2},{4,3},{5,4},{6,5},{7,6},{8,7},{9,8},{10,9},{11,1... | collective-permute-start | bytes 983048 | tf_op jit(solution)/shard_map/ppermute | solution.py:429
  18.2 11.5 %collective-permute-start.2 = (bf16[8,128,128]{2,1,0:T(8,128)(2,1)S(1)}, bf16[8,128,128]{2,1,0:T(8,128)(2,1)S(1)}, u32[]{:S(2)}, u32[]{:S(2)}) collective-permute-start(bf16[8,128,128]{2,1,0:T(8,128)(2,1)S(1)} %get-tuple-element.25.early_0), channel_id=1, source_target_pairs={{0,8},{8,0},{16,24},{24,16},{1,9},{9,1},{17,25},{25,17},{2,10},{10... | collective-permute-start | bytes 786440 | tf_op jit(solution)/shard_map/ppermute | solution.py:403
  22.0 9.5 %collective-permute-start.3 = (bf16[8,128,128]{2,1,0:T(8,128)(2,1)S(1)}, bf16[8,128,128]{2,1,0:T(8,128)(2,1)S(1)}, u32[]{:S(2)}, u32[]{:S(2)}) collective-permute-start(bf16[8,128,128]{2,1,0:T(8,128)(2,1)S(1)} %get-tuple-element.25.early_0), channel_id=1, source_target_pairs={{0,16},{8,24},{16,0},{24,8},{1,17},{9,25},{17,1},{25,9},{2,18},{10... | collective-permute-start | bytes 786440 | tf_op jit(solution)/shard_map/ppermute | solution.py:403
  26.5 7.4 %collective-permute-start.4 = (bf16[4,128,128]{2,1,0:T(8,128)(2,1)S(1)}, bf16[4,128,128]{2,1,0:T(8,128)(2,1)S(1)}, u32[]{:S(2)}, u32[]{:S(2)}) collective-permute-start(bf16[4,128,128]{2,1,0:T(8,128)(2,1)S(1)} %get-tuple-element.27.late_0), channel_id=1, source_target_pairs={{0,16},{8,24},{16,0},{24,8},{1,17},{9,25},{17,1},{25,9},{2,18},{10... | collective-permute-start | bytes 393224 | tf_op jit(solution)/shard_map/ppermute | solution.py:403
  33.9 1.9 %collective-permute-start.5 = (bf16[8,128,128]{2,1,0:T(8,128)(2,1)S(1)}, bf16[8,128,128]{2,1,0:T(8,128)(2,1)S(1)}, u32[]{:S(2)}, u32[]{:S(2)}) collective-permute-start(bf16[8,128,128]{2,1,0:T(8,128)(2,1)S(1)} %collective-permute-done.3.early_2), channel_id=1, source_target_pairs={{0,8},{8,0},{16,24},{24,16},{1,9},{9,1},{17,25},{25,17},{2,10},{10... | collective-permute-start | bytes 786440 | tf_op jit(solution)/shard_map/ppermute | solution.py:403
  33.9 1.7 %collective-permute-start.6 = (bf16[4,128,128]{2,1,0:T(8,128)(2,1)S(1)}, bf16[4,128,128]{2,1,0:T(8,128)(2,1)S(1)}, u32[]{:S(2)}, u32[]{:S(2)}) collective-permute-start(bf16[4,128,128]{2,1,0:T(8,128)(2,1)S(1)} %get-tuple-element.27.late_0), channel_id=1, source_target_pairs={{0,8},{8,0},{16,24},{24,16},{1,9},{9,1},{17,25},{25,17},{2,10},{10... | collective-permute-start | bytes 393224 | tf_op jit(solution)/shard_map/ppermute | solution.py:403
  34.5 1.4 %collective-permute-start.7 = (bf16[4,128,128]{2,1,0:T(8,128)(2,1)S(1)}, bf16[4,128,128]{2,1,0:T(8,128)(2,1)S(1)}, u32[]{:S(2)}, u32[]{:S(2)}) collective-permute-start(bf16[4,128,128]{2,1,0:T(8,128)(2,1)S(1)} %collective-permute-done.4.late_2), channel_id=1, source_target_pairs={{0,8},{8,0},{16,24},{24,16},{1,9},{9,1},{17,25},{25,17},{2,10},{10... | collective-permute-start | bytes 393224 | tf_op jit(solution)/shard_map/ppermute | solution.py:403

commit v4 on v3

--- a/solution.py
+++ b/solution.py
@@ -62,18 +62,28 @@
     return start, pltpu.make_async_copy(offs_hbm.at[:, pl.ds(start, 256)], offs, sem)
 
 
+def side_of(rows, own, step):
+    odd = lax.rem(own // rows, 2)
+    side = 1 - odd if step == 0 else odd
+    return side, 1 - 2 * side
+
+
 def edges_kernel(
-    rows, total, offs_hbm, tiles_hbm, basis_hbm, low_ref, high_ref, tiles, basis, offs, cols, sems
+    rows, total, offs_hbm, tiles_hbm, basis_hbm, first_ref, second_ref, tiles, basis, offs, cols, sems
 ):
     own = place_of(rows)
     start, offs_in = offsets_copy(own, total, offs_hbm, offs, sems.at[4])
     copies = []
-    for side in range(2):
-        first, far = (0, 0) if side == 0 else (rows - 4, rows - 6)
+    for t in range(2):
+        side, way = side_of(rows, own, t)
         copies.append(
             [
-                pltpu.make_async_copy(basis_hbm.at[pl.ds(far, 6)], basis.at[side], sems.at[2 * side]),
-                pltpu.make_async_copy(tiles_hbm.at[pl.ds(first, 4)], tiles.at[side], sems.at[2 * side + 1]),
+                pltpu.make_async_copy(
+                    basis_hbm.at[pl.ds(side * (rows - 6), 6)], basis.at[t], sems.at[2 * t]
+                ),
+                pltpu.make_async_copy(
+                    tiles_hbm.at[pl.ds(side * (rows - 4), 4)], tiles.at[t], sems.at[2 * t + 1]
+                ),
             ]
         )
     offs_in.start()
@@ -84,27 +94,31 @@
     for group in copies:
         for c in group:
             c.wait()
-    for side, out in enumerate((low_ref, high_ref)):
-        shift = 0 if side == 0 else 2
-        outer = (0, 1) if side == 0 else (2, 3)
+    for t, out in enumerate((first_ref, second_ref)):
+        side, way = side_of(rows, own, t)
+
+        def tile(d, k, t=t, side=side, way=way):
+            return tiles[t, side * 3 + way * d, k]
+
+        def block(d, t=t, side=side, way=way):
+            return basis[t, side * 5 + way * d]
+
         near = [
-            [i + shift + offs[k, own - start + (i if side == 0 else rows - 4 + i)] for k in range(2)]
-            for i in range(4)
+            [d + way * offs[k, own - start + side * (rows - 1) + way * d] for k in range(2)] for d in range(4)
         ]
-        for i in range(4):
-            blocks = [basis[side, i + shift]] + [basis[side, jnp.clip(n, 0, 5)] for n in near[i]]
-            p0, p1, p2 = smooth_row([tiles[side, i, k] for k in range(3)], blocks)
-            w1, w2 = [weight((n >= 0) & (n <= 5)) for n in near[i]]
-            cols[side, i] = (p0.astype(f32) + w1 * p1.astype(f32) + w2 * p2.astype(f32)).astype(bf16)
-        for j, i in enumerate(outer):
-            out[3 * j] = tiles[side, i, 0]
+        for d in range(4):
+            blocks = [block(d)] + [block(jnp.clip(n, 0, 5)) for n in near[d]]
+            p0, p1, p2 = smooth_row([tile(d, k) for k in range(3)], blocks)
+            w1, w2 = [weight(n >= 0) for n in near[d]]
+            cols[t, d] = (p0.astype(f32) + w1 * p1.astype(f32) + w2 * p2.astype(f32)).astype(bf16)
+        for d in range(2):
+            out[3 * d] = tile(d, 0)
             for k in range(2):
-                n = near[i][k]
-                beyond = (n >= 2) if side == 0 else (n <= 3)
-                product = dot(tiles[side, i, 1 + k], cols[side, jnp.clip(n - shift, 0, 3)]).astype(bf16)
-                out[3 * j + 1 + k] = jnp.where(beyond, product, tiles[side, i, 1 + k])
-            out[6 + j] = cols[side, i]
-            out[8 + j] = basis[side, i + shift]
+                n = near[d][k]
+                product = dot(tile(d, 1 + k), cols[t, jnp.clip(n, 0, 3)]).astype(bf16)
+                out[3 * d + 1 + k] = jnp.where(n >= 2, product, tile(d, 1 + k))
+            out[6 + d] = cols[t, d]
+            out[8 + d] = block(d)
 
 
 def interior_kernel(
@@ -236,114 +250,100 @@
 
 
 def rim_kernel(
-    rows, total, offs_hbm, low_got, high_got, tiles, basis, pc_ref, mid_ref, prol_in,
-    prol_hbm, late_ref, offs, prol, low_cols, high_cols, sems,
+    rows, total, offs_hbm, first_got, second_got, tiles, basis, pc_ref, mid_ref, prol_in,
+    prol_hbm, late_ref, offs, first_prol, second_prol, first_cols, second_cols, sems,
 ):
     own = place_of(rows)
-    size = low_cols.shape[-2]
+    size = tiles.shape[-1]
     start, offs_in = offsets_copy(own, total, offs_hbm, offs, sems.at[2])
     offs_in.start()
-    sides = ((0, low_got, low_cols, -2, (0, 1), (2, 3)), (1, high_got, high_cols, rows - 4, (4, 5), (2, 3)))
-    scales = []
-    for side, got, cols, first, theirs, mine in sides:
-        own_at = (0, 1) if side == 0 else (2, 3)
-        scales.append({e: row_scale(got[3 * i]) for i, e in enumerate(theirs)})
-        scales[side].update({e: row_scale(tiles[side, own_at[i], 0]) for i, e in enumerate(mine)})
+    borders = []
+    for step, got, prol, cols in ((0, first_got, first_prol, first_cols), (1, second_got, second_prol, second_cols)):
+        side, way = side_of(rows, own, step)
+
+        def tile(f, k, step=step, got=got, side=side, way=way):
+            return got[3 * (1 - f) + k] if f < 2 else tiles[step, side * 3 + way * (f - 2), k]
+
+        scales = [row_scale(tile(f, 0)) for f in range(4)]
+        for f in range(2):
+            cols[f, :, :size] = got[7 - f]
+        for i in range(4):
+            cols[4 + i, :, size:] = pc_ref[side * 7 + way * i]
+            cols[4 + i, :, :size] = jnp.zeros((size, size), bf16)
+        borders.append((step, got, prol, cols, side, way, tile, scales))
     offs_in.wait()
 
-    outs, near = [], []
-    for side, got, cols, first, theirs, mine in sides:
-        nb, me = (0, 1) if side == 0 else (1, 0)
-        shift = -2 if side == 0 else 0
-
-        def near_of(e, first=first):
-            m = own + first + e
+    near = []
+    for step, got, prol, cols, side, way, tile, scales in borders:
+
+        def near_of(f, side=side, way=way):
+            m = own + side * (rows - 1) + way * (f - 2)
             inside = (m >= 0) & (m < total)
             at = jnp.clip(m, 0, total - 1) - start
-            return [e + jnp.where(inside, offs[k, at], 0) for k in range(2)]
-
-        def put(e, which, block, cols=cols):
-            cols[2 + e, :, which * size : (which + 1) * size] = block
-
-        near.append([near_of(e) for e in range(6)])
-        for i in range(2):
-            put(theirs[i], nb, got[6 + i])
-        for i in range(4):
-            e = i + 4 if side == 0 else i - 2
-            put(e, me, pc_ref[4 * side + i])
-            put(e, nb, jnp.zeros((size, size), bf16))
-
-        def basis_of(x, side=side, got=got, theirs=theirs):
-            outside = (x < 2) if side == 0 else (x > 3)
-            at = jnp.clip(x - 2 if side == 0 else x + 2, 0, 5)
-            return jnp.where(outside, got[8 + lax.rem(jnp.clip(x, 0, 5), 2)], basis[side, at])
-
-        for e in (*mine, *theirs):
-            w1, w2 = [weight((x >= 2) if side == 0 else (x <= 3)) for x in near[side][e]]
-            held = [got[3 * theirs.index(e) + k] if e in theirs else tiles[side, e + shift, k] for k in range(3)]
-            scale = scales[side][e]
+            return [f + way * jnp.where(inside, offs[k, at], 0) for k in range(2)]
+
+        def basis_of(x, step=step, got=got, side=side, way=way):
+            mine = basis[step, side * 5 + way * jnp.clip(x - 2, 0, 5)]
+            return jnp.where(x < 2, got[9 - jnp.clip(x, 0, 1)], mine)
+
+        near.append([near_of(f) for f in range(6)])
+        for f in (2, 3, 0, 1):
+            w1, w2 = [weight(x >= 2) for x in near[step][f]]
             p1, p2 = [
-                (scale * dot(held[1 + k], basis_of(near[side][e][k]))).astype(bf16) for k in range(2)
+                (scales[f] * dot(tile(f, 1 + k), basis_of(near[step][f][k]))).astype(bf16) for k in range(2)
             ]
             q1, q2 = p1.astype(f32), p2.astype(f32)
-            if e in mine:
-                here = basis[side, e - 2 if side == 0 else e + 2]
-                p0 = (here.astype(f32) + scale * dot(held[0], here)).astype(bf16)
+            if f >= 2:
+                here = basis[step, side * 5 + way * (f - 2)]
+                p0 = (here.astype(f32) + scales[f] * dot(tile(f, 0), here)).astype(bf16)
                 for k, block in enumerate((p0, p1, p2)):
-                    prol[side, e - 2, k] = block
-                put(e, me, (p0.astype(f32) + w1 * q1 + w2 * q2).astype(bf16))
-                put(e, nb, ((1.0 - w1) * q1 + (1.0 - w2) * q2).astype(bf16))
+                    prol[side + way * (f - 2), k] = block
+                cols[f, :, size:] = (p0.astype(f32) + w1 * q1 + w2 * q2).astype(bf16)
+                cols[f, :, :size] = ((1.0 - w1) * q1 + (1.0 - w2) * q2).astype(bf16)
             else:
-                put(e, me, (w1 * q1 + w2 * q2).astype(bf16))
-    for side in range(2):
-        out = pltpu.make_async_copy(
-            prol.at[side], prol_hbm.at[pl.ds(0 if side == 0 else rows - 2, 2)], sems.at[side]
-        )
-        out.start()
-        outs.append(out)
-    for side, got, cols, first, theirs, mine in sides:
-        nb, me = (0, 1) if side == 0 else (1, 0)
-        shift = -2 if side == 0 else 0
+                cols[f, :, size:] = (w1 * q1 + w2 * q2).astype(bf16)
+    outs = []
+    for step, got, prol, cols, side, way, tile, scales in borders:
+        outs.append(pltpu.make_async_copy(prol, prol_hbm.at[pl.ds(side * (rows - 2), 2)], sems.at[step]))
+        outs[step].start()
+    products = []
+    for step, got, prol, cols, side, way, tile, scales in borders:
         left, right = [], []
-        for e in range(6):
-            x1, x2 = near[side][e]
-            if e in theirs:
-                held = [got[3 * theirs.index(e) + k] for k in range(3)]
-                kept = [(x >= 0) & (x <= 5) for x in (x1, x2)]
-                zero = jnp.zeros_like(held[0])
-                lhs = wide([held[0]] + [jnp.where(kept[k], held[1 + k], zero) for k in range(2)])
-                more = sum(jnp.where(kept[k], zero, held[1 + k]).astype(f32) for k in range(2))
-                x1, x2 = jnp.clip(x1, 0, 5), jnp.clip(x2, 0, 5)
+        for f in range(6):
+            x1, x2 = near[step][f]
+            if f < 2:
+                zero = jnp.zeros((size, size), bf16)
+                lhs = wide([tile(f, 0)] + [jnp.where(x >= 0, tile(f, 1 + k), zero) for k, x in enumerate((x1, x2))])
+                more = sum(jnp.where(x >= 0, zero, tile(f, 1 + k)).astype(f32) for k, x in enumerate((x1, x2)))
+                x1, x2 = jnp.clip(x1, 0, 3), jnp.clip(x2, 0, 3)
+                product = dot(lhs, tall([cols[x] for x in (f, x1, x2)]))
+                product = wide([product[:, :size] + more, product[:, size:]])
             else:
-                lhs, more = wide([tiles[side, e + shift, k] for k in range(3)]), None
-            product = dot(lhs, tall([cols[2 + x] for x in (e, x1, x2)]))
-            if more is not None:
-                halves = [product[:, :size], product[:, size:]]
-                halves[nb] += more
-                product = wide(halves)
+                product = dot(wide([tile(f, k) for k in range(3)]), tall([cols[x] for x in (f, x1, x2)]))
             right.append(product.astype(bf16))
-            left.append(cols[2 + e, :, me * size : (me + 1) * size])
-        added = dot_t(tall(left), tall(right))
-        if side == 0:
-            late_ref[0] = added[:, :size].astype(bf16)
-            late_ref[1] = (added[:, size:] + mid_ref[0]).astype(bf16)
-        else:
-            late_ref[2] = (added[:, :size] + mid_ref[1]).astype(bf16)
-            late_ref[3] = added[:, size:].astype(bf16)
+            left.append(cols[f, :, size:])
+        products.append(dot_t(tall(left), tall(right)))
+    for step, got, prol, cols, side, way, tile, scales in borders:
+        late_ref[3 * side] = products[step][:, :size].astype(bf16)
+        late_ref[side + 1] = (products[step][:, size:] + mid_ref[side]).astype(bf16)
     for out in outs:
         out.wait()
 
 
-def place_early(block, early, count):
+def place_rows(block, early, late, count):
+    block[0, 0] = late[0]
+    block[0, 1] = late[1]
     block[0, 2] = early[0]
     for b in range(3):
         block[1, b] = early[1 + b]
         block[2, b] = early[4 + b]
         block[3, b] = jnp.zeros_like(early[0])
     block[count - 1, 0] = early[7]
-
-
-def near_kernel(rows, aggs_hbm, early_0, early_1, out_hbm, counts, aggs, blocks, sem, sems):
+    block[count - 1, 1] = late[2]
+    block[count - 1, 2] = late[3]
+
+
+def near_kernel(rows, aggs_hbm, early_0, early_1, late_0, late_1, out_hbm, counts, aggs, blocks, sem, sems):
     aggs_in = pltpu.make_async_copy(aggs_hbm, aggs, sem)
     aggs_in.start()
     aggs_in.wait()
@@ -355,7 +355,7 @@
         count = aggs[own + rows - 1] - aggs[own] + 1
         counts[j : j + 1, :] = jnp.full((1, counts.shape[1]), count, jnp.int32)
         if j < 2:
-            place_early(blocks.at[j], (early_0, early_1)[j], count)
+            place_rows(blocks.at[j], (early_0, early_1)[j], (late_0, late_1)[j], count)
             copies.append(
                 pltpu.make_async_copy(blocks.at[j], out_hbm.at[pl.ds(source * MOSTA, MOSTA)], sems.at[j])
             )
@@ -364,28 +364,14 @@
         c.wait()
 
 
-def far_kernel(counts, early_2, early_3, late_0, late_1, late_2, late_3, coarse_in, out, blocks, sems):
+def far_kernel(counts, early_2, early_3, late_2, late_3, coarse_in, out, blocks, sems):
     region = lax.axis_index("region")
     copies = []
-    for j, late in enumerate((late_0, late_1)):
-        at = lax.bitwise_xor(region, j) * MOSTA
-        copies.append(pltpu.make_async_copy(late.at[pl.ds(0, 2)], out.at[at, pl.ds(0, 2)], sems.at[2 * j]))
-        copies.append(
-            pltpu.make_async_copy(
-                late.at[pl.ds(2, 2)], out.at[at + counts[j, 0] - 1, pl.ds(1, 2)], sems.at[2 * j + 1]
-            )
-        )
-    for c in copies:
-        c.start()
     for j, (early, late) in enumerate(((early_2, late_2), (early_3, late_3))):
-        block, count = blocks.at[j], counts[2 + j, 0]
-        place_early(block, early, count)
-        for b in range(2):
-            block[0, b] = late[b]
-            block[count - 1, 1 + b] = late[2 + b]
+        place_rows(blocks.at[j], early, late, counts[2 + j, 0])
         at = lax.bitwise_xor(region, 2 + j) * MOSTA
-        copies.append(pltpu.make_async_copy(block, out.at[pl.ds(at, MOSTA)], sems.at[4 + j]))
-        copies[-1].start()
+        copies.append(pltpu.make_async_copy(blocks.at[j], out.at[pl.ds(at, MOSTA)], sems.at[j]))
+        copies[j].start()
     for c in copies:
         c.wait()
 
@@ -414,7 +400,7 @@
     window = pltpu.SMEM((2, 256), jnp.int32)
     ids = pltpu.SMEM((total,), jnp.int32)
     first, middle, last = [pltpu.CompilerParams(vmem_limit_bytes=int(x * 2**20)) for x in LIMITS]
-    low, high, edge_tiles, edge_basis = pl.pallas_call(
+    first_out, second_out, edge_tiles, edge_basis = pl.pallas_call(
         functools.partial(edges_kernel, rows, total),
         out_shape=[pltpu.VMEM(x + block, bf16) for x in ((10,), (10,), (2, 4, 3), (2, 6))],
         in_specs=[ANY, ANY, ANY],
@@ -425,8 +411,12 @@
         name="edges",
     )(offs_all, tile_values, basis_tiles)
     devices = lax.axis_size(AXES)
-    from_low = lax.ppermute(high, AXES, [(i, i + 1) for i in range(devices - 1)])
-    from_high = lax.ppermute(low, AXES, [(i + 1, i) for i in range(devices - 1)])
+    first_pairs = [(i, i + 1) for i in range(0, devices - 1, 2)]
+    second_pairs = [(i, i + 1) for i in range(1, devices - 1, 2)]
+    got = [
+        lax.ppermute(x, AXES, pairs + [(j, i) for i, j in pairs])
+        for x, pairs in ((first_out, first_pairs), (second_out, second_pairs))
+    ]
     prol, early, mid, pc = pl.pallas_call(
         functools.partial(interior_kernel, rows, total),
         out_shape=[
@@ -462,40 +452,41 @@
         out_specs=[ANY, VM],
         scratch_shapes=[
             window,
-            pltpu.VMEM((2, 2, 3, *block), bf16),
-            pltpu.VMEM((10, size, 2 * width), bf16),
-            pltpu.VMEM((10, size, 2 * width), bf16),
+            pltpu.VMEM((2, 3, *block), bf16),
+            pltpu.VMEM((2, 3, *block), bf16),
+            pltpu.VMEM((8, size, 2 * width), bf16),
+            pltpu.VMEM((8, size, 2 * width), bf16),
             DMA((3,)),
         ],
         input_output_aliases={7: 0},
         compiler_params=last,
-        cost_estimate=cost(140, 3 * 10**6),
+        cost_estimate=cost(140, 2 * 10**6),
         name="rim",
-    )(offs_all, from_low, from_high, edge_tiles, edge_basis, pc, mid, prol)
+    )(offs_all, *got, edge_tiles, edge_basis, pc, mid, prol)
     late_across, late_beside = swap(late, 2), swap(late, 1)
     coarse, counts = pl.pallas_call(
         functools.partial(near_kernel, rows),
         out_shape=[sds((4 * MOSTA, 3, *block), bf16), pltpu.VMEM((8, 128), jnp.int32)],
-        in_specs=[ANY, VM, VM],
+        in_specs=[ANY] + [VM] * 4,
         out_specs=[ANY, VM],
         scratch_shapes=[ids, pltpu.VMEM((2, MOSTA, 3, *block), bf16), DMA, DMA((2,))],
         compiler_params=last,
         cost_estimate=cost(0, 2 * 10**6),
         name="near",
-    )(aggregate_ids, early, early_beside)
+    )(aggregate_ids, early, early_beside, late, late_beside)
     early_across, late_across, coarse = lax.optimization_barrier((early_across, late_across, coarse))
     early_both, late_both = swap(early_across, 1), swap(late_across, 1)
     coarse = pl.pallas_call(
         far_kernel,
         out_shape=sds((4 * MOSTA, 3, *block), bf16),
-        in_specs=[VM] * 7 + [ANY],
+        in_specs=[VM] * 5 + [ANY],
         out_specs=ANY,
-        scratch_shapes=[pltpu.VMEM((2, MOSTA, 3, *block), bf16), DMA((6,))],
-        input_output_aliases={7: 0},
+        scratch_shapes=[pltpu.VMEM((2, MOSTA, 3, *block), bf16), DMA((2,))],
+        input_output_aliases={5: 0},
         compiler_params=last,
         cost_estimate=cost(0, 2 * 10**6),
         name="far",
-    )(counts, early_across, early_both, late, late_beside, late_across, late_both, coarse)
+    )(counts, early_across, early_both, late_across, late_both, coarse)
     return prol, coarse
 
 

time: 37.2 us -> 34.8 us (0.935)
  starting transfers between devices: 15.9 us -> 11.4 us
  waiting for transfers between devices: 3.89 us -> 5.78 us
    ppermute x2, starting transfers between devices: 6.18 us -> 3.7 us  [local(): lax.ppermute(x, AXES, pairs + [(j, i) for i, j in pairs])]
    ppermute x6, starting transfers between devices: 9.74 us -> 7.66 us  [swap(): lax.ppermute(block, 'region', [(i, i ^ by) for i in range(lax.axis_size('...]
    ppermute x6, waiting for transfers between devices: 3.89 us -> 5.78 us  [swap(): lax.ppermute(block, 'region', [(i, i ^ by) for i in range(lax.axis_size('...]
  transfers between devices with their start and end apart: 8 -> 8, of which waited for: 3 -> 4; matrix products, arithmetic and copies ran while one was open for 0% -> 0% of each run, Pallas kernels for 35% -> 39%
where the time goes in v4:
time: 34.8 us; the launch traced here: 34.5 us
  Pallas kernels  16.6 us (48%)
  starting transfers between devices  11.4 us (33%)
  waiting for transfers between devices  5.78 us (17%)
  between operations  0.68 us (2%)
    pallas_call x1, Pallas kernels, local(): pl.pallas_call(functools.partial(interior_kernel, rows, total), out_shape...  9.07 us
    ppermute x6, starting transfers between devices, swap(): lax.ppermute(block, 'region', [(i, i ^ by) for i in range(lax.axis_size('...  7.66 us
    ppermute x6, waiting for transfers between devices, swap(): lax.ppermute(block, 'region', [(i, i ^ by) for i in range(lax.axis_size('...  5.78 us
    ppermute x2, starting transfers between devices, local(): lax.ppermute(x, AXES, pairs + [(j, i) for i, j in pairs])  3.7 us
    pallas_call x1, Pallas kernels, local(): pl.pallas_call(functools.partial(rim_kernel, rows, total), out_shape=[sds...  2.61 us
    pallas_call x1, Pallas kernels, local(): pl.pallas_call(functools.partial(edges_kernel, rows, total), out_shape=[p...  2.27 us
    pallas_call x1, Pallas kernels, local(): pl.pallas_call(functools.partial(near_kernel, rows), out_shape=[sds((4 *...  1.73 us
    pallas_call x1, Pallas kernels, local(): pl.pallas_call(far_kernel, out_shape=sds((4 * MOSTA, 3, *block), bf16), i...  0.95 us
  transfers between devices with their start and end apart: 8, of which 4 were waited for; matrix products, arithmetic and copies ran while one was open for 0% of the time, Pallas kernels for 39%

profile of v4, /device:TPU:0, one launch (start us, length us, event | category | flops | bytes accessed | tf_op | source)
XLA Modules:
  0.0 34.5 jit_solution(1619546721583649309)
XLA Ops:
  0.6 2.3 %edges.1 = (bf16[10,128,128]{2,1,0:T(8,128)(2,1)S(1)}, bf16[10,128,128]{2,1,0:T(8,128)(2,1)S(1)}, bf16[2,4,3,128,128]{4,3,2,1,0:T(8,128)(2,1)S(1)}, bf16[2,6,128,128]{3,2,1,0:T(8,128)(2,1)S(1)}) custom-call(s32[2,2048]{1,0:T(2,128)} %bitcast.1, bf16[64,3,128,128]{3,2,1,0:T(8,128)(2,1)} %tiles_hbm.3, bf16[64,128,128]{2,1,0:T(8,128)(2,1)} %basis_hbm.3), custom_call_target="tpu_custom_call" | custom-call | flops 100663296 | bytes 2000000 | tf_op jit(solution)/shard_map/edges/pallas_call | solution.py:403
  2.9 3.0 %collective-permute-start = (bf16[10,128,128]{2,1,0:T(8,128)(2,1)S(1)}, bf16[10,128,128]{2,1,0:T(8,128)(2,1)S(1)}, u32[]{:S(2)}, u32[]{:S(2)}) collective-permute-start(bf16[10,128,128]{2,1,0:T(8,128)(2,1)S(1)} %get-tuple-element.17), channel_id=1, source_target_pairs={{0,1},{2,3},{4,5},{6,7},{8,9},{10,11},{12,13},{14,15},{16,17},{18,... | collective-permute-start | bytes 983048 | tf_op jit(solution)/shard_map/ppermute | solution.py:417
  5.9 0.7 %collective-permute-start.1 = (bf16[10,128,128]{2,1,0:T(8,128)(2,1)S(1)}, bf16[10,128,128]{2,1,0:T(8,128)(2,1)S(1)}, u32[]{:S(2)}, u32[]{:S(2)}) collective-permute-start(bf16[10,128,128]{2,1,0:T(8,128)(2,1)S(1)} %get-tuple-element.18), channel_id=1, source_target_pairs={{1,2},{3,4},{5,6},{7,8},{9,10},{11,12},{13,14},{15,16},{17,18},{19... | collective-permute-start | bytes 983048 | tf_op jit(solution)/shard_map/ppermute | solution.py:417
  6.6 9.1 %interior.1 = (bf16[64,3,128,128]{3,2,1,0:T(8,128)(2,1)}, bf16[8,128,128]{2,1,0:T(8,128)(2,1)S(1)}, f32[2,128,128]{2,1,0:T(8,128)S(1)}, bf16[8,128,128]{2,1,0:T(8,128)(2,1)S(1)}) custom-call(s32[2,2048]{1,0:T(2,128)} %bitcast.2, s32[2048]{0:T(1024)} %aggs_hbm.3, bf16[64,3,128,128]{3,2,1,0:T(8,128)(2,1)} %tiles_hbm.3, bf16[64,128,128]{2,1,0:T(8,128)(2,1)} %basis_hbm.3), custom_call_target="tpu_custom_call" | custom-call | flops 2684354560 | bytes 16000000 | tf_op jit(solution)/shard_map/interior/pallas_call | solution.py:420
  15.7 5.0 %collective-permute-start.2 = (bf16[8,128,128]{2,1,0:T(8,128)(2,1)S(1)}, bf16[8,128,128]{2,1,0:T(8,128)(2,1)S(1)}, u32[]{:S(2)}, u32[]{:S(2)}) collective-permute-start(bf16[8,128,128]{2,1,0:T(8,128)(2,1)S(1)} %get-tuple-element.25.early_0), channel_id=1, source_target_pairs={{0,8},{8,0},{16,24},{24,16},{1,9},{9,1},{17,25},{25,17},{2,10},{10... | collective-permute-start | bytes 786440 | tf_op jit(solution)/shard_map/ppermute | solution.py:389
  20.7 1.5 %collective-permute-start.4 = (bf16[8,128,128]{2,1,0:T(8,128)(2,1)S(1)}, bf16[8,128,128]{2,1,0:T(8,128)(2,1)S(1)}, u32[]{:S(2)}, u32[]{:S(2)}) collective-permute-start(bf16[8,128,128]{2,1,0:T(8,128)(2,1)S(1)} %get-tuple-element.25.early_0), channel_id=1, source_target_pairs={{0,16},{8,24},{16,0},{24,8},{1,17},{9,25},{17,1},{25,9},{2,18},{10... | collective-permute-start | bytes 786440 | tf_op jit(solution)/shard_map/ppermute | solution.py:389
  22.2 0.0 collective-permute-done.first_got
  22.2 0.0 collective-permute-done.1.second_got
  22.2 2.6 %rim.1 = (bf16[64,3,128,128]{3,2,1,0:T(8,128)(2,1)}, bf16[4,128,128]{2,1,0:T(8,128)(2,1)S(1)}) custom-call(s32[2,2048]{1,0:T(2,128)} %bitcast.3, bf16[10,128,128]{2,1,0:T(8,128)(2,1)S(1)} %collective-permute-done.first_got, bf16[10,128,128]{2,1,0:T(8,128)(2,1)S(1)} %collective-permute-done.1.second_got, ...), custom_call_target="tpu_custom_call", output_to_operand_aliasing={{0}: (7, {})} | custom-call | flops 587202560 | bytes 2000000 | tf_op jit(solution)/shard_map/rim/pallas_call | solution.py:448
  24.8 0.1 collective-permute-start.3
  24.9 0.6 %collective-permute-start.5 = (bf16[4,128,128]{2,1,0:T(8,128)(2,1)S(1)}, bf16[4,128,128]{2,1,0:T(8,128)(2,1)S(1)}, u32[]{:S(2)}, u32[]{:S(2)}) collective-permute-start(bf16[4,128,128]{2,1,0:T(8,128)(2,1)S(1)} %get-tuple-element.26.late_0), channel_id=1, source_target_pairs={{0,16},{8,24},{16,0},{24,8},{1,17},{9,25},{17,1},{25,9},{2,18},{10... | collective-permute-start | bytes 393224 | tf_op jit(solution)/shard_map/ppermute | solution.py:389
  25.5 0.0 collective-permute-done.2.early_1
  25.5 0.7 %collective-permute-done.3.late_1 = bf16[4,128,128]{2,1,0:T(8,128)(2,1)S(1)} collective-permute-done((bf16[4,128,128]{2,1,0:T(8,128)(2,1)S(1)}, bf16[4,128,128]{2,1,0:T(8,128)(2,1)S(1)}, u32[]{:S(2)}, u32[]{:S(2)}) %collective-permute-start.3) | collective-permute-done | bytes 131104 | tf_op jit(solution)/shard_map/ppermute | solution.py:389
  26.2 1.7 %near.1 = (bf16[16,3,128,128]{3,2,1,0:T(8,128)(2,1)}, s32[8,128]{1,0:T(8,128)S(1)}) custom-call(s32[2048]{0:T(1024)} %aggs_hbm.3, bf16[8,128,128]{2,1,0:T(8,128)(2,1)S(1)} %get-tuple-element.25.early_0, bf16[8,128,128]{2,1,0:T(8,128)(2,1)S(1)} %collective-permute-done.2.early_1, bf16[4,128,128]{2,1,0:T(8,128)(2,1)S(1)} %get-tuple-element.26.late_0, ...), custom_call_target="tpu_custom_call" | custom-call | bytes 2000000 | tf_op jit(solution)/shard_map/near/pallas_call | solution.py:467
  28.0 1.9 %collective-permute-done.4.early_2 = bf16[8,128,128]{2,1,0:T(8,128)(2,1)S(1)} collective-permute-done((bf16[8,128,128]{2,1,0:T(8,128)(2,1)S(1)}, bf16[8,128,128]{2,1,0:T(8,128)(2,1)S(1)}, u32[]{:S(2)}, u32[]{:S(2)}) %collective-permute-start.4) | collective-permute-done | bytes 262176 | tf_op jit(solution)/shard_map/ppermute | solution.py:389
  29.8 1.9 %collective-permute-done.5.late_2 = bf16[4,128,128]{2,1,0:T(8,128)(2,1)S(1)} collective-permute-done((bf16[4,128,128]{2,1,0:T(8,128)(2,1)S(1)}, bf16[4,128,128]{2,1,0:T(8,128)(2,1)S(1)}, u32[]{:S(2)}, u32[]{:S(2)}) %collective-permute-start.5) | collective-permute-done | bytes 131104 | tf_op jit(solution)/shard_map/ppermute | solution.py:389
  31.8 0.0 collective-permute-start.6
  31.8 0.5 %collective-permute-start.7 = (bf16[4,128,128]{2,1,0:T(8,128)(2,1)S(1)}, bf16[4,128,128]{2,1,0:T(8,128)(2,1)S(1)}, u32[]{:S(2)}, u32[]{:S(2)}) collective-permute-start(bf16[4,128,128]{2,1,0:T(8,128)(2,1)S(1)} %collective-permute-done.5.late_2), channel_id=1, source_target_pairs={{0,8},{8,0},{16,24},{24,16},{1,9},{9,1},{17,25},{25,17},{2,10},{10... | collective-permute-start | bytes 393224 | tf_op jit(solution)/shard_map/ppermute | solution.py:389
  32.3 1.2 %collective-permute-done.7.late_3 = bf16[4,128,128]{2,1,0:T(8,128)(2,1)S(1)} collective-permute-done((bf16[4,128,128]{2,1,0:T(8,128)(2,1)S(1)}, bf16[4,128,128]{2,1,0:T(8,128)(2,1)S(1)}, u32[]{:S(2)}, u32[]{:S(2)}) %collective-permute-start.7) | collective-permute-done | bytes 131104 | tf_op jit(solution)/shard_map/ppermute | solution.py:389
  33.5 0.0 collective-permute-done.6.early_3
  33.5 0.9 %far.1 = bf16[16,3,128,128]{3,2,1,0:T(8,128)(2,1)} custom-call(s32[8,128]{1,0:T(8,128)S(1)} %get-tuple-element.27.counts, bf16[8,128,128]{2,1,0:T(8,128)(2,1)S(1)} %collective-permute-done.4.early_2, bf16[8,128,128]{2,1,0:T(8,128)(2,1)S(1)} %collective-permute-done.6.early_3, ...), custom_call_target="tpu_custom_call", output_to_operand_aliasing={{}: (5, {})} | custom-call | bytes 2000000 | tf_op jit(solution)/shard_map/far/pallas_call | solution.py:479
Async XLA Ops:
  2.9 19.3 %collective-permute-start = (bf16[10,128,128]{2,1,0:T(8,128)(2,1)S(1)}, bf16[10,128,128]{2,1,0:T(8,128)(2,1)S(1)}, u32[]{:S(2)}, u32[]{:S(2)}) collective-permute-start(bf16[10,128,128]{2,1,0:T(8,128)(2,1)S(1)} %get-tuple-element.17), channel_id=1, source_target_pairs={{0,1},{2,3},{4,5},{6,7},{8,9},{10,11},{12,13},{14,15},{16,17},{18,... | collective-permute-start | bytes 983048 | tf_op jit(solution)/shard_map/ppermute | solution.py:417
  5.9 16.2 %collective-permute-start.1 = (bf16[10,128,128]{2,1,0:T(8,128)(2,1)S(1)}, bf16[10,128,128]{2,1,0:T(8,128)(2,1)S(1)}, u32[]{:S(2)}, u32[]{:S(2)}) collective-permute-start(bf16[10,128,128]{2,1,0:T(8,128)(2,1)S(1)} %get-tuple-element.18), channel_id=1, source_target_pairs={{1,2},{3,4},{5,6},{7,8},{9,10},{11,12},{13,14},{15,16},{17,18},{19... | collective-permute-start | bytes 983048 | tf_op jit(solution)/shard_map/ppermute | solution.py:417
  15.7 9.8 %collective-permute-start.2 = (bf16[8,128,128]{2,1,0:T(8,128)(2,1)S(1)}, bf16[8,128,128]{2,1,0:T(8,128)(2,1)S(1)}, u32[]{:S(2)}, u32[]{:S(2)}) collective-permute-start(bf16[8,128,128]{2,1,0:T(8,128)(2,1)S(1)} %get-tuple-element.25.early_0), channel_id=1, source_target_pairs={{0,8},{8,0},{16,24},{24,16},{1,9},{9,1},{17,25},{25,17},{2,10},{10... | collective-permute-start | bytes 786440 | tf_op jit(solution)/shard_map/ppermute | solution.py:389
  20.7 9.2 %collective-permute-start.4 = (bf16[8,128,128]{2,1,0:T(8,128)(2,1)S(1)}, bf16[8,128,128]{2,1,0:T(8,128)(2,1)S(1)}, u32[]{:S(2)}, u32[]{:S(2)}) collective-permute-start(bf16[8,128,128]{2,1,0:T(8,128)(2,1)S(1)} %get-tuple-element.25.early_0), channel_id=1, source_target_pairs={{0,16},{8,24},{16,0},{24,8},{1,17},{9,25},{17,1},{25,9},{2,18},{10... | collective-permute-start | bytes 786440 | tf_op jit(solution)/shard_map/ppermute | solution.py:389
  24.8 1.4 %collective-permute-start.3 = (bf16[4,128,128]{2,1,0:T(8,128)(2,1)S(1)}, bf16[4,128,128]{2,1,0:T(8,128)(2,1)S(1)}, u32[]{:S(2)}, u32[]{:S(2)}) collective-permute-start(bf16[4,128,128]{2,1,0:T(8,128)(2,1)S(1)} %get-tuple-element.26.late_0), channel_id=1, source_target_pairs={{0,8},{8,0},{16,24},{24,16},{1,9},{9,1},{17,25},{25,17},{2,10},{10... | collective-permute-start | bytes 393224 | tf_op jit(solution)/shard_map/ppermute | solution.py:389
  24.9 6.9 %collective-permute-start.5 = (bf16[4,128,128]{2,1,0:T(8,128)(2,1)S(1)}, bf16[4,128,128]{2,1,0:T(8,128)(2,1)S(1)}, u32[]{:S(2)}, u32[]{:S(2)}) collective-permute-start(bf16[4,128,128]{2,1,0:T(8,128)(2,1)S(1)} %get-tuple-element.26.late_0), channel_id=1, source_target_pairs={{0,16},{8,24},{16,0},{24,8},{1,17},{9,25},{17,1},{25,9},{2,18},{10... | collective-permute-start | bytes 393224 | tf_op jit(solution)/shard_map/ppermute | solution.py:389
  31.8 1.7 %collective-permute-start.6 = (bf16[8,128,128]{2,1,0:T(8,128)(2,1)S(1)}, bf16[8,128,128]{2,1,0:T(8,128)(2,1)S(1)}, u32[]{:S(2)}, u32[]{:S(2)}) collective-permute-start(bf16[8,128,128]{2,1,0:T(8,128)(2,1)S(1)} %collective-permute-done.4.early_2), channel_id=1, source_target_pairs={{0,8},{8,0},{16,24},{24,16},{1,9},{9,1},{17,25},{25,17},{2,10},{10... | collective-permute-start | bytes 786440 | tf_op jit(solution)/shard_map/ppermute | solution.py:389
  31.8 1.7 %collective-permute-start.7 = (bf16[4,128,128]{2,1,0:T(8,128)(2,1)S(1)}, bf16[4,128,128]{2,1,0:T(8,128)(2,1)S(1)}, u32[]{:S(2)}, u32[]{:S(2)}) collective-permute-start(bf16[4,128,128]{2,1,0:T(8,128)(2,1)S(1)} %collective-permute-done.5.late_2), channel_id=1, source_target_pairs={{0,8},{8,0},{16,24},{24,16},{1,9},{9,1},{17,25},{25,17},{2,10},{10... | collective-permute-start | bytes 393224 | tf_op jit(solution)/shard_map/ppermute | solution.py:389

commit v5 on v4

--- a/solution.py
+++ b/solution.py
@@ -21,8 +21,7 @@
     on = lax.broadcasted_iota(jnp.int32, (size, size), 0) == lax.broadcasted_iota(
         jnp.int32, (size, size), 1
     )
-    kept = jnp.where(on, diagonal_tile, jnp.zeros_like(diagonal_tile))
-    diag = dot(kept, jnp.ones_like(kept))
+    diag = jnp.sum(jnp.where(on, diagonal_tile.astype(f32), 0.0), axis=1, keepdims=True)
     return -damping * (1.0 / jnp.where(diag == 0.0, 1.0, diag))
 
 
@@ -474,7 +473,7 @@
         cost_estimate=cost(0, 2 * 10**6),
         name="near",
     )(aggregate_ids, early, early_beside, late, late_beside)
-    early_across, late_across, coarse = lax.optimization_barrier((early_across, late_across, coarse))
+    early_across, coarse = lax.optimization_barrier((early_across, coarse))
     early_both, late_both = swap(early_across, 1), swap(late_across, 1)
     coarse = pl.pallas_call(
         far_kernel,

time: 34.8 us -> 34.1 us (0.980)
  starting transfers between devices: 11.4 us -> 10.8 us
    ppermute x6, starting transfers between devices: 7.66 us -> 7.11 us  [swap(): lax.ppermute(block, 'region', [(i, i ^ by) for i in range(lax.axis_size('...]
where the time goes in v5:
time: 34.1 us; the launch traced here: 33.7 us
  Pallas kernels  16.3 us (48%)
  starting transfers between devices  10.8 us (32%)
  waiting for transfers between devices  5.97 us (18%)
  between operations  0.68 us (2%)
    pallas_call x1, Pallas kernels, local(): pl.pallas_call(functools.partial(interior_kernel, rows, total), out_shape...  8.81 us
    ppermute x6, starting transfers between devices, swap(): lax.ppermute(block, 'region', [(i, i ^ by) for i in range(lax.axis_size('...  7.11 us
    ppermute x6, waiting for transfers between devices, swap(): lax.ppermute(block, 'region', [(i, i ^ by) for i in range(lax.axis_size('...  5.96 us
    ppermute x2, starting transfers between devices, local(): lax.ppermute(x, AXES, pairs + [(j, i) for i, j in pairs])  3.7 us
    pallas_call x1, Pallas kernels, local(): pl.pallas_call(functools.partial(rim_kernel, rows, total), out_shape=[sds...  2.56 us
    pallas_call x1, Pallas kernels, local(): pl.pallas_call(functools.partial(edges_kernel, rows, total), out_shape=[p...  2.24 us
    pallas_call x1, Pallas kernels, local(): pl.pallas_call(functools.partial(near_kernel, rows), out_shape=[sds((4 *...  1.73 us
    pallas_call x1, Pallas kernels, local(): pl.pallas_call(far_kernel, out_shape=sds((4 * MOSTA, 3, *block), bf16), i...  0.95 us
  transfers between devices with their start and end apart: 8, of which 4 were waited for; matrix products, arithmetic and copies ran while one was open for 0% of the time, Pallas kernels for 39%

profile of v5, /device:TPU:0, one launch (start us, length us, event | category | flops | bytes accessed | tf_op | source)
XLA Modules:
  0.0 33.7 jit_solution(6821374911603024968)
XLA Ops:
  0.6 2.2 %edges.1 = (bf16[10,128,128]{2,1,0:T(8,128)(2,1)S(1)}, bf16[10,128,128]{2,1,0:T(8,128)(2,1)S(1)}, bf16[2,4,3,128,128]{4,3,2,1,0:T(8,128)(2,1)S(1)}, bf16[2,6,128,128]{3,2,1,0:T(8,128)(2,1)S(1)}) custom-call(s32[2,2048]{1,0:T(2,128)} %bitcast.1, bf16[64,3,128,128]{3,2,1,0:T(8,128)(2,1)} %tiles_hbm.3, bf16[64,128,128]{2,1,0:T(8,128)(2,1)} %basis_hbm.3), custom_call_target="tpu_custom_call" | custom-call | flops 100663296 | bytes 2000000 | tf_op jit(solution)/shard_map/edges/pallas_call | solution.py:402
  2.9 3.0 %collective-permute-start = (bf16[10,128,128]{2,1,0:T(8,128)(2,1)S(1)}, bf16[10,128,128]{2,1,0:T(8,128)(2,1)S(1)}, u32[]{:S(2)}, u32[]{:S(2)}) collective-permute-start(bf16[10,128,128]{2,1,0:T(8,128)(2,1)S(1)} %get-tuple-element.16), channel_id=1, source_target_pairs={{0,1},{2,3},{4,5},{6,7},{8,9},{10,11},{12,13},{14,15},{16,17},{18,... | collective-permute-start | bytes 983048 | tf_op jit(solution)/shard_map/ppermute | solution.py:416
  5.9 0.7 %collective-permute-start.1 = (bf16[10,128,128]{2,1,0:T(8,128)(2,1)S(1)}, bf16[10,128,128]{2,1,0:T(8,128)(2,1)S(1)}, u32[]{:S(2)}, u32[]{:S(2)}) collective-permute-start(bf16[10,128,128]{2,1,0:T(8,128)(2,1)S(1)} %get-tuple-element.17), channel_id=1, source_target_pairs={{1,2},{3,4},{5,6},{7,8},{9,10},{11,12},{13,14},{15,16},{17,18},{19... | collective-permute-start | bytes 983048 | tf_op jit(solution)/shard_map/ppermute | solution.py:416
  6.6 8.8 %interior.1 = (bf16[64,3,128,128]{3,2,1,0:T(8,128)(2,1)}, bf16[8,128,128]{2,1,0:T(8,128)(2,1)S(1)}, f32[2,128,128]{2,1,0:T(8,128)S(1)}, bf16[8,128,128]{2,1,0:T(8,128)(2,1)S(1)}) custom-call(s32[2,2048]{1,0:T(2,128)} %bitcast.2, s32[2048]{0:T(1024)} %aggs_hbm.3, bf16[64,3,128,128]{3,2,1,0:T(8,128)(2,1)} %tiles_hbm.3, bf16[64,128,128]{2,1,0:T(8,128)(2,1)} %basis_hbm.3), custom_call_target="tpu_custom_call" | custom-call | flops 2684354560 | bytes 16000000 | tf_op jit(solution)/shard_map/interior/pallas_call | solution.py:419
  15.4 4.9 %collective-permute-start.2 = (bf16[8,128,128]{2,1,0:T(8,128)(2,1)S(1)}, bf16[8,128,128]{2,1,0:T(8,128)(2,1)S(1)}, u32[]{:S(2)}, u32[]{:S(2)}) collective-permute-start(bf16[8,128,128]{2,1,0:T(8,128)(2,1)S(1)} %get-tuple-element.24.early_0), channel_id=1, source_target_pairs={{0,8},{8,0},{16,24},{24,16},{1,9},{9,1},{17,25},{25,17},{2,10},{10... | collective-permute-start | bytes 786440 | tf_op jit(solution)/shard_map/ppermute | solution.py:388
  20.3 1.5 %collective-permute-start.4 = (bf16[8,128,128]{2,1,0:T(8,128)(2,1)S(1)}, bf16[8,128,128]{2,1,0:T(8,128)(2,1)S(1)}, u32[]{:S(2)}, u32[]{:S(2)}) collective-permute-start(bf16[8,128,128]{2,1,0:T(8,128)(2,1)S(1)} %get-tuple-element.24.early_0), channel_id=1, source_target_pairs={{0,16},{8,24},{16,0},{24,8},{1,17},{9,25},{17,1},{25,9},{2,18},{10... | collective-permute-start | bytes 786440 | tf_op jit(solution)/shard_map/ppermute | solution.py:388
  21.8 0.0 collective-permute-done.first_got
  21.8 0.0 collective-permute-done.1.second_got
  21.8 2.6 %rim.1 = (bf16[64,3,128,128]{3,2,1,0:T(8,128)(2,1)}, bf16[4,128,128]{2,1,0:T(8,128)(2,1)S(1)}) custom-call(s32[2,2048]{1,0:T(2,128)} %bitcast.3, bf16[10,128,128]{2,1,0:T(8,128)(2,1)S(1)} %collective-permute-done.first_got, bf16[10,128,128]{2,1,0:T(8,128)(2,1)S(1)} %collective-permute-done.1.second_got, ...), custom_call_target="tpu_custom_call", output_to_operand_aliasing={{0}: (7, {})} | custom-call | flops 587202560 | bytes 2000000 | tf_op jit(solution)/shard_map/rim/pallas_call | solution.py:447
  24.4 0.1 collective-permute-start.3
  24.5 0.6 %collective-permute-start.6 = (bf16[4,128,128]{2,1,0:T(8,128)(2,1)S(1)}, bf16[4,128,128]{2,1,0:T(8,128)(2,1)S(1)}, u32[]{:S(2)}, u32[]{:S(2)}) collective-permute-start(bf16[4,128,128]{2,1,0:T(8,128)(2,1)S(1)} %get-tuple-element.25.late_0), channel_id=1, source_target_pairs={{0,16},{8,24},{16,0},{24,8},{1,17},{9,25},{17,1},{25,9},{2,18},{10... | collective-permute-start | bytes 393224 | tf_op jit(solution)/shard_map/ppermute | solution.py:388
  25.1 0.0 collective-permute-done.2.early_1
  25.1 0.7 %collective-permute-done.3.late_1 = bf16[4,128,128]{2,1,0:T(8,128)(2,1)S(1)} collective-permute-done((bf16[4,128,128]{2,1,0:T(8,128)(2,1)S(1)}, bf16[4,128,128]{2,1,0:T(8,128)(2,1)S(1)}, u32[]{:S(2)}, u32[]{:S(2)}) %collective-permute-start.3) | collective-permute-done | bytes 131104 | tf_op jit(solution)/shard_map/ppermute | solution.py:388
  25.8 1.7 %near.1 = (bf16[16,3,128,128]{3,2,1,0:T(8,128)(2,1)}, s32[8,128]{1,0:T(8,128)S(1)}) custom-call(s32[2048]{0:T(1024)} %aggs_hbm.3, bf16[8,128,128]{2,1,0:T(8,128)(2,1)S(1)} %get-tuple-element.24.early_0, bf16[8,128,128]{2,1,0:T(8,128)(2,1)S(1)} %collective-permute-done.2.early_1, bf16[4,128,128]{2,1,0:T(8,128)(2,1)S(1)} %get-tuple-element.25.late_0, ...), custom_call_target="tpu_custom_call" | custom-call | bytes 2000000 | tf_op jit(solution)/shard_map/near/pallas_call | solution.py:466
  27.6 1.9 %collective-permute-done.4.early_2 = bf16[8,128,128]{2,1,0:T(8,128)(2,1)S(1)} collective-permute-done((bf16[8,128,128]{2,1,0:T(8,128)(2,1)S(1)}, bf16[8,128,128]{2,1,0:T(8,128)(2,1)S(1)}, u32[]{:S(2)}, u32[]{:S(2)}) %collective-permute-start.4) | collective-permute-done | bytes 262176 | tf_op jit(solution)/shard_map/ppermute | solution.py:388
  29.5 0.0 collective-permute-start.5
  29.5 1.9 %collective-permute-done.6.late_2 = bf16[4,128,128]{2,1,0:T(8,128)(2,1)S(1)} collective-permute-done((bf16[4,128,128]{2,1,0:T(8,128)(2,1)S(1)}, bf16[4,128,128]{2,1,0:T(8,128)(2,1)S(1)}, u32[]{:S(2)}, u32[]{:S(2)}) %collective-permute-start.6) | collective-permute-done | bytes 131104 | tf_op jit(solution)/shard_map/ppermute | solution.py:388
  31.4 0.0 collective-permute-start.7
  31.4 1.3 %collective-permute-done.7.late_3 = bf16[4,128,128]{2,1,0:T(8,128)(2,1)S(1)} collective-permute-done((bf16[4,128,128]{2,1,0:T(8,128)(2,1)S(1)}, bf16[4,128,128]{2,1,0:T(8,128)(2,1)S(1)}, u32[]{:S(2)}, u32[]{:S(2)}) %collective-permute-start.7) | collective-permute-done | bytes 131104 | tf_op jit(solution)/shard_map/ppermute | solution.py:388
  32.8 0.0 collective-permute-done.5.early_3
  32.8 0.9 %far.1 = bf16[16,3,128,128]{3,2,1,0:T(8,128)(2,1)} custom-call(s32[8,128]{1,0:T(8,128)S(1)} %get-tuple-element.26.counts, bf16[8,128,128]{2,1,0:T(8,128)(2,1)S(1)} %collective-permute-done.4.early_2, bf16[8,128,128]{2,1,0:T(8,128)(2,1)S(1)} %collective-permute-done.5.early_3, ...), custom_call_target="tpu_custom_call", output_to_operand_aliasing={{}: (5, {})} | custom-call | bytes 2000000 | tf_op jit(solution)/shard_map/far/pallas_call | solution.py:478
Async XLA Ops:
  2.9 19.0 %collective-permute-start = (bf16[10,128,128]{2,1,0:T(8,128)(2,1)S(1)}, bf16[10,128,128]{2,1,0:T(8,128)(2,1)S(1)}, u32[]{:S(2)}, u32[]{:S(2)}) collective-permute-start(bf16[10,128,128]{2,1,0:T(8,128)(2,1)S(1)} %get-tuple-element.16), channel_id=1, source_target_pairs={{0,1},{2,3},{4,5},{6,7},{8,9},{10,11},{12,13},{14,15},{16,17},{18,... | collective-permute-start | bytes 983048 | tf_op jit(solution)/shard_map/ppermute | solution.py:416
  5.9 15.9 %collective-permute-start.1 = (bf16[10,128,128]{2,1,0:T(8,128)(2,1)S(1)}, bf16[10,128,128]{2,1,0:T(8,128)(2,1)S(1)}, u32[]{:S(2)}, u32[]{:S(2)}) collective-permute-start(bf16[10,128,128]{2,1,0:T(8,128)(2,1)S(1)} %get-tuple-element.17), channel_id=1, source_target_pairs={{1,2},{3,4},{5,6},{7,8},{9,10},{11,12},{13,14},{15,16},{17,18},{19... | collective-permute-start | bytes 983048 | tf_op jit(solution)/shard_map/ppermute | solution.py:416
  15.4 9.7 %collective-permute-start.2 = (bf16[8,128,128]{2,1,0:T(8,128)(2,1)S(1)}, bf16[8,128,128]{2,1,0:T(8,128)(2,1)S(1)}, u32[]{:S(2)}, u32[]{:S(2)}) collective-permute-start(bf16[8,128,128]{2,1,0:T(8,128)(2,1)S(1)} %get-tuple-element.24.early_0), channel_id=1, source_target_pairs={{0,8},{8,0},{16,24},{24,16},{1,9},{9,1},{17,25},{25,17},{2,10},{10... | collective-permute-start | bytes 786440 | tf_op jit(solution)/shard_map/ppermute | solution.py:388
  20.3 9.2 %collective-permute-start.4 = (bf16[8,128,128]{2,1,0:T(8,128)(2,1)S(1)}, bf16[8,128,128]{2,1,0:T(8,128)(2,1)S(1)}, u32[]{:S(2)}, u32[]{:S(2)}) collective-permute-start(bf16[8,128,128]{2,1,0:T(8,128)(2,1)S(1)} %get-tuple-element.24.early_0), channel_id=1, source_target_pairs={{0,16},{8,24},{16,0},{24,8},{1,17},{9,25},{17,1},{25,9},{2,18},{10... | collective-permute-start | bytes 786440 | tf_op jit(solution)/shard_map/ppermute | solution.py:388
  24.4 1.4 %collective-permute-start.3 = (bf16[4,128,128]{2,1,0:T(8,128)(2,1)S(1)}, bf16[4,128,128]{2,1,0:T(8,128)(2,1)S(1)}, u32[]{:S(2)}, u32[]{:S(2)}) collective-permute-start(bf16[4,128,128]{2,1,0:T(8,128)(2,1)S(1)} %get-tuple-element.25.late_0), channel_id=1, source_target_pairs={{0,8},{8,0},{16,24},{24,16},{1,9},{9,1},{17,25},{25,17},{2,10},{10... | collective-permute-start | bytes 393224 | tf_op jit(solution)/shard_map/ppermute | solution.py:388
  24.5 7.0 %collective-permute-start.6 = (bf16[4,128,128]{2,1,0:T(8,128)(2,1)S(1)}, bf16[4,128,128]{2,1,0:T(8,128)(2,1)S(1)}, u32[]{:S(2)}, u32[]{:S(2)}) collective-permute-start(bf16[4,128,128]{2,1,0:T(8,128)(2,1)S(1)} %get-tuple-element.25.late_0), channel_id=1, source_target_pairs={{0,16},{8,24},{16,0},{24,8},{1,17},{9,25},{17,1},{25,9},{2,18},{10... | collective-permute-start | bytes 393224 | tf_op jit(solution)/shard_map/ppermute | solution.py:388
  29.5 3.3 %collective-permute-start.5 = (bf16[8,128,128]{2,1,0:T(8,128)(2,1)S(1)}, bf16[8,128,128]{2,1,0:T(8,128)(2,1)S(1)}, u32[]{:S(2)}, u32[]{:S(2)}) collective-permute-start(bf16[8,128,128]{2,1,0:T(8,128)(2,1)S(1)} %collective-permute-done.4.early_2), channel_id=1, source_target_pairs={{0,8},{8,0},{16,24},{24,16},{1,9},{9,1},{17,25},{25,17},{2,10},{10... | collective-permute-start | bytes 786440 | tf_op jit(solution)/shard_map/ppermute | solution.py:388
  31.4 1.3 %collective-permute-start.7 = (bf16[4,128,128]{2,1,0:T(8,128)(2,1)S(1)}, bf16[4,128,128]{2,1,0:T(8,128)(2,1)S(1)}, u32[]{:S(2)}, u32[]{:S(2)}) collective-permute-start(bf16[4,128,128]{2,1,0:T(8,128)(2,1)S(1)} %collective-permute-done.6.late_2), channel_id=1, source_target_pairs={{0,8},{8,0},{16,24},{24,16},{1,9},{9,1},{17,25},{25,17},{2,10},{10... | collective-permute-start | bytes 393224 | tf_op jit(solution)/shard_map/ppermute | solution.py:388

commit v6 on v5

--- a/solution.py
+++ b/solution.py
@@ -121,8 +121,8 @@
 
 
 def interior_kernel(
-    rows, total, offs_hbm, aggs_hbm, tiles_hbm, basis_hbm, prol_hbm, early_ref, mid_ref, pc_ref,
-    offs, aggs, tiles, basis, prol, cols, acc, tile_sems, basis_sems, out_sems, small_sems,
+    rows, total, offs_hbm, aggs_hbm, tiles, basis, prol_hbm, early_ref, mid_ref, pc_ref,
+    offs, aggs, prol, cols, acc, out_sems, small_sems,
 ):
     own = place_of(rows)
     units = rows // GRP
@@ -132,26 +132,14 @@
     def part_of(u):
         return pl.ds(u * GRP, GRP)
 
-    def tile_copy(u):
-        return pltpu.make_async_copy(tiles_hbm.at[part_of(u)], tiles.at[part_of(u)], tile_sems.at[u])
-
-    def basis_copy(u):
-        return pltpu.make_async_copy(basis_hbm.at[part_of(u)], basis.at[part_of(u)], basis_sems.at[u])
-
     def out_copy(u):
         return pltpu.make_async_copy(prol.at[part_of(u)], prol_hbm.at[part_of(u)], out_sems.at[u])
 
     offs_in.start()
     aggs_in.start()
-    basis_copy(0).start()
-    for u in range(units):
-        tile_copy(u).start()
-        if u < units - 1:
-            basis_copy(u + 1).start()
     acc[...] = jnp.zeros_like(acc)
     offs_in.wait()
     aggs_in.wait()
-    basis_copy(0).wait()
     base = aggs[own]
     count = aggs[own + rows - 1] - base + 1
 
@@ -212,20 +200,11 @@
                         r * size : (r + 1) * size, s * size : (s + 1) * size
                     ]
 
-    def arrived(u):
-        tile_copy(u).wait()
-
-        @pl.when(u < units - 1)
-        def _():
-            basis_copy(u + 1).wait()
-
     for u in range(2):
-        arrived(u)
         smooth(u)
         out_copy(u).start()
 
     def unit(u, carry):
-        arrived(u)
         step(u - 1, u)
         out_copy(u).start()
         return carry
@@ -392,6 +371,8 @@
     rows, _, size, width = tile_values.shape
     total = tile_offsets.shape[0]
     hbm = lambda x: pltpu.with_memory_space_constraint(x, pltpu.HBM)
+    vmem = lambda x: pltpu.with_memory_space_constraint(x, pltpu.VMEM)
+    vmem_tiles, vmem_basis = vmem(tile_values), vmem(basis_tiles)
     tile_values, basis_tiles, aggregate_ids = hbm(tile_values), hbm(basis_tiles), hbm(aggregate_ids)
     offs_all = hbm(tile_offsets.T)
     block = (size, width)
@@ -424,25 +405,21 @@
             pltpu.VMEM((2, *block), f32),
             pltpu.VMEM((8, *block), bf16),
         ],
-        in_specs=[ANY, ANY, ANY, ANY],
+        in_specs=[ANY, ANY, VM, VM],
         out_specs=[ANY, VM, VM, VM],
         scratch_shapes=[
             window,
             ids,
             pltpu.VMEM((rows, 3, *block), bf16),
-            pltpu.VMEM((rows, *block), bf16),
-            pltpu.VMEM((rows, 3, *block), bf16),
             pltpu.VMEM((rows, 2, *block), bf16),
             pltpu.VMEM((MOSTA, 3, *block), f32),
-            DMA((rows // GRP,)),
-            DMA((rows // GRP,)),
             DMA((rows // GRP,)),
             DMA((2,)),
         ],
         compiler_params=middle,
         cost_estimate=cost(64 * 10, 16 * 10**6),
         name="interior",
-    )(offs_all, aggregate_ids, tile_values, basis_tiles)
+    )(offs_all, aggregate_ids, vmem_tiles, vmem_basis)
     early_across, early_beside = swap(early, 2), swap(early, 1)
     prol, late = pl.pallas_call(
         functools.partial(rim_kernel, rows, total),

time: 34.1 us -> 33.5 us (0.982)
  starting transfers between devices: 10.8 us -> 11.5 us
  waiting for transfers between devices: 5.97 us -> 5.3 us
  Pallas kernels: 16.3 us -> 15.7 us
    pallas_call x1, Pallas kernels: 8.81 us -> 8.1 us  [local(): pl.pallas_call(functools.partial(interior_kernel, rows, total), out_shape...]
    ppermute x6, starting transfers between devices: 7.11 us -> 7.78 us  [swap(): lax.ppermute(block, 'region', [(i, i ^ by) for i in range(lax.axis_size('...]
    ppermute x6, waiting for transfers between devices: 5.96 us -> 5.3 us  [swap(): lax.ppermute(block, 'region', [(i, i ^ by) for i in range(lax.axis_size('...]
  transfers between devices with their start and end apart: 8 -> 8, of which waited for: 4 -> 4; matrix products, arithmetic and copies ran while one was open for 0% -> 0% of each run, Pallas kernels for 39% -> 37%
where the time goes in v6:
time: 33.5 us; the launch traced here: 33.2 us
  Pallas kernels  15.7 us (47%)
  starting transfers between devices  11.5 us (34%)
  waiting for transfers between devices  5.3 us (16%)
  between operations  0.72 us (2%)
    pallas_call x1, Pallas kernels, local(): pl.pallas_call(functools.partial(interior_kernel, rows, total), out_shape...  8.1 us
    ppermute x6, starting transfers between devices, swap(): lax.ppermute(block, 'region', [(i, i ^ by) for i in range(lax.axis_size('...  7.78 us
    ppermute x6, waiting for transfers between devices, swap(): lax.ppermute(block, 'region', [(i, i ^ by) for i in range(lax.axis_size('...  5.3 us
    ppermute x2, starting transfers between devices, local(): lax.ppermute(x, AXES, pairs + [(j, i) for i, j in pairs])  3.7 us
    pallas_call x1, Pallas kernels, local(): pl.pallas_call(functools.partial(rim_kernel, rows, total), out_shape=[sds...  2.56 us
    pallas_call x1, Pallas kernels, local(): pl.pallas_call(functools.partial(edges_kernel, rows, total), out_shape=[p...  2.38 us
    pallas_call x1, Pallas kernels, local(): pl.pallas_call(functools.partial(near_kernel, rows), out_shape=[sds((4 *...  1.73 us
    pallas_call x1, Pallas kernels, local(): pl.pallas_call(far_kernel, out_shape=sds((4 * MOSTA, 3, *block), bf16), i...  0.95 us
  transfers between devices with their start and end apart: 8, of which 4 were waited for; matrix products, arithmetic and copies ran while one was open for 0% of the time, Pallas kernels for 37%

profile of v6, /device:TPU:0, one launch (start us, length us, event | category | flops | bytes accessed | tf_op | source)
XLA Modules:
  0.0 33.2 jit_solution(3764235330932908493)
XLA Ops:
  0.6 0.0 copy-start.1
  0.6 0.0 copy-start
  0.6 2.4 %edges.1 = (bf16[10,128,128]{2,1,0:T(8,128)(2,1)S(1)}, bf16[10,128,128]{2,1,0:T(8,128)(2,1)S(1)}, bf16[2,4,3,128,128]{4,3,2,1,0:T(8,128)(2,1)S(1)}, bf16[2,6,128,128]{3,2,1,0:T(8,128)(2,1)S(1)}) custom-call(s32[2,2048]{1,0:T(2,128)} %bitcast.1, bf16[64,3,128,128]{3,2,1,0:T(8,128)(2,1)} %tiles.1, bf16[64,128,128]{2,1,0:T(8,128)(2,1)} %basis.1), custom_call_target="tpu_custom_call" | custom-call | flops 100663296 | bytes 2000000 | tf_op jit(solution)/shard_map/edges/pallas_call | solution.py:383
  3.0 3.0 %collective-permute-start = (bf16[10,128,128]{2,1,0:T(8,128)(2,1)S(1)}, bf16[10,128,128]{2,1,0:T(8,128)(2,1)S(1)}, u32[]{:S(2)}, u32[]{:S(2)}) collective-permute-start(bf16[10,128,128]{2,1,0:T(8,128)(2,1)S(1)} %get-tuple-element.16), channel_id=1, source_target_pairs={{0,1},{2,3},{4,5},{6,7},{8,9},{10,11},{12,13},{14,15},{16,17},{18,... | collective-permute-start | bytes 983048 | tf_op jit(solution)/shard_map/ppermute | solution.py:397
  6.1 0.7 %collective-permute-start.1 = (bf16[10,128,128]{2,1,0:T(8,128)(2,1)S(1)}, bf16[10,128,128]{2,1,0:T(8,128)(2,1)S(1)}, u32[]{:S(2)}, u32[]{:S(2)}) collective-permute-start(bf16[10,128,128]{2,1,0:T(8,128)(2,1)S(1)} %get-tuple-element.17), channel_id=1, source_target_pairs={{1,2},{3,4},{5,6},{7,8},{9,10},{11,12},{13,14},{15,16},{17,18},{19... | collective-permute-start | bytes 983048 | tf_op jit(solution)/shard_map/ppermute | solution.py:397
  6.7 0.0 copy-done.1
  6.8 0.0 copy-done
  6.8 8.1 %interior.1 = (bf16[64,3,128,128]{3,2,1,0:T(8,128)(2,1)}, bf16[8,128,128]{2,1,0:T(8,128)(2,1)S(1)}, f32[2,128,128]{2,1,0:T(8,128)S(1)}, bf16[8,128,128]{2,1,0:T(8,128)(2,1)S(1)}) custom-call(s32[2,2048]{1,0:T(2,128)} %bitcast.2, s32[2048]{0:T(1024)} %aggs_hbm.3, bf16[64,3,128,128]{3,2,1,0:T(8,128)(2,1)S(1)} %copy-done, bf16[64,128,128]{2,1,0:T(8,128)(2,1)S(1)} %copy-done.1), custom_call_target="tpu_custom_call" | custom-call | flops 2684354560 | bytes 16000000 | tf_op jit(solution)/shard_map/interior/pallas_call | solution.py:400
  14.9 4.9 %collective-permute-start.2 = (bf16[8,128,128]{2,1,0:T(8,128)(2,1)S(1)}, bf16[8,128,128]{2,1,0:T(8,128)(2,1)S(1)}, u32[]{:S(2)}, u32[]{:S(2)}) collective-permute-start(bf16[8,128,128]{2,1,0:T(8,128)(2,1)S(1)} %get-tuple-element.24.early_0), channel_id=1, source_target_pairs={{0,8},{8,0},{16,24},{24,16},{1,9},{9,1},{17,25},{25,17},{2,10},{10... | collective-permute-start | bytes 786440 | tf_op jit(solution)/shard_map/ppermute | solution.py:367
  19.8 1.5 %collective-permute-start.4 = (bf16[8,128,128]{2,1,0:T(8,128)(2,1)S(1)}, bf16[8,128,128]{2,1,0:T(8,128)(2,1)S(1)}, u32[]{:S(2)}, u32[]{:S(2)}) collective-permute-start(bf16[8,128,128]{2,1,0:T(8,128)(2,1)S(1)} %get-tuple-element.24.early_0), channel_id=1, source_target_pairs={{0,16},{8,24},{16,0},{24,8},{1,17},{9,25},{17,1},{25,9},{2,18},{10... | collective-permute-start | bytes 786440 | tf_op jit(solution)/shard_map/ppermute | solution.py:367
  21.3 0.0 collective-permute-done.first_got
  21.3 0.0 collective-permute-done.1.second_got
  21.3 2.6 %rim.1 = (bf16[64,3,128,128]{3,2,1,0:T(8,128)(2,1)}, bf16[4,128,128]{2,1,0:T(8,128)(2,1)S(1)}) custom-call(s32[2,2048]{1,0:T(2,128)} %bitcast.3, bf16[10,128,128]{2,1,0:T(8,128)(2,1)S(1)} %collective-permute-done.first_got, bf16[10,128,128]{2,1,0:T(8,128)(2,1)S(1)} %collective-permute-done.1.second_got, ...), custom_call_target="tpu_custom_call", output_to_operand_aliasing={{0}: (7, {})} | custom-call | flops 587202560 | bytes 2000000 | tf_op jit(solution)/shard_map/rim/pallas_call | solution.py:424
  23.9 0.1 collective-permute-start.3
  24.0 1.3 %collective-permute-start.6 = (bf16[4,128,128]{2,1,0:T(8,128)(2,1)S(1)}, bf16[4,128,128]{2,1,0:T(8,128)(2,1)S(1)}, u32[]{:S(2)}, u32[]{:S(2)}) collective-permute-start(bf16[4,128,128]{2,1,0:T(8,128)(2,1)S(1)} %get-tuple-element.25.late_0), channel_id=1, source_target_pairs={{0,16},{8,24},{16,0},{24,8},{1,17},{9,25},{17,1},{25,9},{2,18},{10... | collective-permute-start | bytes 393224 | tf_op jit(solution)/shard_map/ppermute | solution.py:367
  25.2 0.0 collective-permute-done.2.early_1
  25.2 0.1 collective-permute-done.3.late_1
  25.3 1.7 %near.1 = (bf16[16,3,128,128]{3,2,1,0:T(8,128)(2,1)}, s32[8,128]{1,0:T(8,128)S(1)}) custom-call(s32[2048]{0:T(1024)} %aggs_hbm.3, bf16[8,128,128]{2,1,0:T(8,128)(2,1)S(1)} %get-tuple-element.24.early_0, bf16[8,128,128]{2,1,0:T(8,128)(2,1)S(1)} %collective-permute-done.2.early_1, bf16[4,128,128]{2,1,0:T(8,128)(2,1)S(1)} %get-tuple-element.25.late_0, ...), custom_call_target="tpu_custom_call" | custom-call | bytes 2000000 | tf_op jit(solution)/shard_map/near/pallas_call | solution.py:443
  27.0 1.9 %collective-permute-done.4.early_2 = bf16[8,128,128]{2,1,0:T(8,128)(2,1)S(1)} collective-permute-done((bf16[8,128,128]{2,1,0:T(8,128)(2,1)S(1)}, bf16[8,128,128]{2,1,0:T(8,128)(2,1)S(1)}, u32[]{:S(2)}, u32[]{:S(2)}) %collective-permute-start.4) | collective-permute-done | bytes 262176 | tf_op jit(solution)/shard_map/ppermute | solution.py:367
  29.0 0.0 collective-permute-start.5
  29.0 1.9 %collective-permute-done.6.late_2 = bf16[4,128,128]{2,1,0:T(8,128)(2,1)S(1)} collective-permute-done((bf16[4,128,128]{2,1,0:T(8,128)(2,1)S(1)}, bf16[4,128,128]{2,1,0:T(8,128)(2,1)S(1)}, u32[]{:S(2)}, u32[]{:S(2)}) %collective-permute-start.6) | collective-permute-done | bytes 131104 | tf_op jit(solution)/shard_map/ppermute | solution.py:367
  30.9 0.0 collective-permute-start.7
  30.9 1.3 %collective-permute-done.7.late_3 = bf16[4,128,128]{2,1,0:T(8,128)(2,1)S(1)} collective-permute-done((bf16[4,128,128]{2,1,0:T(8,128)(2,1)S(1)}, bf16[4,128,128]{2,1,0:T(8,128)(2,1)S(1)}, u32[]{:S(2)}, u32[]{:S(2)}) %collective-permute-start.7) | collective-permute-done | bytes 131104 | tf_op jit(solution)/shard_map/ppermute | solution.py:367
  32.3 0.0 collective-permute-done.5.early_3
  32.3 0.9 %far.1 = bf16[16,3,128,128]{3,2,1,0:T(8,128)(2,1)} custom-call(s32[8,128]{1,0:T(8,128)S(1)} %get-tuple-element.26.counts, bf16[8,128,128]{2,1,0:T(8,128)(2,1)S(1)} %collective-permute-done.4.early_2, bf16[8,128,128]{2,1,0:T(8,128)(2,1)S(1)} %collective-permute-done.5.early_3, ...), custom_call_target="tpu_custom_call", output_to_operand_aliasing={{}: (5, {})} | custom-call | bytes 2000000 | tf_op jit(solution)/shard_map/far/pallas_call | solution.py:455
Async XLA Ops:
  0.6 6.1 %copy-start.1 = (bf16[64,128,128]{2,1,0:T(8,128)(2,1)S(1)}, bf16[64,128,128]{2,1,0:T(8,128)(2,1)}, u32[]{:S(2)}) copy-start(bf16[64,128,128]{2,1,0:T(8,128)(2,1)} %basis.1) | copy-start | bytes 6291460
  0.6 6.1 %copy-start = (bf16[64,3,128,128]{3,2,1,0:T(8,128)(2,1)S(1)}, bf16[64,3,128,128]{3,2,1,0:T(8,128)(2,1)}, u32[]{:S(2)}) copy-start(bf16[64,3,128,128]{3,2,1,0:T(8,128)(2,1)} %tiles.1) | copy-start | bytes 18874372
  3.0 18.3 %collective-permute-start = (bf16[10,128,128]{2,1,0:T(8,128)(2,1)S(1)}, bf16[10,128,128]{2,1,0:T(8,128)(2,1)S(1)}, u32[]{:S(2)}, u32[]{:S(2)}) collective-permute-start(bf16[10,128,128]{2,1,0:T(8,128)(2,1)S(1)} %get-tuple-element.16), channel_id=1, source_target_pairs={{0,1},{2,3},{4,5},{6,7},{8,9},{10,11},{12,13},{14,15},{16,17},{18,... | collective-permute-start | bytes 983048 | tf_op jit(solution)/shard_map/ppermute | solution.py:397
  6.1 15.3 %collective-permute-start.1 = (bf16[10,128,128]{2,1,0:T(8,128)(2,1)S(1)}, bf16[10,128,128]{2,1,0:T(8,128)(2,1)S(1)}, u32[]{:S(2)}, u32[]{:S(2)}) collective-permute-start(bf16[10,128,128]{2,1,0:T(8,128)(2,1)S(1)} %get-tuple-element.17), channel_id=1, source_target_pairs={{1,2},{3,4},{5,6},{7,8},{9,10},{11,12},{13,14},{15,16},{17,18},{19... | collective-permute-start | bytes 983048 | tf_op jit(solution)/shard_map/ppermute | solution.py:397
  14.9 10.4 %collective-permute-start.2 = (bf16[8,128,128]{2,1,0:T(8,128)(2,1)S(1)}, bf16[8,128,128]{2,1,0:T(8,128)(2,1)S(1)}, u32[]{:S(2)}, u32[]{:S(2)}) collective-permute-start(bf16[8,128,128]{2,1,0:T(8,128)(2,1)S(1)} %get-tuple-element.24.early_0), channel_id=1, source_target_pairs={{0,8},{8,0},{16,24},{24,16},{1,9},{9,1},{17,25},{25,17},{2,10},{10... | collective-permute-start | bytes 786440 | tf_op jit(solution)/shard_map/ppermute | solution.py:367
  19.8 9.2 %collective-permute-start.4 = (bf16[8,128,128]{2,1,0:T(8,128)(2,1)S(1)}, bf16[8,128,128]{2,1,0:T(8,128)(2,1)S(1)}, u32[]{:S(2)}, u32[]{:S(2)}) collective-permute-start(bf16[8,128,128]{2,1,0:T(8,128)(2,1)S(1)} %get-tuple-element.24.early_0), channel_id=1, source_target_pairs={{0,16},{8,24},{16,0},{24,8},{1,17},{9,25},{17,1},{25,9},{2,18},{10... | collective-permute-start | bytes 786440 | tf_op jit(solution)/shard_map/ppermute | solution.py:367
  23.9 1.4 %collective-permute-start.3 = (bf16[4,128,128]{2,1,0:T(8,128)(2,1)S(1)}, bf16[4,128,128]{2,1,0:T(8,128)(2,1)S(1)}, u32[]{:S(2)}, u32[]{:S(2)}) collective-permute-start(bf16[4,128,128]{2,1,0:T(8,128)(2,1)S(1)} %get-tuple-element.25.late_0), channel_id=1, source_target_pairs={{0,8},{8,0},{16,24},{24,16},{1,9},{9,1},{17,25},{25,17},{2,10},{10... | collective-permute-start | bytes 393224 | tf_op jit(solution)/shard_map/ppermute | solution.py:367
  24.0 6.9 %collective-permute-start.6 = (bf16[4,128,128]{2,1,0:T(8,128)(2,1)S(1)}, bf16[4,128,128]{2,1,0:T(8,128)(2,1)S(1)}, u32[]{:S(2)}, u32[]{:S(2)}) collective-permute-start(bf16[4,128,128]{2,1,0:T(8,128)(2,1)S(1)} %get-tuple-element.25.late_0), channel_id=1, source_target_pairs={{0,16},{8,24},{16,0},{24,8},{1,17},{9,25},{17,1},{25,9},{2,18},{10... | collective-permute-start | bytes 393224 | tf_op jit(solution)/shard_map/ppermute | solution.py:367
  29.0 3.3 %collective-permute-start.5 = (bf16[8,128,128]{2,1,0:T(8,128)(2,1)S(1)}, bf16[8,128,128]{2,1,0:T(8,128)(2,1)S(1)}, u32[]{:S(2)}, u32[]{:S(2)}) collective-permute-start(bf16[8,128,128]{2,1,0:T(8,128)(2,1)S(1)} %collective-permute-done.4.early_2), channel_id=1, source_target_pairs={{0,8},{8,0},{16,24},{24,16},{1,9},{9,1},{17,25},{25,17},{2,10},{10... | collective-permute-start | bytes 786440 | tf_op jit(solution)/shard_map/ppermute | solution.py:367
  30.9 1.3 %collective-permute-start.7 = (bf16[4,128,128]{2,1,0:T(8,128)(2,1)S(1)}, bf16[4,128,128]{2,1,0:T(8,128)(2,1)S(1)}, u32[]{:S(2)}, u32[]{:S(2)}) collective-permute-start(bf16[4,128,128]{2,1,0:T(8,128)(2,1)S(1)} %collective-permute-done.6.late_2), channel_id=1, source_target_pairs={{0,8},{8,0},{16,24},{24,16},{1,9},{9,1},{17,25},{25,17},{2,10},{10... | collective-permute-start | bytes 393224 | tf_op jit(solution)/shard_map/ppermute | solution.py:367

commit v7 on v6

--- a/solution.py
+++ b/solution.py
@@ -90,11 +90,10 @@
         for c in group:
             c.start()
     offs_in.wait()
-    for group in copies:
-        for c in group:
-            c.wait()
     for t, out in enumerate((first_ref, second_ref)):
         side, way = side_of(rows, own, t)
+        for c in copies[t]:
+            c.wait()
 
         def tile(d, k, t=t, side=side, way=way):
             return tiles[t, side * 3 + way * d, k]
@@ -450,7 +449,7 @@
         cost_estimate=cost(0, 2 * 10**6),
         name="near",
     )(aggregate_ids, early, early_beside, late, late_beside)
-    early_across, coarse = lax.optimization_barrier((early_across, coarse))
+    early_across, ignored = lax.optimization_barrier((early_across, late_beside))
     early_both, late_both = swap(early_across, 1), swap(late_across, 1)
     coarse = pl.pallas_call(
         far_kernel,

time: 33.5 us -> 33.3 us (level)
  waiting for transfers between devices: 5.3 us -> 3.88 us
  starting transfers between devices: 11.5 us -> 12.7 us
    ppermute x6, waiting for transfers between devices: 5.3 us -> 3.88 us  [swap(): lax.ppermute(block, 'region', [(i, i ^ by) for i in range(lax.axis_size('...]
    ppermute x6, starting transfers between devices: 7.78 us -> 9 us  [swap(): lax.ppermute(block, 'region', [(i, i ^ by) for i in range(lax.axis_size('...]
  transfers between devices with their start and end apart: 8 -> 8, of which waited for: 4 -> 2; matrix products, arithmetic and copies ran while one was open for 0% -> 0% of each run, Pallas kernels for 37% -> 38%
where the time goes in v7:
time: 33.3 us; the launch traced here: 33 us
  Pallas kernels  15.7 us (47%)
  starting transfers between devices  12.7 us (38%)
  waiting for transfers between devices  3.88 us (12%)
  between operations  0.72 us (2%)
    ppermute x6, starting transfers between devices, swap(): lax.ppermute(block, 'region', [(i, i ^ by) for i in range(lax.axis_size('...  9 us
    pallas_call x1, Pallas kernels, local(): pl.pallas_call(functools.partial(interior_kernel, rows, total), out_shape...  8.1 us
    ppermute x6, waiting for transfers between devices, swap(): lax.ppermute(block, 'region', [(i, i ^ by) for i in range(lax.axis_size('...  3.88 us
    ppermute x2, starting transfers between devices, local(): lax.ppermute(x, AXES, pairs + [(j, i) for i, j in pairs])  3.7 us
    pallas_call x1, Pallas kernels, local(): pl.pallas_call(functools.partial(rim_kernel, rows, total), out_shape=[sds...  2.56 us
    pallas_call x1, Pallas kernels, local(): pl.pallas_call(functools.partial(edges_kernel, rows, total), out_shape=[p...  2.35 us
    pallas_call x1, Pallas kernels, local(): pl.pallas_call(functools.partial(near_kernel, rows), out_shape=[sds((4 *...  1.73 us
    pallas_call x1, Pallas kernels, local(): pl.pallas_call(far_kernel, out_shape=sds((4 * MOSTA, 3, *block), bf16), i...  0.95 us
  transfers between devices with their start and end apart: 8, of which 2 were waited for; matrix products, arithmetic and copies ran while one was open for 0% of the time, Pallas kernels for 38%

profile of v7, /device:TPU:0, one launch (start us, length us, event | category | flops | bytes accessed | tf_op | source)
XLA Modules:
  0.0 33.0 jit_solution(2360606453758237796)
XLA Ops:
  0.6 0.0 copy-start.1
  0.6 0.0 copy-start
  0.6 2.4 %edges.1 = (bf16[10,128,128]{2,1,0:T(8,128)(2,1)S(1)}, bf16[10,128,128]{2,1,0:T(8,128)(2,1)S(1)}, bf16[2,4,3,128,128]{4,3,2,1,0:T(8,128)(2,1)S(1)}, bf16[2,6,128,128]{3,2,1,0:T(8,128)(2,1)S(1)}) custom-call(s32[2,2048]{1,0:T(2,128)} %bitcast.1, bf16[64,3,128,128]{3,2,1,0:T(8,128)(2,1)} %tiles.1, bf16[64,128,128]{2,1,0:T(8,128)(2,1)} %basis.1), custom_call_target="tpu_custom_call" | custom-call | flops 100663296 | bytes 2000000 | tf_op jit(solution)/shard_map/edges/pallas_call | solution.py:382
  3.0 3.0 %collective-permute-start = (bf16[10,128,128]{2,1,0:T(8,128)(2,1)S(1)}, bf16[10,128,128]{2,1,0:T(8,128)(2,1)S(1)}, u32[]{:S(2)}, u32[]{:S(2)}) collective-permute-start(bf16[10,128,128]{2,1,0:T(8,128)(2,1)S(1)} %get-tuple-element.15), channel_id=1, source_target_pairs={{0,1},{2,3},{4,5},{6,7},{8,9},{10,11},{12,13},{14,15},{16,17},{18,... | collective-permute-start | bytes 983048 | tf_op jit(solution)/shard_map/ppermute | solution.py:396
  6.0 0.7 %collective-permute-start.1 = (bf16[10,128,128]{2,1,0:T(8,128)(2,1)S(1)}, bf16[10,128,128]{2,1,0:T(8,128)(2,1)S(1)}, u32[]{:S(2)}, u32[]{:S(2)}) collective-permute-start(bf16[10,128,128]{2,1,0:T(8,128)(2,1)S(1)} %get-tuple-element.16), channel_id=1, source_target_pairs={{1,2},{3,4},{5,6},{7,8},{9,10},{11,12},{13,14},{15,16},{17,18},{19... | collective-permute-start | bytes 983048 | tf_op jit(solution)/shard_map/ppermute | solution.py:396
  6.7 0.0 copy-done.1
  6.7 0.0 copy-done
  6.7 8.1 %interior.1 = (bf16[64,3,128,128]{3,2,1,0:T(8,128)(2,1)}, bf16[8,128,128]{2,1,0:T(8,128)(2,1)S(1)}, f32[2,128,128]{2,1,0:T(8,128)S(1)}, bf16[8,128,128]{2,1,0:T(8,128)(2,1)S(1)}) custom-call(s32[2,2048]{1,0:T(2,128)} %bitcast.2, s32[2048]{0:T(1024)} %aggs_hbm.3, bf16[64,3,128,128]{3,2,1,0:T(8,128)(2,1)S(1)} %copy-done, bf16[64,128,128]{2,1,0:T(8,128)(2,1)S(1)} %copy-done.1), custom_call_target="tpu_custom_call" | custom-call | flops 2684354560 | bytes 16000000 | tf_op jit(solution)/shard_map/interior/pallas_call | solution.py:399
  14.8 5.6 %collective-permute-start.4 = (bf16[8,128,128]{2,1,0:T(8,128)(2,1)S(1)}, bf16[8,128,128]{2,1,0:T(8,128)(2,1)S(1)}, u32[]{:S(2)}, u32[]{:S(2)}) collective-permute-start(bf16[8,128,128]{2,1,0:T(8,128)(2,1)S(1)} %get-tuple-element.23.early_0), channel_id=1, source_target_pairs={{0,16},{8,24},{16,0},{24,8},{1,17},{9,25},{17,1},{25,9},{2,18},{10... | collective-permute-start | bytes 786440 | tf_op jit(solution)/shard_map/ppermute | solution.py:366
  20.4 0.0 collective-permute-done.first_got
  20.4 0.0 collective-permute-done.1.second_got
  20.4 2.6 %rim.1 = (bf16[64,3,128,128]{3,2,1,0:T(8,128)(2,1)}, bf16[4,128,128]{2,1,0:T(8,128)(2,1)S(1)}) custom-call(s32[2,2048]{1,0:T(2,128)} %bitcast.3, bf16[10,128,128]{2,1,0:T(8,128)(2,1)S(1)} %collective-permute-done.first_got, bf16[10,128,128]{2,1,0:T(8,128)(2,1)S(1)} %collective-permute-done.1.second_got, ...), custom_call_target="tpu_custom_call", output_to_operand_aliasing={{0}: (7, {})} | custom-call | flops 587202560 | bytes 2000000 | tf_op jit(solution)/shard_map/rim/pallas_call | solution.py:423
  23.0 0.7 %collective-permute-start.3 = (bf16[4,128,128]{2,1,0:T(8,128)(2,1)S(1)}, bf16[4,128,128]{2,1,0:T(8,128)(2,1)S(1)}, u32[]{:S(2)}, u32[]{:S(2)}) collective-permute-start(bf16[4,128,128]{2,1,0:T(8,128)(2,1)S(1)} %get-tuple-element.24.late_0), channel_id=1, source_target_pairs={{0,8},{8,0},{16,24},{24,16},{1,9},{9,1},{17,25},{25,17},{2,10},{10... | collective-permute-start | bytes 393224 | tf_op jit(solution)/shard_map/ppermute | solution.py:366
  23.7 0.1 collective-permute-start.2
  23.7 1.9 %collective-permute-start.6 = (bf16[4,128,128]{2,1,0:T(8,128)(2,1)S(1)}, bf16[4,128,128]{2,1,0:T(8,128)(2,1)S(1)}, u32[]{:S(2)}, u32[]{:S(2)}) collective-permute-start(bf16[4,128,128]{2,1,0:T(8,128)(2,1)S(1)} %get-tuple-element.24.late_0), channel_id=1, source_target_pairs={{0,16},{8,24},{16,0},{24,8},{1,17},{9,25},{17,1},{25,9},{2,18},{10... | collective-permute-start | bytes 393224 | tf_op jit(solution)/shard_map/ppermute | solution.py:366
  25.6 1.6 %collective-permute-done.4.early_2 = bf16[8,128,128]{2,1,0:T(8,128)(2,1)S(1)} collective-permute-done((bf16[8,128,128]{2,1,0:T(8,128)(2,1)S(1)}, bf16[8,128,128]{2,1,0:T(8,128)(2,1)S(1)}, u32[]{:S(2)}, u32[]{:S(2)}) %collective-permute-start.4) | collective-permute-done | bytes 262176 | tf_op jit(solution)/shard_map/ppermute | solution.py:366
  27.3 0.0 collective-permute-done.3.late_1
  27.3 0.7 %collective-permute-start.5 = (bf16[8,128,128]{2,1,0:T(8,128)(2,1)S(1)}, bf16[8,128,128]{2,1,0:T(8,128)(2,1)S(1)}, u32[]{:S(2)}, u32[]{:S(2)}) collective-permute-start(bf16[8,128,128]{2,1,0:T(8,128)(2,1)S(1)} %collective-permute-done.4.early_2), channel_id=1, source_target_pairs={{0,8},{8,0},{16,24},{24,16},{1,9},{9,1},{17,25},{25,17},{2,10},{10... | collective-permute-start | bytes 786440 | tf_op jit(solution)/shard_map/ppermute | solution.py:366
  27.9 2.2 %collective-permute-done.6.late_2 = bf16[4,128,128]{2,1,0:T(8,128)(2,1)S(1)} collective-permute-done((bf16[4,128,128]{2,1,0:T(8,128)(2,1)S(1)}, bf16[4,128,128]{2,1,0:T(8,128)(2,1)S(1)}, u32[]{:S(2)}, u32[]{:S(2)}) %collective-permute-start.6) | collective-permute-done | bytes 131104 | tf_op jit(solution)/shard_map/ppermute | solution.py:366
  30.2 0.1 collective-permute-start.7
  30.3 0.0 collective-permute-done.2.early_1
  30.3 1.7 %near.1 = (bf16[16,3,128,128]{3,2,1,0:T(8,128)(2,1)}, s32[8,128]{1,0:T(8,128)S(1)}) custom-call(s32[2048]{0:T(1024)} %aggs_hbm.3, bf16[8,128,128]{2,1,0:T(8,128)(2,1)S(1)} %get-tuple-element.23.early_0, bf16[8,128,128]{2,1,0:T(8,128)(2,1)S(1)} %collective-permute-done.2.early_1, bf16[4,128,128]{2,1,0:T(8,128)(2,1)S(1)} %get-tuple-element.24.late_0, ...), custom_call_target="tpu_custom_call" | custom-call | bytes 2000000 | tf_op jit(solution)/shard_map/near/pallas_call | solution.py:442
  32.0 0.0 collective-permute-done.7.late_3
  32.0 0.0 collective-permute-done.5.early_3
  32.1 1.0 %far.1 = bf16[16,3,128,128]{3,2,1,0:T(8,128)(2,1)} custom-call(s32[8,128]{1,0:T(8,128)S(1)} %get-tuple-element.25.counts, bf16[8,128,128]{2,1,0:T(8,128)(2,1)S(1)} %collective-permute-done.4.early_2, bf16[8,128,128]{2,1,0:T(8,128)(2,1)S(1)} %collective-permute-done.5.early_3, ...), custom_call_target="tpu_custom_call", output_to_operand_aliasing={{}: (5, {})} | custom-call | bytes 2000000 | tf_op jit(solution)/shard_map/far/pallas_call | solution.py:454
Async XLA Ops:
  0.6 6.1 %copy-start.1 = (bf16[64,128,128]{2,1,0:T(8,128)(2,1)S(1)}, bf16[64,128,128]{2,1,0:T(8,128)(2,1)}, u32[]{:S(2)}) copy-start(bf16[64,128,128]{2,1,0:T(8,128)(2,1)} %basis.1) | copy-start | bytes 6291460
  0.6 6.1 %copy-start = (bf16[64,3,128,128]{3,2,1,0:T(8,128)(2,1)S(1)}, bf16[64,3,128,128]{3,2,1,0:T(8,128)(2,1)}, u32[]{:S(2)}) copy-start(bf16[64,3,128,128]{3,2,1,0:T(8,128)(2,1)} %tiles.1) | copy-start | bytes 18874372
  3.0 17.4 %collective-permute-start = (bf16[10,128,128]{2,1,0:T(8,128)(2,1)S(1)}, bf16[10,128,128]{2,1,0:T(8,128)(2,1)S(1)}, u32[]{:S(2)}, u32[]{:S(2)}) collective-permute-start(bf16[10,128,128]{2,1,0:T(8,128)(2,1)S(1)} %get-tuple-element.15), channel_id=1, source_target_pairs={{0,1},{2,3},{4,5},{6,7},{8,9},{10,11},{12,13},{14,15},{16,17},{18,... | collective-permute-start | bytes 983048 | tf_op jit(solution)/shard_map/ppermute | solution.py:396
  6.0 14.4 %collective-permute-start.1 = (bf16[10,128,128]{2,1,0:T(8,128)(2,1)S(1)}, bf16[10,128,128]{2,1,0:T(8,128)(2,1)S(1)}, u32[]{:S(2)}, u32[]{:S(2)}) collective-permute-start(bf16[10,128,128]{2,1,0:T(8,128)(2,1)S(1)} %get-tuple-element.16), channel_id=1, source_target_pairs={{1,2},{3,4},{5,6},{7,8},{9,10},{11,12},{13,14},{15,16},{17,18},{19... | collective-permute-start | bytes 983048 | tf_op jit(solution)/shard_map/ppermute | solution.py:396
  14.8 12.4 %collective-permute-start.4 = (bf16[8,128,128]{2,1,0:T(8,128)(2,1)S(1)}, bf16[8,128,128]{2,1,0:T(8,128)(2,1)S(1)}, u32[]{:S(2)}, u32[]{:S(2)}) collective-permute-start(bf16[8,128,128]{2,1,0:T(8,128)(2,1)S(1)} %get-tuple-element.23.early_0), channel_id=1, source_target_pairs={{0,16},{8,24},{16,0},{24,8},{1,17},{9,25},{17,1},{25,9},{2,18},{10... | collective-permute-start | bytes 786440 | tf_op jit(solution)/shard_map/ppermute | solution.py:366
  23.0 4.3 %collective-permute-start.3 = (bf16[4,128,128]{2,1,0:T(8,128)(2,1)S(1)}, bf16[4,128,128]{2,1,0:T(8,128)(2,1)S(1)}, u32[]{:S(2)}, u32[]{:S(2)}) collective-permute-start(bf16[4,128,128]{2,1,0:T(8,128)(2,1)S(1)} %get-tuple-element.24.late_0), channel_id=1, source_target_pairs={{0,8},{8,0},{16,24},{24,16},{1,9},{9,1},{17,25},{25,17},{2,10},{10... | collective-permute-start | bytes 393224 | tf_op jit(solution)/shard_map/ppermute | solution.py:366
  23.7 6.6 %collective-permute-start.2 = (bf16[8,128,128]{2,1,0:T(8,128)(2,1)S(1)}, bf16[8,128,128]{2,1,0:T(8,128)(2,1)S(1)}, u32[]{:S(2)}, u32[]{:S(2)}) collective-permute-start(bf16[8,128,128]{2,1,0:T(8,128)(2,1)S(1)} %get-tuple-element.23.early_0), channel_id=1, source_target_pairs={{0,8},{8,0},{16,24},{24,16},{1,9},{9,1},{17,25},{25,17},{2,10},{10... | collective-permute-start | bytes 786440 | tf_op jit(solution)/shard_map/ppermute | solution.py:366
  23.7 6.4 %collective-permute-start.6 = (bf16[4,128,128]{2,1,0:T(8,128)(2,1)S(1)}, bf16[4,128,128]{2,1,0:T(8,128)(2,1)S(1)}, u32[]{:S(2)}, u32[]{:S(2)}) collective-permute-start(bf16[4,128,128]{2,1,0:T(8,128)(2,1)S(1)} %get-tuple-element.24.late_0), channel_id=1, source_target_pairs={{0,16},{8,24},{16,0},{24,8},{1,17},{9,25},{17,1},{25,9},{2,18},{10... | collective-permute-start | bytes 393224 | tf_op jit(solution)/shard_map/ppermute | solution.py:366
  27.3 4.8 %collective-permute-start.5 = (bf16[8,128,128]{2,1,0:T(8,128)(2,1)S(1)}, bf16[8,128,128]{2,1,0:T(8,128)(2,1)S(1)}, u32[]{:S(2)}, u32[]{:S(2)}) collective-permute-start(bf16[8,128,128]{2,1,0:T(8,128)(2,1)S(1)} %collective-permute-done.4.early_2), channel_id=1, source_target_pairs={{0,8},{8,0},{16,24},{24,16},{1,9},{9,1},{17,25},{25,17},{2,10},{10... | collective-permute-start | bytes 786440 | tf_op jit(solution)/shard_map/ppermute | solution.py:366
  30.2 1.9 %collective-permute-start.7 = (bf16[4,128,128]{2,1,0:T(8,128)(2,1)S(1)}, bf16[4,128,128]{2,1,0:T(8,128)(2,1)S(1)}, u32[]{:S(2)}, u32[]{:S(2)}) collective-permute-start(bf16[4,128,128]{2,1,0:T(8,128)(2,1)S(1)} %collective-permute-done.6.late_2), channel_id=1, source_target_pairs={{0,8},{8,0},{16,24},{24,16},{1,9},{9,1},{17,25},{25,17},{2,10},{10... | collective-permute-start | bytes 393224 | tf_op jit(solution)/shard_map/ppermute | solution.py:366
